TPU v7x, 32 devices: a whole 2x2x4 slice. The times are simulated.
32 devices in a mesh: pipe: 2 (over core), ctx: 4 (over y, x), tensor: 4 (over z).
Axes of the slice: x: 2, y: 2, z: 4, core: 2. Of those that a mesh axis runs over, the one named last changes fastest.
Arguments:
- inputs: bfloat16 [2, 1024, 2048], P(None, 'ctx'), may hold values from -6 to 6
- out_grad: bfloat16 [2, 1024, 2048], P(None, 'ctx'), may hold values from -6 to 6
- positions: int32 [2, 1024], P(None, 'ctx'), may hold values from 0 to 255, as said below
- attn_gain: bfloat16 [2, 2048], P('pipe', 'ctx'), may hold values from 0.25 to 1.75
- w_query: bfloat16 [2, 2048, 2048], P('pipe', 'ctx', 'tensor'), may hold values from -0.125 to 0.125
- w_key: bfloat16 [2, 2048, 512], P('pipe', 'ctx', 'tensor'), may hold values from -0.125 to 0.125
- w_value: bfloat16 [2, 2048, 512], P('pipe', 'ctx', 'tensor'), may hold values from -0.125 to 0.125
- w_out: bfloat16 [2, 2048, 2048], P('pipe', 'tensor', 'ctx'), may hold values from -0.5 to 0.5
- ffn_gain: bfloat16 [2, 2048], P('pipe', 'ctx'), may hold values from 0.25 to 1.75
- w_gate: bfloat16 [2, 2048, 8192], P('pipe', 'ctx', 'tensor'), may hold values from -0.125 to 0.125
- w_up: bfloat16 [2, 2048, 8192], P('pipe', 'ctx', 'tensor'), may hold values from -0.125 to 0.125
- w_down: bfloat16 [2, 8192, 2048], P('pipe', 'tensor', 'ctx'), may hold values from -0.0625 to 0.0625
Outputs:
- section_outputs: bfloat16 [2, 2, 1024, 2048], P('pipe', None, 'ctx')
- boundary_grads: bfloat16 [2, 2, 1024, 2048], P('pipe', None, 'ctx')
- attn_gain_grad: float32 [2, 2048], P('pipe', 'ctx')
- w_query_grad: float32 [2, 2048, 2048], P('pipe', 'ctx', 'tensor')
- w_key_grad: float32 [2, 2048, 512], P('pipe', 'ctx', 'tensor')
- w_value_grad: float32 [2, 2048, 512], P('pipe', 'ctx', 'tensor')
- w_out_grad: float32 [2, 2048, 2048], P('pipe', 'tensor', 'ctx')
- ffn_gain_grad: float32 [2, 2048], P('pipe', 'ctx')
- w_gate_grad: float32 [2, 2048, 8192], P('pipe', 'ctx', 'tensor')
- w_up_grad: float32 [2, 2048, 8192], P('pipe', 'ctx', 'tensor')
- w_down_grad: float32 [2, 8192, 2048], P('pipe', 'tensor', 'ctx')
Inputs may be any that keep to these rules, and one draw needn't show every extreme that they name: positions[m, 0] = 0 and each entry is 0 or the entry before it plus 1, so sequences are runs of consecutive tokens; no sequence has more than 256 tokens and every micro-batch has one of exactly 256.
All inputs are finite; a program needn't handle non-finite values.
Results may differ from a plain program's by a relative error of at most 0.025.
Values may be sent and summed in bfloat16 or wider, within the bound.
No kernel may reach another device: no remote copies, remote signals or barrier semaphores. Data moves between devices by JAX's collectives and lax.ppermute only.
A program may use at most 320 MiB of HBM per device.

v0:
```python
import math

import jax
import jax.numpy as jnp
from jax import lax
from jax.sharding import PartitionSpec as P

HEADS = 32
KV_HEADS = 8
HEAD_DIM = 64
MAXLEN = 256


epsilon = 1e-05
rope_base = 500000.0


def from_behind(block, axis, distance):
    devices = range(lax.axis_size(axis))
    route = [(i - distance, i) for i in devices if i - distance in devices]
    return lax.ppermute(block, axis, route)


def rows_product(left, right):
    return lax.dot_general(
        left, right, (((0,), (0,)), ((), ())), preferred_element_type=jnp.float32
    )


def cols_product(left, right):
    return lax.dot_general(
        left, right, (((1,), (1,)), ((), ())), preferred_element_type=jnp.float32
    )


def rope_tables(positions_row, width):
    frequency = jnp.exp(
        jnp.arange(width // 2, dtype=jnp.float32) * (-2.0 * math.log(rope_base) / width)
    )
    angles = positions_row.astype(jnp.float32)[:, None] * frequency[None, :]
    cosine_table = jnp.concatenate([jnp.cos(angles), jnp.cos(angles)], axis=1)
    sine_table = jnp.concatenate([jnp.sin(angles), jnp.sin(angles)], axis=1)
    return (cosine_table, sine_table)


def rotate(values, cosine_table, sine_table):
    half_width = values.shape[-1] // 2
    turned = jnp.concatenate([-values[..., half_width:], values[..., :half_width]], axis=-1)
    return values * cosine_table[:, None, :] + turned * sine_table[:, None, :]


def rotate_back(grads_in, cosine_table, sine_table):
    half_width = grads_in.shape[-1] // 2
    scaled = grads_in * sine_table[:, None, :]
    turned = jnp.concatenate([-scaled[..., half_width:], scaled[..., :half_width]], axis=-1)
    return grads_in * cosine_table[:, None, :] - turned


def norm_forward(stream, gain_vector):
    inv_rms = lax.rsqrt(jnp.mean(stream * stream, axis=-1) + epsilon)
    return (stream * inv_rms[:, None] * gain_vector[None, :], inv_rms)


def norm_backward(stream, inv_rms, gain_vector, upstream):
    weighted = upstream * gain_vector[None, :]
    gain_grad = jnp.sum(upstream * stream * inv_rms[:, None], axis=0)
    inner_mean = jnp.mean(stream * weighted, axis=-1)
    stream_grad = (
        weighted * inv_rms[:, None] - stream * (inv_rms * inv_rms * inv_rms * inner_mean)[:, None]
    )
    return (stream_grad, gain_grad)


def scores(query_block, key_block, query_pos, query_index, key_index):
    raw_scores = jnp.einsum(
        "qkgd,skd->kgqs", query_block, key_block, preferred_element_type=jnp.float32
    ) * HEAD_DIM ** (-0.5)
    distance = query_index[:, None] - key_index[None, :]
    allowed = (distance >= 0) & (distance <= query_pos[:, None])
    return jnp.where(allowed[None, None], raw_scores, -1e30)


def attend(query_block, key_block, value_block, query_pos, query_index, key_index):
    masked = scores(query_block, key_block, query_pos, query_index, key_index)
    row_top = jnp.max(masked, axis=-1, keepdims=True)
    exponent = jnp.exp(masked - row_top)
    row_total = jnp.sum(exponent, axis=-1, keepdims=True)
    weights_block = (exponent / row_total).astype(jnp.bfloat16)
    mixed_rows = jnp.einsum(
        "kgqs,skd->qkgd", weights_block, value_block, preferred_element_type=jnp.float32
    )
    return (mixed_rows, (row_top + jnp.log(row_total))[..., 0])


def attend_back(
    query_block,
    key_block,
    value_block,
    query_pos,
    query_index,
    key_index,
    log_block,
    mixed_block,
    grad_block,
):
    masked = scores(query_block, key_block, query_pos, query_index, key_index)
    probability = jnp.exp(masked - log_block[..., None])
    prob_grad = jnp.einsum(
        "qkgd,skd->kgqs", grad_block, value_block, preferred_element_type=jnp.float32
    )
    row_delta = jnp.transpose(
        jnp.sum(grad_block.astype(jnp.float32) * mixed_block.astype(jnp.float32), axis=-1),
        (1, 2, 0),
    )
    score_grad = (probability * (prob_grad - row_delta[..., None])).astype(jnp.bfloat16)
    scale_factor = HEAD_DIM ** (-0.5)
    query_grad = (
        jnp.einsum("kgqs,skd->qkgd", score_grad, key_block, preferred_element_type=jnp.float32)
        * scale_factor
    )
    key_part = (
        jnp.einsum("kgqs,qkgd->skd", score_grad, query_block, preferred_element_type=jnp.float32)
        * scale_factor
    )
    value_part = jnp.einsum(
        "kgqs,qkgd->skd",
        probability.astype(jnp.bfloat16),
        grad_block,
        preferred_element_type=jnp.float32,
    )
    return (query_grad, key_part, value_part)


def attention_forward(queries, keys_window, values_window, positions_row, row_base):
    length = queries.shape[0]
    block_count = length // MAXLEN

    def one_block(block_index):
        row_start = block_index * MAXLEN
        query_index = row_base + row_start + jnp.arange(MAXLEN, dtype=jnp.int32)
        key_index = row_base + row_start - MAXLEN + jnp.arange(2 * MAXLEN, dtype=jnp.int32)
        return attend(queries, keys_window, values_window, positions_row, query_index, key_index)

    mixed_rows, log_totals = lax.map(one_block, jnp.arange(block_count, dtype=jnp.int32))
    return (mixed_rows.reshape((length,) + mixed_rows.shape[2:]), log_totals)


def attention_backward(
    queries, keys_window, values_window, positions_row, row_base, log_totals, mixed_all, grad_all
):
    length = queries.shape[0]
    block_count = length // MAXLEN
    zero_grads = jnp.zeros(keys_window.shape, jnp.float32)

    def one_block(carry, block_index):
        key_grads, value_grads = carry
        row_start = block_index * MAXLEN
        query_index = row_base + row_start + jnp.arange(MAXLEN, dtype=jnp.int32)
        key_index = row_base + row_start - MAXLEN + jnp.arange(2 * MAXLEN, dtype=jnp.int32)
        query_grad, key_part, value_part = attend_back(
            queries,
            keys_window,
            values_window,
            positions_row,
            query_index,
            key_index,
            log_totals[block_index],
            mixed_all,
            grad_all,
        )
        key_grads = key_grads + key_part
        value_grads = value_grads + value_part
        return ((key_grads, value_grads), query_grad)

    (key_grads, value_grads), query_grads = lax.scan(
        one_block, (zero_grads, zero_grads), jnp.arange(block_count, dtype=jnp.int32)
    )
    return (query_grads.reshape((length,) + query_grads.shape[2:]), key_grads, value_grads)


def layer_forward(stream_bf, positions_row, weights, row_base):
    attn_gain, w_query, w_key, w_value, w_out, ffn_gain, w_gate, w_up, w_down = weights
    length = stream_bf.shape[0]
    local_heads = w_query.shape[1] // HEAD_DIM
    local_groups = w_key.shape[1] // HEAD_DIM
    stream_in = stream_bf.astype(jnp.float32)
    normed, inv_attn = norm_forward(stream_in, attn_gain.astype(jnp.float32))
    normed_attn = normed.astype(jnp.bfloat16)
    cosine_table, sine_table = rope_tables(positions_row, HEAD_DIM)
    queries = rotate(
        jnp.dot(normed_attn, w_query, preferred_element_type=jnp.float32).reshape(
            length, local_heads, HEAD_DIM
        ),
        cosine_table,
        sine_table,
    ).astype(jnp.bfloat16)
    keys_own = rotate(
        jnp.dot(normed_attn, w_key, preferred_element_type=jnp.float32).reshape(
            length, local_groups, HEAD_DIM
        ),
        cosine_table,
        sine_table,
    ).astype(jnp.bfloat16)
    values_own = (
        jnp.dot(normed_attn, w_value, preferred_element_type=jnp.float32)
        .astype(jnp.bfloat16)
        .reshape(length, local_groups, HEAD_DIM)
    )
    keys_tail, values_tail = from_behind((keys_own, values_own), "ctx", 1)
    keys_window = jnp.concatenate([keys_tail, keys_own], axis=0)
    values_window = jnp.concatenate([values_tail, values_own], axis=0)
    grouped = queries.reshape(length, local_groups, HEADS // KV_HEADS, HEAD_DIM)
    mixed_rows, log_totals = attention_forward(
        grouped, keys_window, values_window, positions_row, row_base
    )
    attn_mixed = mixed_rows.astype(jnp.bfloat16).reshape(length, local_heads * HEAD_DIM)
    partial_attn = jnp.dot(attn_mixed, w_out, preferred_element_type=jnp.float32)
    stream_mid = stream_in + lax.psum(partial_attn, "tensor")
    normed_two, inv_ffn = norm_forward(stream_mid, ffn_gain.astype(jnp.float32))
    normed_ffn = normed_two.astype(jnp.bfloat16)
    gate_proj = jnp.dot(normed_ffn, w_gate, preferred_element_type=jnp.float32)
    up_proj = jnp.dot(normed_ffn, w_up, preferred_element_type=jnp.float32)
    hidden = (jax.nn.silu(gate_proj) * up_proj).astype(jnp.bfloat16)
    partial_ffn = jnp.dot(hidden, w_down, preferred_element_type=jnp.float32)
    stream_out = (stream_mid + lax.psum(partial_ffn, "tensor")).astype(jnp.bfloat16)
    saved_state = (
        stream_in,
        inv_attn,
        normed_attn,
        grouped,
        keys_window,
        values_window,
        positions_row,
        cosine_table,
        sine_table,
        log_totals,
        attn_mixed,
        stream_mid,
        inv_ffn,
        normed_ffn,
        gate_proj,
        up_proj,
        hidden,
    )
    return (stream_out, saved_state)


def layer_backward(upstream, saved_state, weights, row_base):
    attn_gain, w_query, w_key, w_value, w_out, ffn_gain, w_gate, w_up, w_down = weights
    (
        stream_in,
        inv_attn,
        normed_attn,
        grouped,
        keys_window,
        values_window,
        positions_row,
        cosine_table,
        sine_table,
        log_totals,
        attn_mixed,
        stream_mid,
        inv_ffn,
        normed_ffn,
        gate_proj,
        up_proj,
        hidden,
    ) = saved_state
    length = stream_in.shape[0]
    local_heads = w_query.shape[1] // HEAD_DIM
    local_groups = w_key.shape[1] // HEAD_DIM
    upstream_b = upstream.astype(jnp.bfloat16)
    down_term = rows_product(hidden, upstream_b)
    hidden_grad = cols_product(upstream_b, w_down)
    sigmoid_gate = jax.nn.sigmoid(gate_proj)
    gate_grad = (
        hidden_grad * up_proj * sigmoid_gate * (1.0 + gate_proj * (1.0 - sigmoid_gate))
    ).astype(jnp.bfloat16)
    up_grad = (hidden_grad * gate_proj * sigmoid_gate).astype(jnp.bfloat16)
    gate_term = rows_product(normed_ffn, gate_grad)
    up_term = rows_product(normed_ffn, up_grad)
    partial_ffn_grad = cols_product(gate_grad, w_gate) + cols_product(up_grad, w_up)
    normed_ffn_grad = lax.psum(partial_ffn_grad, "tensor")
    mid_part, ffn_gain_term = norm_backward(
        stream_mid, inv_ffn, ffn_gain.astype(jnp.float32), normed_ffn_grad
    )
    mid_grad = upstream + mid_part
    mid_grad_b = mid_grad.astype(jnp.bfloat16)
    out_term = rows_product(attn_mixed, mid_grad_b)
    mixed_grad = cols_product(mid_grad_b, w_out).astype(jnp.bfloat16)
    grouped_shape = grouped.shape
    query_grads, key_grads, value_grads = attention_backward(
        grouped,
        keys_window,
        values_window,
        positions_row,
        row_base,
        log_totals,
        attn_mixed.reshape(grouped_shape),
        mixed_grad.reshape(grouped_shape),
    )
    back_keys, back_values = from_behind((key_grads[:MAXLEN], value_grads[:MAXLEN]), "ctx", -1)
    key_own = key_grads[MAXLEN:]
    value_own = value_grads[MAXLEN:]
    key_own = jnp.concatenate([key_own[: length - MAXLEN], key_own + back_keys], axis=0)
    value_own = jnp.concatenate([value_own[: length - MAXLEN], value_own + back_values], axis=0)
    query_grad_b = (
        rotate_back(query_grads.reshape(length, local_heads, HEAD_DIM), cosine_table, sine_table)
        .astype(jnp.bfloat16)
        .reshape(length, local_heads * HEAD_DIM)
    )
    key_grad_b = (
        rotate_back(key_own, cosine_table, sine_table)
        .astype(jnp.bfloat16)
        .reshape(length, local_groups * HEAD_DIM)
    )
    value_grad_b = value_own.astype(jnp.bfloat16).reshape(length, local_groups * HEAD_DIM)
    query_term = rows_product(normed_attn, query_grad_b)
    key_term = rows_product(normed_attn, key_grad_b)
    value_term = rows_product(normed_attn, value_grad_b)
    partial_grad = (
        cols_product(query_grad_b, w_query)
        + cols_product(key_grad_b, w_key)
        + cols_product(value_grad_b, w_value)
    )
    normed_attn_grad = lax.psum(partial_grad, "tensor")
    input_part, attn_gain_term = norm_backward(
        stream_in, inv_attn, attn_gain.astype(jnp.float32), normed_attn_grad
    )
    sent_grad = (mid_grad + input_part).astype(jnp.bfloat16)
    return (
        sent_grad,
        (
            attn_gain_term,
            query_term,
            key_term,
            value_term,
            out_term,
            ffn_gain_term,
            gate_term,
            up_term,
            down_term,
        ),
    )


def on_device(
    inputs,
    out_grad,
    positions,
    attn_gain,
    w_query,
    w_key,
    w_value,
    w_out,
    ffn_gain,
    w_gate,
    w_up,
    w_down,
):
    section_index = lax.axis_index("pipe")
    first_section = section_index == 0
    weights = (
        lax.all_gather(attn_gain[0], "ctx", axis=0, tiled=True),
        lax.all_gather(w_query[0], "ctx", axis=0, tiled=True),
        lax.all_gather(w_key[0], "ctx", axis=0, tiled=True),
        lax.all_gather(w_value[0], "ctx", axis=0, tiled=True),
        lax.all_gather(w_out[0], "ctx", axis=1, tiled=True),
        lax.all_gather(ffn_gain[0], "ctx", axis=0, tiled=True),
        lax.all_gather(w_gate[0], "ctx", axis=0, tiled=True),
        lax.all_gather(w_up[0], "ctx", axis=0, tiled=True),
        lax.all_gather(w_down[0], "ctx", axis=1, tiled=True),
    )
    length = inputs.shape[1]
    micro_count = inputs.shape[0]
    row_base = lax.axis_index("ctx") * length
    received = jnp.zeros(inputs.shape[1:], jnp.bfloat16)
    produced = []
    saved = []
    for clock_step in range(micro_count + 1):
        own_micro = min(clock_step, micro_count - 1)
        prior_micro = max(clock_step - 1, 0)
        stream = jnp.where(first_section, inputs[own_micro], received)
        positions_row = jnp.where(first_section, positions[own_micro], positions[prior_micro])
        rounded_out, saved_state = layer_forward(stream, positions_row, weights, row_base)
        produced.append(rounded_out)
        saved.append(saved_state)
        if clock_step < micro_count:
            received = from_behind(rounded_out, "pipe", 1)
    section_outputs = jnp.stack(
        [
            jnp.where(first_section, produced[micro_index], produced[micro_index + 1])
            for micro_index in range(micro_count)
        ]
    )
    returned = jnp.zeros(inputs.shape[1:], jnp.bfloat16)
    boundary = []
    shares = None
    for clock_step in range(micro_count + 1):
        micro_index = clock_step - 1 + section_index
        is_valid = (micro_index >= 0) & (micro_index < micro_count)
        arriving = jnp.where(first_section, returned, out_grad[min(clock_step, micro_count - 1)])
        upstream = jnp.where(is_valid, arriving.astype(jnp.float32), 0.0)
        saved_state = jax.tree.map(
            lambda from_early, from_late: jnp.where(first_section, from_early, from_late),
            saved[max(clock_step - 1, 0)],
            saved[min(clock_step + 1, micro_count)],
        )
        sent_grad, weight_grads = layer_backward(upstream, saved_state, weights, row_base)
        boundary.append(sent_grad)
        if clock_step < micro_count:
            returned = from_behind(sent_grad, "pipe", -1)
        tick_share = (
            lax.psum_scatter(weight_grads[0], "ctx", scatter_dimension=0, tiled=True),
            lax.psum_scatter(weight_grads[1], "ctx", scatter_dimension=0, tiled=True),
            lax.psum_scatter(weight_grads[2], "ctx", scatter_dimension=0, tiled=True),
            lax.psum_scatter(weight_grads[3], "ctx", scatter_dimension=0, tiled=True),
            lax.psum_scatter(weight_grads[4], "ctx", scatter_dimension=1, tiled=True),
            lax.psum_scatter(weight_grads[5], "ctx", scatter_dimension=0, tiled=True),
            lax.psum_scatter(weight_grads[6], "ctx", scatter_dimension=0, tiled=True),
            lax.psum_scatter(weight_grads[7], "ctx", scatter_dimension=0, tiled=True),
            lax.psum_scatter(weight_grads[8], "ctx", scatter_dimension=1, tiled=True),
        )
        shares = tick_share if shares is None else jax.tree.map(jnp.add, shares, tuple(tick_share))
    shares = tuple(shares)
    boundary_grads = jnp.stack(
        [
            jnp.where(first_section, boundary[micro_index + 1], boundary[micro_index])
            for micro_index in range(micro_count)
        ]
    )
    return (
        section_outputs[None],
        boundary_grads[None],
        shares[0][None],
        shares[1][None],
        shares[2][None],
        shares[3][None],
        shares[4][None],
        shares[5][None],
        shares[6][None],
        shares[7][None],
        shares[8][None],
    )


def solution(mesh):
    in_specs = (
        P(None, "ctx", None),
        P(None, "ctx", None),
        P(None, "ctx"),
        P("pipe", "ctx"),
        P("pipe", "ctx", "tensor"),
        P("pipe", "ctx", "tensor"),
        P("pipe", "ctx", "tensor"),
        P("pipe", "tensor", "ctx"),
        P("pipe", "ctx"),
        P("pipe", "ctx", "tensor"),
        P("pipe", "ctx", "tensor"),
        P("pipe", "tensor", "ctx"),
    )
    out_specs = (
        P("pipe", None, "ctx", None),
        P("pipe", None, "ctx", None),
        P("pipe", "ctx"),
        P("pipe", "ctx", "tensor"),
        P("pipe", "ctx", "tensor"),
        P("pipe", "ctx", "tensor"),
        P("pipe", "tensor", "ctx"),
        P("pipe", "ctx"),
        P("pipe", "ctx", "tensor"),
        P("pipe", "ctx", "tensor"),
        P("pipe", "tensor", "ctx"),
    )
    return jax.shard_map(
        on_device, mesh=mesh, in_specs=in_specs, out_specs=out_specs, check_vma=False
    )
```

profile of v0, /device:TPU:0, one launch (start us, length us, event | category | flops | bytes accessed | tf_op | source)
XLA Modules:
  0.0 2281.4 jit_solution(17500128762599029235)
XLA Ops:
  23.5 11.3 all-gather.2
  40.2 14.3 all-gather.1
  70.5 21.1 all-gather.17.cloned.1.call-done
  105.4 76.5 %all-reduce.16.cloned.1.call-done = f32[256,2048]{1,0:T(8,128)} async-done(((f32[256,2048]{1,0:T(8,128)}), f32[256,2048]{1,0:T(8,128)}) %all-reduce.16.cloned.1.call-update) | async-done | bytes 2097168 | tf_op jit(solution)/shard_map/psum | solution.py:218
  184.7 85.7 %all-gather.19.cloned.1.call-done = bf16[1,2048,2048]{2,1,0:T(8,128)(2,1)} async-done(((bf16[1,512,2048]{2,1,0:T(8,128)(2,1)}), bf16[1,2048,2048]{2,1,0:T(8,128)(2,1)}) %all-gather.19.cloned.1.call-update) | async-done | bytes 8388624 | tf_op jit(solution)/shard_map/all_gather | solution.py:370
  277.4 82.5 %all-gather.21.cloned.1.call-done = bf16[1,2048,2048]{2,1,0:T(8,128)(2,1)} async-done(((bf16[1,512,2048]{2,1,0:T(8,128)(2,1)}), bf16[1,2048,2048]{2,1,0:T(8,128)(2,1)}) %all-gather.21.cloned.1.call-update) | async-done | bytes 8388624 | tf_op jit(solution)/shard_map/all_gather | solution.py:371
  368.1 81.1 %all-gather.23.cloned.1.call-done = bf16[1,2048,2048]{2,1,0:T(8,128)(2,1)} async-done(((bf16[1,2048,512]{2,1,0:T(8,128)(2,1)}), bf16[1,2048,2048]{2,1,0:T(8,128)(2,1)}) %all-gather.23.cloned.1.call-update) | async-done | bytes 8388624 | tf_op jit(solution)/shard_map/all_gather | solution.py:372
  456.7 86.6 %all-reduce.18.cloned.1.call-done = f32[256,2048]{1,0:T(8,128)} async-done(((f32[256,2048]{1,0:T(8,128)}), f32[256,2048]{1,0:T(8,128)}) %all-reduce.18.cloned.1.call-update) | async-done | bytes 2097168 | tf_op jit(solution)/shard_map/psum | solution.py:225
  566.9 86.1 %all-reduce.20.cloned.1.call-done = f32[256,2048]{1,0:T(8,128)} async-done(((f32[256,2048]{1,0:T(8,128)}), f32[256,2048]{1,0:T(8,128)}) %all-reduce.20.cloned.1.call-update) | async-done | bytes 2097168 | tf_op jit(solution)/shard_map/psum | solution.py:218
  699.5 154.4 %all-reduce.32.cloned.1.call-done = (f32[256,2048]{1,0:T(8,128)}, f32[256,2048]{1,0:T(8,128)}) async-done(((f32[256,2048]{1,0:T(8,128)}, f32[256,2048]{1,0:T(8,128)}), (f32[256,2048]{1,0:T(8,128)}, f32[256,2048]{1,0:T(8,128)})) %all-reduce.32.cloned.1.call-update) | async-done | bytes 4194320 | tf_op jit(solution)/shard_map/psum | solution.py:225
  907.5 157.2 %all-reduce.30.cloned.1.call-done = (f32[256,2048]{1,0:T(8,128)}, f32[256,2048]{1,0:T(8,128)}) async-done(((f32[256,2048]{1,0:T(8,128)}, f32[256,2048]{1,0:T(8,128)}), (f32[256,2048]{1,0:T(8,128)}, f32[256,2048]{1,0:T(8,128)})) %all-reduce.30.cloned.1.call-update) | async-done | bytes 4194320 | tf_op jit(solution)/shard_map/psum | solution.py:218
  1108.2 82.0 %all-reduce.22.cloned.1.call-done = f32[256,2048]{1,0:T(8,128)} async-done(((f32[256,2048]{1,0:T(8,128)}), f32[256,2048]{1,0:T(8,128)}) %all-reduce.22.cloned.1.call-update) | async-done | bytes 2097168 | tf_op jit(solution)/shard_map/psum | solution.py:283
  1221.9 86.1 %all-reduce.24.cloned.1.call-done = f32[256,2048]{1,0:T(8,128)} async-done(((f32[256,2048]{1,0:T(8,128)}), f32[256,2048]{1,0:T(8,128)}) %all-reduce.24.cloned.1.call-update) | async-done | bytes 2097168 | tf_op jit(solution)/shard_map/psum | solution.py:326
  1322.3 12.2 multiply_convert_fusion.1
  1360.1 74.0 %all-reduce.26.cloned.1.call-done = f32[256,2048]{1,0:T(8,128)} async-done(((f32[256,2048]{1,0:T(8,128)}), f32[256,2048]{1,0:T(8,128)}) %all-reduce.26.cloned.1.call-update) | async-done | bytes 2097168 | tf_op jit(solution)/shard_map/psum | solution.py:283
  1469.5 150.9 %all-reduce.28.cloned.1.call-done = (f32[256,2048]{1,0:T(8,128)}, f32[256,2048]{1,0:T(8,128)}) async-done(((f32[256,2048]{1,0:T(8,128)}, f32[256,2048]{1,0:T(8,128)}), (f32[256,2048]{1,0:T(8,128)}, f32[256,2048]{1,0:T(8,128)})) %all-reduce.28.cloned.1.call-update) | async-done | bytes 4194320 | tf_op jit(solution)/shard_map/psum | solution.py:225
  1665.6 19.0 add_add_fusion.2
  1703.3 19.4 add_add_fusion.1
  1742.6 18.8 add_add_fusion
  1763.4 16.7 all-reduce.5
  1785.2 16.1 reduce-scatter.8.cloned.1.call-done
  1801.2 157.8 %reduce-scatter.16.cloned.1.call-done = f32[512,2048]{1,0:T(8,128)} async-done(((f32[2048,2048]{1,0:T(8,128)}), f32[512,2048]{1,0:T(8,128)}) %reduce-scatter.16.cloned.1.call-update) | async-done | bytes 4194320 | tf_op jit(solution)/shard_map/reduce_scatter | solution.py:420
  1959.0 157.6 %reduce-scatter.18.cloned.1.call-done = f32[512,2048]{1,0:T(8,128)} async-done(((f32[2048,2048]{1,0:T(8,128)}), f32[512,2048]{1,0:T(8,128)}) %reduce-scatter.18.cloned.1.call-update) | async-done | bytes 4194320 | tf_op jit(solution)/shard_map/reduce_scatter | solution.py:421
  2116.6 157.8 %reduce-scatter.20.cloned.1.call-done = f32[2048,512]{1,0:T(8,128)} async-done(((f32[2048,2048]{1,0:T(8,128)}), f32[2048,512]{1,0:T(8,128)}) %reduce-scatter.20.cloned.1.call-update) | async-done | bytes 4194320 | tf_op jit(solution)/shard_map/reduce_scatter | solution.py:422
  (687 shorter events, 438.4 us)
Async XLA Ops:
  7.2 52.9 %all-gather.15.cloned.1.call-start = ((), (), s32[]{:S(2)}) async-start(), calls=%async_computation.13 | async-start | bytes 2621440 | tf_op jit(solution)/shard_map/all_gather | solution.py:365
  7.9 83.7 %all-gather.17.cloned.1.call-start = ((), (), s32[]{:S(2)}) async-start(), calls=%async_computation.14 | async-start | bytes 2621440 | tf_op jit(solution)/shard_map/all_gather | solution.py:368
  8.7 173.3 %all-reduce.16.cloned.1.call-start = ((), (), s32[]{:S(2)}) async-start(), calls=%async_computation.7 | async-start | bytes 4194304 | tf_op jit(solution)/shard_map/psum | solution.py:218
  37.8 28.8 %collective-permute-start.1 = (bf16[256,2,64]{0,2,1:T(8,128)(2,1)S(1)}, bf16[256,2,64]{0,2,1:T(8,128)(2,1)S(1)}, u32[]{:S(2)}, u32[]{:S(2)}) collective-permute-start(bf16[256,2,64]{0,2,1:T(8,128)(2,1)S(1)} %fusion.223), channel_id=1, source_target_pairs={{0,4},{4,8},{8,12},{1,5},{5,9},{9,13},{2,6},{6,10},{10,14},{3,7},{... | collective-permute-start | bytes 196616 | tf_op jit(solution)/shard_map/ppermute | solution.py:21
  95.3 175.1 %all-gather.19.cloned.1.call-start = ((), (), s32[]{:S(2)}) async-start(), calls=%async_computation.15 | async-start | bytes 10485760 | tf_op jit(solution)/shard_map/all_gather | solution.py:370
  95.9 264.0 %all-gather.21.cloned.1.call-start = ((), (), s32[]{:S(2)}) async-start(), calls=%async_computation.16 | async-start | bytes 10485760 | tf_op jit(solution)/shard_map/all_gather | solution.py:371
  96.5 352.7 %all-gather.23.cloned.1.call-start = ((), (), s32[]{:S(2)}) async-start(), calls=%async_computation.17 | async-start | bytes 10485760 | tf_op jit(solution)/shard_map/all_gather | solution.py:372
  97.0 446.3 %all-reduce.18.cloned.1.call-start = ((), (), s32[]{:S(2)}) async-start(), calls=%async_computation.8 | async-start | bytes 4194304 | tf_op jit(solution)/shard_map/psum | solution.py:225
  456.7 196.4 %all-reduce.20.cloned.1.call-start = ((), (), s32[]{:S(2)}) async-start(), calls=%async_computation.9 | async-start | bytes 4194304 | tf_op jit(solution)/shard_map/psum | solution.py:218
  566.8 287.1 %all-reduce.32.cloned.1.call-start = ((), (), s32[]{:S(2)}) async-start(), calls=%async_computation.27 | async-start | bytes 8388608 | tf_op jit(solution)/shard_map/psum | solution.py:225
  699.5 365.3 %all-reduce.30.cloned.1.call-start = ((), (), s32[]{:S(2)}) async-start(), calls=%async_computation.26 | async-start | bytes 8388608 | tf_op jit(solution)/shard_map/psum | solution.py:218
  870.3 15.3 collective-permute-start.7
  874.3 23.3 %collective-permute-start.6 = (bf16[256,2,64]{0,2,1:T(8,128)(2,1)}, bf16[256,2,64]{0,2,1:T(8,128)(2,1)}, u32[]{:S(2)}, u32[]{:S(2)}) collective-permute-start(bf16[256,2,64]{0,2,1:T(8,128)(2,1)} %bitcast.42), channel_id=1, source_target_pairs={{0,4},{4,8},{8,12},{1,5},{5,9},{9,13},{2,6},{6,10},{10,14},{3,7},{... | collective-permute-start | bytes 196616 | tf_op jit(solution)/shard_map/ppermute | solution.py:21
  907.5 282.7 %all-reduce.22.cloned.1.call-start = ((), (), s32[]{:S(2)}) async-start(), calls=%async_computation.10 | async-start | bytes 4194304 | tf_op jit(solution)/shard_map/psum | solution.py:283
  1104.3 203.7 %all-reduce.24.cloned.1.call-start = ((), (), s32[]{:S(2)}) async-start(), calls=%async_computation.11 | async-start | bytes 4194304 | tf_op jit(solution)/shard_map/psum | solution.py:326
  1221.9 212.2 %all-reduce.26.cloned.1.call-start = ((), (), s32[]{:S(2)}) async-start(), calls=%async_computation.12 | async-start | bytes 4194304 | tf_op jit(solution)/shard_map/psum | solution.py:283
  1348.5 272.0 %all-reduce.28.cloned.1.call-start = ((), (), s32[]{:S(2)}) async-start(), calls=%async_computation.25 | async-start | bytes 8388608 | tf_op jit(solution)/shard_map/psum | solution.py:225
  1465.5 319.7 %reduce-scatter.10.cloned.1.call-start = ((), (), s32[]{:S(2)}) async-start(), calls=%async_computation.19 | async-start | bytes 1310720 | tf_op jit(solution)/shard_map/reduce_scatter | solution.py:416
  1630.4 154.8 %reduce-scatter.12.cloned.1.call-start = ((), (), s32[]{:S(2)}) async-start(), calls=%async_computation.20 | async-start | bytes 1310720 | tf_op jit(solution)/shard_map/reduce_scatter | solution.py:417
  1633.7 151.5 %reduce-scatter.14.cloned.1.call-start = ((), (), s32[]{:S(2)}) async-start(), calls=%async_computation.21 | async-start | bytes 5242880 | tf_op jit(solution)/shard_map/reduce_scatter | solution.py:418
  1640.2 161.0 %reduce-scatter.8.cloned.1.call-start = ((), (), s32[]{:S(2)}) async-start(), calls=%async_computation.18 | async-start | bytes 5242880 | tf_op jit(solution)/shard_map/reduce_scatter | solution.py:415
  1646.3 312.7 %reduce-scatter.16.cloned.1.call-start = ((), (), s32[]{:S(2)}) async-start(), calls=%async_computation.22 | async-start | bytes 20971520 | tf_op jit(solution)/shard_map/reduce_scatter | solution.py:420
  1684.6 432.0 %reduce-scatter.18.cloned.1.call-start = ((), (), s32[]{:S(2)}) async-start(), calls=%async_computation.23 | async-start | bytes 20971520 | tf_op jit(solution)/shard_map/reduce_scatter | solution.py:421
  1722.8 551.6 %reduce-scatter.20.cloned.1.call-start = ((), (), s32[]{:S(2)}) async-start(), calls=%async_computation.24 | async-start | bytes 20971520 | tf_op jit(solution)/shard_map/reduce_scatter | solution.py:422
  (220 other events, 2076.1 us)
Sparse Core Ops, SparseCore 0:
  9.9 44.6 all-gather.14
  56.4 35.1 all-gather.16
  95.4 86.5 all-reduce.15
  183.8 86.5 all-gather.18
  272.2 87.5 all-gather.20
  361.7 87.4 all-gather.22
  456.8 86.4 all-reduce.17
  567.0 86.0 all-reduce.19
  699.6 154.2 all-reduce.31
  907.6 157.1 all-reduce.29
  1104.4 85.7 all-reduce.21
  1222.0 85.9 all-reduce.23
  1348.6 85.4 all-reduce.25
  1465.6 154.7 all-reduce.27
  1630.5 26.7 reduce-scatter.9
  1660.6 27.7 reduce-scatter.11
  1692.0 52.6 reduce-scatter.13
  1748.1 53.1 reduce-scatter.7
  1805.2 153.7 reduce-scatter.15
  1962.8 153.7 reduce-scatter.17
  2120.6 153.7 reduce-scatter.19
where the time goes:
time: 2290 us; the launch traced here: 2280 us
  waiting for transfers between devices  1730 us (76%)
  matrix products  327 us (14%)
  other arithmetic  73.3 us (3%)
  blocking collectives  60.2 us (3%)
  starting transfers between devices  38 us (2%)
  local copies, waits for them, and re-layouts  31.8 us (1%)
    psum x3, waiting for transfers between devices, layer_forward(): lax.psum(partial_ffn, 'tensor')  392 us
    psum x3, waiting for transfers between devices, layer_forward(): stream_mid = stream_in + lax.psum(partial_attn, 'tensor')  320 us
    reduce_scatter x1, waiting for transfers between devices, on_device(): lax.psum_scatter(weight_grads[6], 'ctx', scatter_dimension=0, tiled=True)  158 us
    reduce_scatter x1, waiting for transfers between devices, on_device(): lax.psum_scatter(weight_grads[8], 'ctx', scatter_dimension=1, tiled=True)  158 us
    reduce_scatter x1, waiting for transfers between devices, on_device(): lax.psum_scatter(weight_grads[7], 'ctx', scatter_dimension=0, tiled=True)  158 us
    psum x2, waiting for transfers between devices, layer_backward(): normed_ffn_grad = lax.psum(partial_ffn_grad, 'tensor')  156 us
    dot_general x21, matrix products, rows_product(): lax.dot_general(left, right, (((0,), (0,)), ((), ())), preferred_element_...  128 us
    psum x1, waiting for transfers between devices, layer_backward(): normed_attn_grad = lax.psum(partial_grad, 'tensor')  86.1 us
  transfers between devices with their start and end apart: 37, of which 24 were waited for; matrix products, arithmetic and copies ran while one was open for 10% of the time, Pallas kernels for 0%

commit v1 on v0

v1 whole, which is shorter than its diff:
```python
import math

import jax
import jax.numpy as jnp
from jax import lax
from jax.sharding import PartitionSpec as P

HEADS = 32
KV_HEADS = 8
HEAD_DIM = 64
MAXLEN = 256

epsilon = 1e-05
rope_base = 500000.0
bf16 = jnp.bfloat16
f32 = jnp.float32


def swap_cores(block):
    return lax.ppermute(block, "pipe", [(0, 1), (1, 0)])


def from_behind(block, axis, distance):
    devices = range(lax.axis_size(axis))
    route = [(i - distance, i) for i in devices if i - distance in devices]
    return lax.ppermute(block, axis, route)


def product(left, right):
    return lax.dot_general(
        left, right, (((1,), (0,)), ((), ())), preferred_element_type=f32
    )


def rows_product(left, right):
    return lax.dot_general(
        left, right, (((0,), (0,)), ((), ())), preferred_element_type=f32
    )


def cols_product(left, right):
    return lax.dot_general(
        left, right, (((1,), (1,)), ((), ())), preferred_element_type=f32
    )


def rope_tables(positions_row, width):
    frequency = jnp.exp(
        jnp.arange(width // 2, dtype=f32) * (-2.0 * math.log(rope_base) / width)
    )
    angles = positions_row.astype(f32)[:, None] * frequency[None, :]
    cosine_table = jnp.concatenate([jnp.cos(angles), jnp.cos(angles)], axis=1)
    sine_table = jnp.concatenate([jnp.sin(angles), jnp.sin(angles)], axis=1)
    return (cosine_table, sine_table)


def rotate(values, cosine_table, sine_table):
    half_width = values.shape[-1] // 2
    turned = jnp.concatenate([-values[..., half_width:], values[..., :half_width]], axis=-1)
    return values * cosine_table[:, None, :] + turned * sine_table[:, None, :]


def rotate_back(grads_in, cosine_table, sine_table):
    half_width = grads_in.shape[-1] // 2
    scaled = grads_in * sine_table[:, None, :]
    turned = jnp.concatenate([-scaled[..., half_width:], scaled[..., :half_width]], axis=-1)
    return grads_in * cosine_table[:, None, :] - turned


def norm_forward(stream, gain_vector):
    inv_rms = lax.rsqrt(jnp.mean(stream * stream, axis=-1) + epsilon)
    return ((stream * inv_rms[:, None] * gain_vector[None, :]).astype(bf16), inv_rms)


def norm_backward(stream, inv_rms, gain_vector, upstream):
    weighted = upstream * gain_vector[None, :]
    gain_grad = jnp.sum(upstream * stream * inv_rms[:, None], axis=0)
    inner_mean = jnp.mean(stream * weighted, axis=-1)
    stream_grad = (
        weighted * inv_rms[:, None] - stream * (inv_rms * inv_rms * inv_rms * inner_mean)[:, None]
    )
    return (stream_grad, gain_grad)


def scores(query_block, key_block, allowed):
    raw_scores = jnp.einsum(
        "qkgd,skd->kgqs", query_block, key_block, preferred_element_type=f32
    ) * HEAD_DIM ** (-0.5)
    return jnp.where(allowed[None, None], raw_scores, -1e30)


def attend(query_block, key_block, value_block, allowed):
    masked = scores(query_block, key_block, allowed)
    row_top = jnp.max(masked, axis=-1, keepdims=True)
    exponent = jnp.exp(masked - row_top)
    row_total = jnp.sum(exponent, axis=-1, keepdims=True)
    weights_block = (exponent / row_total).astype(bf16)
    mixed_rows = jnp.einsum(
        "kgqs,skd->qkgd", weights_block, value_block, preferred_element_type=f32
    )
    return (mixed_rows, (row_top + jnp.log(row_total))[..., 0])


def attend_back(
    query_block, key_block, value_block, allowed, log_block, mixed_block, grad_block
):
    masked = scores(query_block, key_block, allowed)
    probability = jnp.exp(masked - log_block[..., None])
    prob_grad = jnp.einsum(
        "qkgd,skd->kgqs", grad_block, value_block, preferred_element_type=f32
    )
    row_delta = jnp.transpose(
        jnp.sum(grad_block.astype(f32) * mixed_block.astype(f32), axis=-1),
        (1, 2, 0),
    )
    score_grad = (probability * (prob_grad - row_delta[..., None])).astype(bf16)
    scale_factor = HEAD_DIM ** (-0.5)
    query_grad = (
        jnp.einsum("kgqs,skd->qkgd", score_grad, key_block, preferred_element_type=f32)
        * scale_factor
    )
    key_part = (
        jnp.einsum("kgqs,qkgd->skd", score_grad, query_block, preferred_element_type=f32)
        * scale_factor
    )
    value_part = jnp.einsum(
        "kgqs,qkgd->skd",
        probability.astype(bf16),
        grad_block,
        preferred_element_type=f32,
    )
    return (query_grad, key_part, value_part)


def sum_tensor(partial):
    return lax.psum(partial.astype(bf16), "tensor").astype(f32)


def own_share(partial, rows):
    arrived = swap_cores(partial[rows:].astype(bf16))
    return partial[:rows] + arrived.astype(f32)


def attention_forward(stream, gain, wide, place):
    allowed, cosine, sine, sizes = place
    n_query, n_key = sizes
    rows = stream.shape[0]
    groups = n_key // HEAD_DIM
    normed, inv_rms = norm_forward(stream, gain)
    raw = product(normed, wide[:, : n_query + 2 * n_key])
    queries = rotate(raw[:, :n_query].reshape(rows, -1, HEAD_DIM), cosine, sine).astype(bf16)
    keys = rotate(
        raw[:, n_query : n_query + n_key].reshape(rows, -1, HEAD_DIM), cosine, sine
    ).astype(bf16)
    values = raw[:, n_query + n_key :].astype(bf16)
    own = jnp.concatenate([keys.reshape(rows, n_key), values], axis=1)
    tail = from_behind(own, "ctx", 1)
    window = jnp.concatenate([tail, own], axis=0)
    keys_window = window[:, :n_key].reshape(2 * rows, groups, HEAD_DIM)
    values_window = window[:, n_key:].reshape(2 * rows, groups, HEAD_DIM)
    grouped = queries.reshape(rows, groups, HEADS // KV_HEADS, HEAD_DIM)
    mixed_rows, log_totals = attend(grouped, keys_window, values_window, allowed)
    mixed = mixed_rows.astype(bf16).reshape(rows, n_query)
    partial = cols_product(mixed, wide[:, n_query + 2 * n_key :])
    middle = stream + sum_tensor(partial)
    saved = (stream, inv_rms, normed, grouped, keys_window, values_window, log_totals, mixed)
    return middle, saved


def ffn_forward_in(middle, gain, wide, hidden_width):
    normed, inv_rms = norm_forward(middle, gain)
    both = jnp.concatenate([normed, swap_cores(normed)], axis=0)
    gate_up = product(both, wide[:, : 2 * hidden_width])
    gate = gate_up[:, :hidden_width]
    up = gate_up[:, hidden_width:]
    hidden = (jax.nn.silu(gate) * up).astype(bf16)
    return (middle, inv_rms, both, gate, up, hidden)


def ffn_forward_out(state, wide, hidden_width):
    middle, hidden = state[0], state[-1]
    partial = cols_product(hidden, wide[:, 2 * hidden_width :])
    return (middle + sum_tensor(own_share(partial, middle.shape[0]))).astype(bf16)


def ffn_backward(upstream, upstream_both, state, gain, wide, hidden_width):
    middle, inv_rms, both, gate, up, hidden = state
    hidden_grad = product(upstream_both, wide[:, 2 * hidden_width :])
    sigmoid_gate = jax.nn.sigmoid(gate)
    gate_grad = (hidden_grad * up * sigmoid_gate * (1.0 + gate * (1.0 - sigmoid_gate))).astype(bf16)
    up_grad = (hidden_grad * gate * sigmoid_gate).astype(bf16)
    grads = jnp.concatenate([gate_grad, up_grad], axis=1)
    partial = cols_product(grads, wide[:, : 2 * hidden_width])
    normed_grad = sum_tensor(own_share(partial, middle.shape[0]))
    down_term = rows_product(upstream_both, hidden).astype(bf16)
    wide_term = rows_product(both, grads).astype(bf16)
    mid_part, gain_term = norm_backward(middle, inv_rms, gain, normed_grad)
    return upstream + mid_part, gain_term, wide_term, down_term


def attention_backward(mid_grad, saved, gain, wide, place):
    allowed, cosine, sine, sizes = place
    n_query, n_key = sizes
    stream, inv_rms, normed, grouped, keys_window, values_window, log_totals, mixed = saved
    rows = stream.shape[0]
    mid_grad_b = mid_grad.astype(bf16)
    out_term = rows_product(mid_grad_b, mixed)
    mixed_grad = product(mid_grad_b, wide[:, n_query + 2 * n_key :]).astype(bf16)
    query_grads, key_grads, value_grads = attend_back(
        grouped,
        keys_window,
        values_window,
        allowed,
        log_totals,
        mixed.reshape(grouped.shape),
        mixed_grad.reshape(grouped.shape),
    )
    both = jnp.concatenate(
        [key_grads.reshape(2 * rows, n_key), value_grads.reshape(2 * rows, n_key)], axis=1
    )
    back = from_behind(both[:rows].astype(bf16), "ctx", -1)
    own = both[rows:] + back.astype(f32)
    query_grad_b = rotate_back(query_grads.reshape(rows, -1, HEAD_DIM), cosine, sine)
    key_grad_b = rotate_back(own[:, :n_key].reshape(rows, -1, HEAD_DIM), cosine, sine)
    grads = jnp.concatenate(
        [
            query_grad_b.reshape(rows, n_query).astype(bf16),
            key_grad_b.reshape(rows, n_key).astype(bf16),
            own[:, n_key:].astype(bf16),
        ],
        axis=1,
    )
    normed_grad = sum_tensor(cols_product(grads, wide[:, : n_query + 2 * n_key]))
    wide_term = rows_product(normed, grads)
    term = jnp.concatenate([wide_term.astype(bf16), out_term.astype(bf16)], axis=1)
    part, gain_term = norm_backward(stream, inv_rms, gain, normed_grad)
    return mid_grad + part, gain_term, term


def on_device(
    inputs,
    out_grad,
    positions,
    attn_gain,
    w_query,
    w_key,
    w_value,
    w_out,
    ffn_gain,
    w_gate,
    w_up,
    w_down,
):
    core = lax.axis_index("pipe")
    first = core == 0
    shard = lax.axis_index("ctx")
    rows = inputs.shape[1]
    width = inputs.shape[2]
    n_query = w_query.shape[2]
    n_key = w_key.shape[2]
    half = w_gate.shape[2] // 2

    def pick(pair, index):
        return lax.dynamic_index_in_dim(pair, index, 0, keepdims=False)

    def mine_theirs(array, axis):
        size = array.shape[axis] // 2
        mine = lax.dynamic_slice_in_dim(array, core * size, size, axis)
        theirs = lax.dynamic_slice_in_dim(array, (1 - core) * size, size, axis)
        return mine, theirs

    gains = lax.all_gather(
        jnp.concatenate([attn_gain, ffn_gain], axis=0), ("pipe", "ctx"), axis=0, tiled=False
    )
    gains = gains.reshape(2, -1, 2, attn_gain.shape[1]).transpose(0, 2, 1, 3)
    gains = gains.reshape(2, 2, width).astype(f32)
    attn_shard = jnp.concatenate([w_query[0], w_key[0], w_value[0], w_out[0].T], axis=1)
    attn_wide = lax.all_gather(attn_shard, ("pipe", "ctx"), axis=0, tiled=True)
    attn_wide = attn_wide.reshape(2, width, -1)
    gate_mine, gate_theirs = mine_theirs(w_gate[0], 1)
    up_mine, up_theirs = mine_theirs(w_up[0], 1)
    down_mine, down_theirs = mine_theirs(w_down[0], 0)
    keep = jnp.concatenate([gate_mine, up_mine, down_mine.T], axis=1)
    give = jnp.concatenate([gate_theirs, up_theirs, down_theirs.T], axis=1)
    got = swap_cores(give)
    ffn_wide = [
        lax.all_gather(jnp.where(first, keep, got), "ctx", axis=0, tiled=True),
        lax.all_gather(jnp.where(first, got, keep), "ctx", axis=0, tiled=True),
    ]

    pos_row = pick(positions, core)
    cosine, sine = rope_tables(pos_row, HEAD_DIM)
    query_index = jnp.arange(rows, dtype=jnp.int32)
    key_index = jnp.arange(2 * rows, dtype=jnp.int32) - rows
    distance = query_index[:, None] - key_index[None, :]
    allowed = (distance >= 0) & (distance <= pos_row[:, None])
    place = (allowed, cosine, sine, (n_query, n_key))

    stream = pick(inputs, core)
    outs = []
    saved = []
    for section in range(2):
        middle, attn_saved = attention_forward(
            stream.astype(f32), gains[section, 0], attn_wide[section], place
        )
        state = ffn_forward_in(middle, gains[section, 1], ffn_wide[section], half)
        stream = ffn_forward_out(state, ffn_wide[section], half)
        outs.append(stream)
        saved.append((attn_saved, state))

    own_grad = pick(out_grad, core)
    both_grad = jnp.concatenate([own_grad, pick(out_grad, 1 - core)], axis=0)
    grads = [None, None]
    boundary = [None, None]
    for section in (1, 0):
        attn_saved, state = saved[section]
        mid_grad, ffn_gain_term, wide_term, down_term = ffn_backward(
            own_grad.astype(f32), both_grad, state, gains[section, 1], ffn_wide[section], half
        )
        down_share = lax.psum_scatter(down_term, "ctx", scatter_dimension=0, tiled=True)
        wide_share = lax.psum_scatter(wide_term, "ctx", scatter_dimension=0, tiled=True)
        stream_grad, attn_gain_term, attn_term = attention_backward(
            mid_grad, attn_saved, gains[section, 0], attn_wide[section], place
        )
        attn_mine, attn_theirs = mine_theirs(attn_term, 1)
        attn_sum = (attn_mine.astype(f32) + swap_cores(attn_theirs).astype(f32)).astype(bf16)
        attn_share = lax.psum_scatter(attn_sum, "ctx", scatter_dimension=0, tiled=True)
        own_grad = stream_grad.astype(bf16)
        boundary[section] = own_grad
        if section == 1:
            both_grad = jnp.concatenate([own_grad, swap_cores(own_grad)], axis=0)
        grads[section] = (wide_share, down_share, attn_share, attn_gain_term, ffn_gain_term)

    def to_owner(pair):
        keep_part = jnp.where(first, pair[0], pair[1])
        got_part = swap_cores(jnp.where(first, pair[1], pair[0]))
        return jnp.where(first, keep_part, got_part), jnp.where(first, got_part, keep_part)

    section_outputs = jnp.stack(to_owner(outs))
    boundary_grads = jnp.stack(to_owner(boundary))
    wide_a, wide_b = to_owner((grads[0][0], grads[1][0]))
    down_a, down_b = to_owner((grads[0][1], grads[1][1]))
    attn_full = jnp.concatenate(to_owner((grads[0][2], grads[1][2])), axis=1).astype(f32)
    gain_terms = jnp.stack([jnp.stack(grads[0][3:]), jnp.stack(grads[1][3:])])
    gain_sum = pick(lax.psum(gain_terms, ("pipe", "ctx")), core)
    own_width = attn_gain.shape[1]
    gain_own = lax.dynamic_slice_in_dim(gain_sum, shard * own_width, own_width, 1)
    key_at = n_query + n_key
    value_at = key_at + n_key
    return (
        section_outputs[None],
        boundary_grads[None],
        gain_own[0][None],
        attn_full[:, :n_query][None],
        attn_full[:, n_query:key_at][None],
        attn_full[:, key_at:value_at][None],
        attn_full[:, value_at:].T[None],
        gain_own[1][None],
        jnp.concatenate([wide_a[:, :half], wide_b[:, :half]], axis=1).astype(f32)[None],
        jnp.concatenate([wide_a[:, half:], wide_b[:, half:]], axis=1).astype(f32)[None],
        jnp.concatenate([down_a.T, down_b.T], axis=0).astype(f32)[None],
    )


def solution(mesh):
    in_specs = (
        P(None, "ctx", None),
        P(None, "ctx", None),
        P(None, "ctx"),
        P("pipe", "ctx"),
        P("pipe", "ctx", "tensor"),
        P("pipe", "ctx", "tensor"),
        P("pipe", "ctx", "tensor"),
        P("pipe", "tensor", "ctx"),
        P("pipe", "ctx"),
        P("pipe", "ctx", "tensor"),
        P("pipe", "ctx", "tensor"),
        P("pipe", "tensor", "ctx"),
    )
    out_specs = (
        P("pipe", None, "ctx", None),
        P("pipe", None, "ctx", None),
        P("pipe", "ctx"),
        P("pipe", "ctx", "tensor"),
        P("pipe", "ctx", "tensor"),
        P("pipe", "ctx", "tensor"),
        P("pipe", "tensor", "ctx"),
        P("pipe", "ctx"),
        P("pipe", "ctx", "tensor"),
        P("pipe", "ctx", "tensor"),
        P("pipe", "tensor", "ctx"),
    )
    return jax.shard_map(
        on_device, mesh=mesh, in_specs=in_specs, out_specs=out_specs, check_vma=False
    )
```

time: 2290 us -> 1140 us (0.50)
  waiting for transfers between devices: 1730 us -> 766 us
  matrix products: 327 us -> 126 us
  other arithmetic: 73.3 us -> 103 us
  local copies, waits for them, and re-layouts: 31.8 us -> 57 us
  starting transfers between devices: 38 us -> 14.6 us
    psum x9 -> x7, waiting for transfers between devices: 954 us -> 310 us  [sum_tensor(): return lax.psum(partial.astype(bf16), 'tensor').astype(f32)]
    reduce_scatter x7 -> x6, waiting for transfers between devices: 489 us -> 244 us  [the longest x2 161 us: on_device(): lax.psum_scatter(wide_term, 'ctx', scatter_dimension=0, tiled=True)]
    all_gather x5 -> x3, waiting for transfers between devices: 270 us -> 173 us  [the longest x1 71.6 us: on_device(): lax.all_gather(jnp.where(first, keep, got), 'ctx', axis=0, tiled=True)]
    dot_general x21 -> x8, matrix products: 128 us -> 39.7 us  [rows_product(): lax.dot_general(left, right, (((0,), (0,)), ((), ())), preferred_element_...]
    dot_general x21 -> x8, matrix products: 82.2 us -> 33 us  [cols_product(): lax.dot_general(left, right, (((1,), (1,)), ((), ())), preferred_element_...]
    dot_general x24 -> x10, matrix products: 84.8 us -> 43.8 us  [the longest x8 36.8 us: product(): lax.dot_general(left, right, (((1,), (0,)), ((), ())), preferred_element_...]
    psum x0 -> x1, blocking collectives: none -> 27.4 us  [on_device(): gain_sum = pick(lax.psum(gain_terms, ('pipe', 'ctx')), core)]
    ppermute x16 -> x4, starting transfers between devices: 35.6 us -> 9.98 us  [from_behind(): return lax.ppermute(block, axis, route)]
  transfers between devices with their start and end apart: 37 -> 35, of which waited for: 24 -> 25; matrix products, arithmetic and copies ran while one was open for 10% -> 13% of each run, Pallas kernels for 0% -> 0%
where the time goes in v1:
time: 1140 us; the launch traced here: 1130 us
  waiting for transfers between devices  766 us (67%)
  matrix products  126 us (11%)
  other arithmetic  103 us (9%)
  local copies, waits for them, and re-layouts  57 us (5%)
  blocking collectives  48.1 us (4%)
  between operations  17.9 us (2%)
  starting transfers between devices  14.6 us (1%)
    psum x7, waiting for transfers between devices, sum_tensor(): return lax.psum(partial.astype(bf16), 'tensor').astype(f32)  310 us
    reduce_scatter x2, waiting for transfers between devices, on_device(): lax.psum_scatter(wide_term, 'ctx', scatter_dimension=0, tiled=True)  161 us
    reduce_scatter x2, waiting for transfers between devices, on_device(): lax.psum_scatter(attn_sum, 'ctx', scatter_dimension=0, tiled=True)  82.5 us
    all_gather x1, waiting for transfers between devices, on_device(): lax.all_gather(jnp.where(first, keep, got), 'ctx', axis=0, tiled=True)  71.6 us
    all_gather x1, waiting for transfers between devices, on_device(): lax.all_gather(jnp.where(first, got, keep), 'ctx', axis=0, tiled=True)  66.2 us
    dot_general x8, matrix products, rows_product(): lax.dot_general(left, right, (((0,), (0,)), ((), ())), preferred_element_...  39.7 us
    dot_general x8, matrix products, product(): lax.dot_general(left, right, (((1,), (0,)), ((), ())), preferred_element_...  36.8 us
    all_gather x1, waiting for transfers between devices, on_device(): attn_wide = lax.all_gather(attn_shard, ('pipe', 'ctx'), axis=0, tiled=True)  34.9 us
  transfers between devices with their start and end apart: 35, of which 25 were waited for; matrix products, arithmetic and copies ran while one was open for 13% of the time, Pallas kernels for 0%

profile of v1, /device:TPU:0, one launch (start us, length us, event | category | flops | bytes accessed | tf_op | source)
XLA Modules:
  0.0 1132.0 jit_solution(13500671897299524115)
XLA Ops:
  23.9 20.8 %all-gather.1 = bf16[8,2,512]{2,1,0:T(2,128)(2,1)S(1)} all-gather(bf16[1,2,512]{2,1,0:T(2,128)(2,1)S(1)} %maximum_bitcast_fusion.4), channel_id=2, replica_groups=mesh['pipe'=2,'ctx'=4,'tensor'=4] {'pipe','ctx'}, dimensions={0}, use_global_device_ids=true | all-gather | bytes 18432 | tf_op jit(solution)/shard_map/all_gather | solution.py:272
  46.8 34.9 %all-gather.6.cloned.1.call-done = bf16[4096,1280]{0,1:T(8,128)(2,1)} async-done(((bf16[512,1280]{0,1:T(8,128)(2,1)}), bf16[4096,1280]{0,1:T(8,128)(2,1)}) %all-gather.6.cloned.1.call-update) | async-done | bytes 10485776 | tf_op jit(solution)/shard_map/all_gather | solution.py:278
  114.8 45.2 %all-reduce.9.cloned.1.call-done = bf16[256,2048]{1,0:T(8,128)(2,1)} async-done(((bf16[256,2048]{1,0:T(8,128)(2,1)}), bf16[256,2048]{1,0:T(8,128)(2,1)}) %all-reduce.9.cloned.1.call-update) | async-done | bytes 1048592 | tf_op jit(solution)/shard_map/psum | solution.py:136
  166.4 71.6 %all-gather.8.cloned.1.call-done = bf16[2048,3072]{1,0:T(8,128)(2,1)} async-done(((bf16[512,3072]{1,0:T(8,128)(2,1)}), bf16[2048,3072]{1,0:T(8,128)(2,1)}) %all-gather.8.cloned.1.call-update) | async-done | bytes 12582928 | tf_op jit(solution)/shard_map/all_gather | solution.py:287
  238.0 7.2 fusion.6
  256.4 51.9 %all-reduce.11.cloned.1.call-done = bf16[256,2048]{1,0:T(8,128)(2,1)} async-done(((bf16[256,2048]{1,0:T(8,128)(2,1)}), bf16[256,2048]{1,0:T(8,128)(2,1)}) %all-reduce.11.cloned.1.call-update) | async-done | bytes 1048592 | tf_op jit(solution)/shard_map/psum | solution.py:136
  335.1 51.3 %all-reduce.13.cloned.1.call-done = bf16[256,2048]{1,0:T(8,128)(2,1)} async-done(((bf16[256,2048]{1,0:T(8,128)(2,1)}), bf16[256,2048]{1,0:T(8,128)(2,1)}) %all-reduce.13.cloned.1.call-update) | async-done | bytes 1048592 | tf_op jit(solution)/shard_map/psum | solution.py:136
  393.0 66.2 %all-gather.10.cloned.1.call-done = bf16[2048,3072]{1,0:T(8,128)(2,1)} async-done(((bf16[512,3072]{1,0:T(8,128)(2,1)}), bf16[2048,3072]{1,0:T(8,128)(2,1)}) %all-gather.10.cloned.1.call-update) | async-done | bytes 12582928 | tf_op jit(solution)/shard_map/all_gather | solution.py:288
  459.2 7.7 fusion.2
  481.4 50.6 %all-reduce.15.cloned.1.call-done = bf16[256,2048]{1,0:T(8,128)(2,1)} async-done(((bf16[256,2048]{1,0:T(8,128)(2,1)}), bf16[256,2048]{1,0:T(8,128)(2,1)}) %all-reduce.15.cloned.1.call-update) | async-done | bytes 1048592 | tf_op jit(solution)/shard_map/psum | solution.py:136
  559.7 51.1 %all-reduce.17.cloned.1.call-done = bf16[256,2048]{1,0:T(8,128)(2,1)} async-done(((bf16[256,2048]{1,0:T(8,128)(2,1)}), bf16[256,2048]{1,0:T(8,128)(2,1)}) %all-reduce.17.cloned.1.call-update) | async-done | bytes 1048592 | tf_op jit(solution)/shard_map/psum | solution.py:136
  617.6 6.3 multiply_convert_fusion.1
  643.6 46.7 %all-reduce.19.cloned.1.call-done = bf16[256,2048]{1,0:T(8,128)(2,1)} async-done(((bf16[256,2048]{1,0:T(8,128)(2,1)}), bf16[256,2048]{1,0:T(8,128)(2,1)}) %all-reduce.19.cloned.1.call-update) | async-done | bytes 1048592 | tf_op jit(solution)/shard_map/psum | solution.py:136
  718.8 5.9 convolution_convert_fusion.2
  726.0 6.0 convolution_convert_fusion.3
  732.4 10.1 convolution_convert_fusion
  742.6 10.2 convolution_convert_fusion.1
  767.4 6.7 add_convert_fusion
  791.3 12.8 %all-reduce.21.cloned.1.call-done = (bf16[256,2048]{1,0:T(8,128)(2,1)}, bf16[256,2048]{1,0:T(8,128)(2,1)}) async-done(((bf16[256,2048]{1,0:T(8,128)(2,1)}, bf16[256,2048]{1,0:T(8,128)(2,1)}), (bf16[256,2048]{1,0:T(8,128)(2,1)}, bf16[256,2048]{1,0:T(8,128)(2,1)})) %all-reduce.21.cloned.1.call-update) | async-done | bytes 2097168 | tf_op jit(solution)/shard_map/psum | solution.py:136
  812.4 27.4 %psum.71 = f32[2,2,2048]{2,1,0:T(2,128)S(1)} all-reduce(f32[2,2,2048]{2,1,0:T(2,128)S(1)} %pad_maximum_fusion.37), channel_id=1, replica_groups=mesh['pipe'=2,'ctx'=4,'tensor'=4] {'pipe','ctx'}, use_global_device_ids=true, to_apply=%region_26.27 | all-reduce | flops 8192 | bytes 65536 | tf_op jit(solution)/shard_map/psum | solution.py:345
  851.0 72.1 %reduce-scatter.13.cloned.1.call-done = bf16[512,2048]{1,0:T(8,128)(2,1)} async-done(((bf16[2048,2048]{1,0:T(8,128)(2,1)}), bf16[512,2048]{1,0:T(8,128)(2,1)}) %reduce-scatter.13.cloned.1.call-update) | async-done | bytes 2097168 | tf_op jit(solution)/shard_map/reduce_scatter | solution.py:321
  923.1 89.4 %reduce-scatter.11.cloned.1.call-done = bf16[512,2048]{1,0:T(8,128)(2,1)} async-done(((bf16[2048,2048]{1,0:T(8,128)(2,1)}), bf16[512,2048]{1,0:T(8,128)(2,1)}) %reduce-scatter.11.cloned.1.call-update) | async-done | bytes 2097168 | tf_op jit(solution)/shard_map/reduce_scatter | solution.py:321
  1015.7 39.3 %reduce-scatter.9.cloned.1.call-done = bf16[512,640]{0,1:T(8,128)(2,1)} async-done(((bf16[2048,640]{0,1:T(8,128)(2,1)}), bf16[512,640]{0,1:T(8,128)(2,1)}) %reduce-scatter.9.cloned.1.call-update) | async-done | bytes 655376 | tf_op jit(solution)/shard_map/reduce_scatter | solution.py:327
  1055.0 43.2 %reduce-scatter.7.cloned.1.call-done = bf16[512,640]{0,1:T(8,128)(2,1)} async-done(((bf16[2048,640]{0,1:T(8,128)(2,1)}), bf16[512,640]{0,1:T(8,128)(2,1)}) %reduce-scatter.7.cloned.1.call-update) | async-done | bytes 655376 | tf_op jit(solution)/shard_map/reduce_scatter | solution.py:327
  (495 shorter events, 279.7 us)
Async XLA Ops:
  8.0 73.6 %all-gather.6.cloned.1.call-start = ((), (), s32[]{:S(2)}) async-start(), calls=%async_computation.6 | async-start | bytes 11796480 | tf_op jit(solution)/shard_map/all_gather | solution.py:278
  13.6 146.4 %all-reduce.9.cloned.1.call-start = ((), (), s32[]{:S(2)}) async-start(), calls=%async_computation.7 | async-start | bytes 2097152 | tf_op jit(solution)/shard_map/psum | solution.py:136
  23.4 85.9 %collective-permute-start.2 = (bf16[512,3072]{1,0:T(8,128)(2,1)}, bf16[512,3072]{1,0:T(8,128)(2,1)}, u32[]{:S(2)}, u32[]{:S(2)}) collective-permute-start(bf16[512,3072]{1,0:T(8,128)(2,1)} %pad_maximum_fusion.1), channel_id=1, source_target_pairs={{0,16},{16,0},{1,17},{17,1},{2,18},{18,2},{3,19},{19,3},{4,20},{20... | collective-permute-start | bytes 9437192 | tf_op jit(solution)/shard_map/ppermute | solution.py:20
  107.0 131.0 %all-gather.8.cloned.1.call-start = ((), (), s32[]{:S(2)}) async-start(), calls=%async_computation.8 | async-start | bytes 15728640 | tf_op jit(solution)/shard_map/all_gather | solution.py:287
  114.5 193.8 %all-reduce.11.cloned.1.call-start = ((), (), s32[]{:S(2)}) async-start(), calls=%async_computation.9 | async-start | bytes 2097152 | tf_op jit(solution)/shard_map/psum | solution.py:136
  256.3 130.0 %all-reduce.13.cloned.1.call-start = ((), (), s32[]{:S(2)}) async-start(), calls=%async_computation.10 | async-start | bytes 2097152 | tf_op jit(solution)/shard_map/psum | solution.py:136
  334.0 125.2 %all-gather.10.cloned.1.call-start = ((), (), s32[]{:S(2)}) async-start(), calls=%async_computation.11 | async-start | bytes 15728640 | tf_op jit(solution)/shard_map/all_gather | solution.py:288
  334.6 197.4 %all-reduce.15.cloned.1.call-start = ((), (), s32[]{:S(2)}) async-start(), calls=%async_computation.12 | async-start | bytes 2097152 | tf_op jit(solution)/shard_map/psum | solution.py:136
  389.6 69.6 %collective-permute-start.5 = (bf16[256,2048]{1,0:T(8,128)(2,1)}, bf16[256,2048]{1,0:T(8,128)(2,1)}, u32[]{:S(2)}, u32[]{:S(2)}) collective-permute-start(bf16[256,2048]{1,0:T(8,128)(2,1)} %multiply_convert_fusion.5), channel_id=1, source_target_pairs={{0,16},{16,0},{1,17},{17,1},{2,18},{18,2},{3,19},{19,3},{4,20},{20... | collective-permute-start | bytes 3145736 | tf_op jit(solution)/shard_map/ppermute | solution.py:20
  480.1 130.7 %all-reduce.17.cloned.1.call-start = ((), (), s32[]{:S(2)}) async-start(), calls=%async_computation.13 | async-start | bytes 2097152 | tf_op jit(solution)/shard_map/psum | solution.py:136
  559.5 130.9 %all-reduce.19.cloned.1.call-start = ((), (), s32[]{:S(2)}) async-start(), calls=%async_computation.14 | async-start | bytes 2097152 | tf_op jit(solution)/shard_map/psum | solution.py:136
  628.7 8.9 collective-permute-start.11
  638.9 165.2 %all-reduce.21.cloned.1.call-start = ((), (), s32[]{:S(2)}) async-start(), calls=%async_computation.21 | async-start | bytes 4194304 | tf_op jit(solution)/shard_map/psum | solution.py:136
  717.6 129.1 %reduce-scatter.17.cloned.1.call-start = ((), (), s32[]{:S(2)}) async-start(), calls=%async_computation.20 | async-start | bytes 5242880 | tf_op jit(solution)/shard_map/reduce_scatter | solution.py:320
  724.8 122.0 %reduce-scatter.15.cloned.1.call-start = ((), (), s32[]{:S(2)}) async-start(), calls=%async_computation.19 | async-start | bytes 5242880 | tf_op jit(solution)/shard_map/reduce_scatter | solution.py:320
  732.0 191.1 %reduce-scatter.13.cloned.1.call-start = ((), (), s32[]{:S(2)}) async-start(), calls=%async_computation.18 | async-start | bytes 10485760 | tf_op jit(solution)/shard_map/reduce_scatter | solution.py:321
  742.6 269.9 %reduce-scatter.11.cloned.1.call-start = ((), (), s32[]{:S(2)}) async-start(), calls=%async_computation.17 | async-start | bytes 10485760 | tf_op jit(solution)/shard_map/reduce_scatter | solution.py:321
  752.9 302.1 %reduce-scatter.9.cloned.1.call-start = ((), (), s32[]{:S(2)}) async-start(), calls=%async_computation.16 | async-start | bytes 3276800 | tf_op jit(solution)/shard_map/reduce_scatter | solution.py:327
  774.1 324.1 %reduce-scatter.7.cloned.1.call-start = ((), (), s32[]{:S(2)}) async-start(), calls=%async_computation.15 | async-start | bytes 3276800 | tf_op jit(solution)/shard_map/reduce_scatter | solution.py:327
  810.3 30.1 %collective-permute-start.13 = (bf16[256,2048]{1,0:T(8,128)(2,1)}, bf16[256,2048]{1,0:T(8,128)(2,1)}, u32[]{:S(2)}, u32[]{:S(2)}) collective-permute-start(bf16[256,2048]{1,0:T(8,128)(2,1)} %get-tuple-element.54), channel_id=1, source_target_pairs={{0,16},{16,0},{1,17},{17,1},{2,18},{18,2},{3,19},{19,3},{4,20},{20... | collective-permute-start | bytes 3145736 | tf_op jit(solution)/shard_map/ppermute | solution.py:20
  811.8 31.8 %collective-permute-start.7 = (bf16[256,2048]{1,0:T(8,128)(2,1)}, bf16[256,2048]{1,0:T(8,128)(2,1)}, u32[]{:S(2)}, u32[]{:S(2)}) collective-permute-start(bf16[256,2048]{1,0:T(8,128)(2,1)} %broadcast_select_fusion.10), channel_id=1, source_target_pairs={{0,16},{16,0},{1,17},{17,1},{2,18},{18,2},{3,19},{19,3},{4,20},{20... | collective-permute-start | bytes 3145736 | tf_op jit(solution)/shard_map/ppermute | solution.py:20
  849.2 251.0 %collective-permute-start.18 = (bf16[512,1024]{1,0:T(8,128)(2,1)}, bf16[512,1024]{1,0:T(8,128)(2,1)}, u32[]{:S(2)}, u32[]{:S(2)}) collective-permute-start(bf16[512,1024]{1,0:T(8,128)(2,1)} %broadcast_select_fusion.6), channel_id=1, source_target_pairs={{0,16},{16,0},{1,17},{17,1},{2,18},{18,2},{3,19},{19,3},{4,20},{20... | collective-permute-start | bytes 3145736 | tf_op jit(solution)/shard_map/ppermute | solution.py:20
  1015.7 99.7 %collective-permute-start.17 = (bf16[512,2048]{1,0:T(8,128)(2,1)}, bf16[512,2048]{1,0:T(8,128)(2,1)}, u32[]{:S(2)}, u32[]{:S(2)}) collective-permute-start(bf16[512,2048]{1,0:T(8,128)(2,1)} %broadcast_select_fusion.4), channel_id=1, source_target_pairs={{0,16},{16,0},{1,17},{17,1},{2,18},{18,2},{3,19},{19,3},{4,20},{20... | collective-permute-start | bytes 6291464 | tf_op jit(solution)/shard_map/ppermute | solution.py:20
  1100.2 9.4 collective-permute-start.16
  (133 other events, 1373.8 us)
Sparse Core Ops, SparseCore 0:
  13.7 67.9 all-gather.5
  107.1 52.8 all-reduce.8
  256.5 51.7 all-reduce.10
  334.1 52.1 all-reduce.12
  480.2 51.7 all-reduce.14
  559.6 51.1 all-reduce.16
  639.1 51.2 all-reduce.18
  717.7 86.3 all-reduce.20
Sparse Core Ops, SparseCore 1:
  114.6 123.3 all-gather.7
  336.5 122.7 all-gather.9
  724.9 51.9 reduce-scatter.16
  780.3 53.0 reduce-scatter.14
  836.8 86.2 reduce-scatter.12
  926.2 86.2 reduce-scatter.10
  1015.6 39.4 reduce-scatter.8
  1058.7 39.4 reduce-scatter.6

commit v2 on v1

--- a/solution.py
+++ b/solution.py
@@ -3,6 +3,8 @@
 import jax
 import jax.numpy as jnp
 from jax import lax
+from jax.experimental import pallas as pl
+from jax.experimental.pallas import tpu as pltpu
 from jax.sharding import PartitionSpec as P
 
 HEADS = 32
@@ -24,6 +26,200 @@
     devices = range(lax.axis_size(axis))
     route = [(i - distance, i) for i in devices if i - distance in devices]
     return lax.ppermute(block, axis, route)
+
+
+def ring_order(count):
+    across = 1 << (count.bit_length() - 1) // 2
+    down = count // across
+    walk = [(0, x) for x in range(across)]
+    for y in range(1, down):
+        columns = range(1, across)
+        walk += [(y, x) for x in (columns if y % 2 == 0 else reversed(columns))]
+    walk += [(y, 0) for y in range(down - 1, 0, -1)]
+    return [y * across + x for y, x in walk]
+
+
+def ring_tools():
+    count = lax.axis_size("ctx")
+    order = ring_order(count)
+    place = [order.index(device) for device in range(count)]
+    ahead = [(order[i], order[(i + 1) % count]) for i in range(count)]
+    behind = [(b, a) for a, b in ahead]
+    at = jnp.asarray(place, jnp.int32)[lax.axis_index("ctx")]
+    table = jnp.asarray(order * 2, jnp.int32)
+
+    def device_at(distance):
+        return table[at + distance % count]
+
+    return count, ahead, behind, device_at
+
+
+def ring_gather(block):
+    count, ahead, behind, device_at = ring_tools()
+    half = block.shape[1] // 2
+    out = jnp.zeros((count,) + block.shape, block.dtype)
+
+    def put(out, piece, distance, column=0):
+        return lax.dynamic_update_slice(out, piece[None], (device_at(distance), 0, column))
+
+    out = put(out, block, 0)
+    from_back, from_front = block, block
+    for distance in range(1, count // 2):
+        from_back = lax.ppermute(from_back, "ctx", ahead)
+        from_front = lax.ppermute(from_front, "ctx", behind)
+        out = put(out, from_back, -distance)
+        out = put(out, from_front, distance)
+    left = lax.ppermute(from_back[:, :half], "ctx", ahead)
+    right = lax.ppermute(from_front[:, half:], "ctx", behind)
+    out = put(out, left, count // 2)
+    return put(out, right, count // 2, half)
+
+
+def ring_scatter(terms):
+    count, ahead, behind, device_at = ring_tools()
+    half = terms.shape[2] // 2
+
+    def term(distance):
+        return lax.dynamic_index_in_dim(terms, device_at(distance), 0, keepdims=False)
+
+    far = term(count // 2)
+    to_front = lax.ppermute(far[:, :half], "ctx", ahead)
+    to_back = lax.ppermute(far[:, half:], "ctx", behind)
+    for distance in range(count // 2 - 1, 0, -1):
+        front, back = term(distance), term(-distance)
+        if distance == count // 2 - 1:
+            front = jnp.concatenate([add_bf16(front[:, :half], to_front), front[:, half:]], axis=1)
+            back = jnp.concatenate([back[:, :half], add_bf16(back[:, half:], to_back)], axis=1)
+        else:
+            front, back = add_bf16(front, to_front), add_bf16(back, to_back)
+        to_front = lax.ppermute(front, "ctx", ahead)
+        to_back = lax.ppermute(back, "ctx", behind)
+    return term(0).astype(f32) + to_front.astype(f32) + to_back.astype(f32)
+
+
+def add_bf16(a, b):
+    return (a.astype(f32) + b.astype(f32)).astype(bf16)
+
+
+def token_terms_kernel(left_ref, right_ref, out_ref):
+    out_ref[...] = lax.dot_general(
+        left_ref[...], right_ref[...], (((0,), (0,)), ((), ())), preferred_element_type=f32
+    ).astype(bf16)
+
+
+def token_terms(left, right):
+    tokens, width = left.shape
+    units = right.shape[1]
+    tile, column = min(width, 1024), min(units, 1024)
+    return pl.pallas_call(
+        token_terms_kernel,
+        grid=(units // column, width // tile),
+        in_specs=[
+            pl.BlockSpec((tokens, tile), lambda j, i: (0, i)),
+            pl.BlockSpec((tokens, column), lambda j, i: (0, j)),
+        ],
+        out_specs=pl.BlockSpec((tile, column), lambda j, i: (i, j)),
+        out_shape=jax.ShapeDtypeStruct((width, units), bf16),
+        compiler_params=pltpu.CompilerParams(vmem_limit_bytes=40 * 2**20),
+        cost_estimate=pl.CostEstimate(
+            flops=2 * tokens * width * units,
+            bytes_accessed=2 * (width * units + tokens * width + tokens * units),
+            transcendentals=0,
+        ),
+        name="token_terms",
+    )(left, right)
+
+
+def wide_outputs_kernel(core_ref, low_ref, high_ref, got_ref, gate_ref, up_ref):
+    first = core_ref[0] == 0
+    units = got_ref.shape[1] // 2
+    keep = jnp.where(first, low_ref[...], high_ref[...])
+    got = got_ref[...]
+    for side in range(2):
+        part = jnp.where(first == (side == 0), keep, got).astype(f32)
+        gate_ref[:, side * units : (side + 1) * units] = part[:, :units]
+        up_ref[:, side * units : (side + 1) * units] = part[:, units:]
+
+
+def down_outputs_kernel(core_ref, low_ref, high_ref, got_ref, down_ref):
+    first = core_ref[0] == 0
+    units = got_ref.shape[1]
+    keep = jnp.where(first, low_ref[...], high_ref[...])
+    got = got_ref[...]
+    for side in range(2):
+        part = jnp.where(first == (side == 0), keep, got).astype(f32)
+        down_ref[side * units : (side + 1) * units, :] = part.T
+
+
+def section_outputs_call(kernel, core, low, high, got, specs, shapes, name):
+    rows, wide = got.shape
+    tile = 128
+    block = pl.BlockSpec((tile, wide), lambda i, core: (i, 0))
+    return pl.pallas_call(
+        kernel,
+        grid_spec=pltpu.PrefetchScalarGridSpec(
+            num_scalar_prefetch=1,
+            grid=(rows // tile,),
+            in_specs=[block, block, block],
+            out_specs=specs(tile),
+        ),
+        out_shape=shapes,
+        compiler_params=pltpu.CompilerParams(vmem_limit_bytes=40 * 2**20),
+        cost_estimate=pl.CostEstimate(
+            flops=0, bytes_accessed=3 * rows * wide * 2 + 2 * rows * wide * 4, transcendentals=0
+        ),
+        name=name,
+    )(core.reshape(1), low, high, got)
+
+
+def wide_outputs(core, low, high, got):
+    rows, units = got.shape[0], got.shape[1] // 2
+    return section_outputs_call(
+        wide_outputs_kernel,
+        core,
+        low,
+        high,
+        got,
+        lambda tile: [pl.BlockSpec((tile, 2 * units), lambda i, core: (i, 0))] * 2,
+        [jax.ShapeDtypeStruct((rows, 2 * units), f32)] * 2,
+        "wide_outputs",
+    )
+
+
+def down_outputs(core, low, high, got):
+    rows, units = got.shape
+    return section_outputs_call(
+        down_outputs_kernel,
+        core,
+        low,
+        high,
+        got,
+        lambda tile: pl.BlockSpec((2 * units, tile), lambda i, core: (0, i)),
+        jax.ShapeDtypeStruct((2 * units, rows), f32),
+        "down_outputs",
+    )
+
+
+def pin(value, *others):
+    return lax.optimization_barrier((value, *others))
+
+
+def share_gains(terms):
+    core, shard = lax.axis_index("pipe"), lax.axis_index("ctx")
+    count = lax.axis_size("ctx")
+    own = lax.dynamic_index_in_dim(terms, core, 0, keepdims=False)
+    other = lax.dynamic_index_in_dim(terms, 1 - core, 0, keepdims=False)
+    total = own + swap_cores(other)
+    blocks = total.reshape(2, count, -1)
+
+    def block(index):
+        return lax.dynamic_index_in_dim(blocks, index, 1, keepdims=False)
+
+    result = block(shard)
+    for step in range(1, count):
+        route = [(i, i ^ step) for i in range(count)]
+        result = result + lax.ppermute(block(shard ^ step), "ctx", route)
+    return result
 
 
 def product(left, right):
@@ -132,8 +328,11 @@
     return (query_grad, key_part, value_part)
 
 
-def sum_tensor(partial):
-    return lax.psum(partial.astype(bf16), "tensor").astype(f32)
+def sum_tensor(partial, *others):
+    partial = partial.astype(bf16)
+    if others:
+        partial, *others = pin(partial, *others)
+    return lax.psum(partial, "tensor").astype(f32), *others
 
 
 def own_share(partial, rows):
@@ -141,7 +340,7 @@
     return partial[:rows] + arrived.astype(f32)
 
 
-def attention_forward(stream, gain, wide, place):
+def attention_forward(stream, gain, wide, place, *others):
     allowed, cosine, sine, sizes = place
     n_query, n_key = sizes
     rows = stream.shape[0]
@@ -162,49 +361,52 @@
     mixed_rows, log_totals = attend(grouped, keys_window, values_window, allowed)
     mixed = mixed_rows.astype(bf16).reshape(rows, n_query)
     partial = cols_product(mixed, wide[:, n_query + 2 * n_key :])
-    middle = stream + sum_tensor(partial)
+    total, *others = sum_tensor(partial, *others)
     saved = (stream, inv_rms, normed, grouped, keys_window, values_window, log_totals, mixed)
-    return middle, saved
+    return stream + total, saved, *others
 
 
 def ffn_forward_in(middle, gain, wide, hidden_width):
     normed, inv_rms = norm_forward(middle, gain)
     both = jnp.concatenate([normed, swap_cores(normed)], axis=0)
-    gate_up = product(both, wide[:, : 2 * hidden_width])
+    gate_up = product(both, wide)
     gate = gate_up[:, :hidden_width]
     up = gate_up[:, hidden_width:]
     hidden = (jax.nn.silu(gate) * up).astype(bf16)
     return (middle, inv_rms, both, gate, up, hidden)
 
 
-def ffn_forward_out(state, wide, hidden_width):
+def ffn_forward_out(state, down, *others):
     middle, hidden = state[0], state[-1]
-    partial = cols_product(hidden, wide[:, 2 * hidden_width :])
-    return (middle + sum_tensor(own_share(partial, middle.shape[0]))).astype(bf16)
-
-
-def ffn_backward(upstream, upstream_both, state, gain, wide, hidden_width):
+    partial = own_share(cols_product(hidden, down), middle.shape[0])
+    total, *others = sum_tensor(partial, *others)
+    return (middle + total).astype(bf16), *others
+
+
+def ffn_backward(upstream, upstream_both, state, gain, wide, down, *others):
     middle, inv_rms, both, gate, up, hidden = state
-    hidden_grad = product(upstream_both, wide[:, 2 * hidden_width :])
+    hidden_grad = product(upstream_both, down)
     sigmoid_gate = jax.nn.sigmoid(gate)
     gate_grad = (hidden_grad * up * sigmoid_gate * (1.0 + gate * (1.0 - sigmoid_gate))).astype(bf16)
     up_grad = (hidden_grad * gate * sigmoid_gate).astype(bf16)
     grads = jnp.concatenate([gate_grad, up_grad], axis=1)
-    partial = cols_product(grads, wide[:, : 2 * hidden_width])
-    normed_grad = sum_tensor(own_share(partial, middle.shape[0]))
-    down_term = rows_product(upstream_both, hidden).astype(bf16)
-    wide_term = rows_product(both, grads).astype(bf16)
+    partial = own_share(cols_product(grads, wide), middle.shape[0])
+    normed_grad, *others = sum_tensor(partial, *others)
+    down_share = lax.psum_scatter(
+        token_terms(upstream_both, hidden), "ctx", scatter_dimension=0, tiled=True
+    )
+    normed_grad, terms = pin(normed_grad, token_terms(both, grads))
+    wide_share = lax.psum_scatter(terms, "ctx", scatter_dimension=0, tiled=True)
     mid_part, gain_term = norm_backward(middle, inv_rms, gain, normed_grad)
-    return upstream + mid_part, gain_term, wide_term, down_term
-
-
-def attention_backward(mid_grad, saved, gain, wide, place):
+    return upstream + mid_part, gain_term, wide_share, down_share, *others
+
+
+def attention_backward(mid_grad, saved, gain, wide, place, *others):
     allowed, cosine, sine, sizes = place
     n_query, n_key = sizes
     stream, inv_rms, normed, grouped, keys_window, values_window, log_totals, mixed = saved
     rows = stream.shape[0]
     mid_grad_b = mid_grad.astype(bf16)
-    out_term = rows_product(mid_grad_b, mixed)
     mixed_grad = product(mid_grad_b, wide[:, n_query + 2 * n_key :]).astype(bf16)
     query_grads, key_grads, value_grads = attend_back(
         grouped,
@@ -230,11 +432,20 @@
         ],
         axis=1,
     )
-    normed_grad = sum_tensor(cols_product(grads, wide[:, : n_query + 2 * n_key]))
-    wide_term = rows_product(normed, grads)
-    term = jnp.concatenate([wide_term.astype(bf16), out_term.astype(bf16)], axis=1)
+    partial = cols_product(grads, wide[:, : n_query + 2 * n_key])
+    normed_grad, *others = sum_tensor(partial, *others)
+    terms = jnp.concatenate(
+        [rows_product(normed, grads).astype(bf16), rows_product(mid_grad_b, mixed).astype(bf16)],
+        axis=1,
+    )
+    count = lax.axis_size("ctx")
+    terms = terms.reshape(count, 2, -1, terms.shape[1])
+    core = lax.axis_index("pipe")
+    mine = lax.dynamic_index_in_dim(terms, core, 1, keepdims=False)
+    theirs = lax.dynamic_index_in_dim(terms, 1 - core, 1, keepdims=False)
+    normed_grad, summed = pin(normed_grad, add_bf16(mine, swap_cores(theirs)))
     part, gain_term = norm_backward(stream, inv_rms, gain, normed_grad)
-    return mid_grad + part, gain_term, term
+    return mid_grad + part, gain_term, ring_scatter(summed).astype(bf16), *others
 
 
 def on_device(
@@ -269,24 +480,47 @@
         theirs = lax.dynamic_slice_in_dim(array, (1 - core) * size, size, axis)
         return mine, theirs
 
-    gains = lax.all_gather(
-        jnp.concatenate([attn_gain, ffn_gain], axis=0), ("pipe", "ctx"), axis=0, tiled=False
-    )
-    gains = gains.reshape(2, -1, 2, attn_gain.shape[1]).transpose(0, 2, 1, 3)
-    gains = gains.reshape(2, 2, width).astype(f32)
+    count = lax.axis_size("ctx")
+    gain_row = jnp.concatenate([attn_gain, ffn_gain], axis=1)
     attn_shard = jnp.concatenate([w_query[0], w_key[0], w_value[0], w_out[0].T], axis=1)
-    attn_wide = lax.all_gather(attn_shard, ("pipe", "ctx"), axis=0, tiled=True)
-    attn_wide = attn_wide.reshape(2, width, -1)
+    wide_columns = attn_shard.shape[1]
+    gain_rows = jnp.pad(gain_row, ((0, 15), (0, wide_columns - gain_row.shape[1])))
+    rows_mine, rows_theirs = mine_theirs(attn_shard, 0)
+    attn_keep = jnp.concatenate([rows_mine, gain_rows], axis=0)
+    attn_got = swap_cores(jnp.concatenate([rows_theirs, gain_rows], axis=0))
+
+    def attn_weights(pieces):
+        got = swap_cores(pieces)
+        both = jnp.stack([jnp.where(first, pieces, got), jnp.where(first, got, pieces)], axis=1)
+        part_rows = attn_shard.shape[0] // 2
+        wide = both[:, :, :part_rows].reshape(width, wide_columns)
+        row = pieces[:, part_rows, : gain_row.shape[1]].astype(f32)
+        return wide, row.reshape(count, 2, -1).transpose(1, 0, 2).reshape(2, width)
+
     gate_mine, gate_theirs = mine_theirs(w_gate[0], 1)
     up_mine, up_theirs = mine_theirs(w_up[0], 1)
+    wide_keep = jnp.concatenate([gate_mine, up_mine], axis=1)
+    wide_got = swap_cores(jnp.concatenate([gate_theirs, up_theirs], axis=1))
     down_mine, down_theirs = mine_theirs(w_down[0], 0)
-    keep = jnp.concatenate([gate_mine, up_mine, down_mine.T], axis=1)
-    give = jnp.concatenate([gate_theirs, up_theirs, down_theirs.T], axis=1)
-    got = swap_cores(give)
-    ffn_wide = [
-        lax.all_gather(jnp.where(first, keep, got), "ctx", axis=0, tiled=True),
-        lax.all_gather(jnp.where(first, got, keep), "ctx", axis=0, tiled=True),
-    ]
+    down_keep, down_got = down_mine.T, swap_cores(down_theirs.T)
+
+    def for_sections(keep, got):
+        return [jnp.where(first, keep, got), jnp.where(first, got, keep)]
+
+    def gather(shard_part):
+        return lax.all_gather(shard_part, "ctx", axis=0, tiled=True)
+
+    attn_parts = for_sections(attn_keep, attn_got)
+    wide_parts = for_sections(wide_keep, wide_got)
+    down_parts = for_sections(down_keep, down_got)
+    wide_low = gather(wide_parts[0])
+    attn_pieces, attn_parts[1], wide_parts[1], *down_parts = pin(
+        ring_gather(attn_parts[0]), attn_parts[1], wide_parts[1], *down_parts
+    )
+    attn_low, gains_low = attn_weights(attn_pieces)
+    down_low = gather(down_parts[0])
+    wide_high = gather(wide_parts[1])
+    down_high = gather(down_parts[1])
 
     pos_row = pick(positions, core)
     cosine, sine = rope_tables(pos_row, HEAD_DIM)
@@ -297,68 +531,78 @@
     place = (allowed, cosine, sine, (n_query, n_key))
 
     stream = pick(inputs, core)
-    outs = []
-    saved = []
-    for section in range(2):
-        middle, attn_saved = attention_forward(
-            stream.astype(f32), gains[section, 0], attn_wide[section], place
-        )
-        state = ffn_forward_in(middle, gains[section, 1], ffn_wide[section], half)
-        stream = ffn_forward_out(state, ffn_wide[section], half)
-        outs.append(stream)
-        saved.append((attn_saved, state))
+    middle, attn_saved_low, wide_low, attn_part_high = attention_forward(
+        stream.astype(f32), gains_low[0], attn_low, place, wide_low, attn_parts[1]
+    )
+    state_low = ffn_forward_in(middle, gains_low[1], wide_low, half)
+    out_low, attn_pieces = ffn_forward_out(state_low, down_low, ring_gather(attn_part_high))
+    attn_high, gains_high = attn_weights(attn_pieces)
+    middle, attn_saved_high, wide_high = attention_forward(
+        out_low.astype(f32), gains_high[0], attn_high, place, wide_high
+    )
+    state_high = ffn_forward_in(middle, gains_high[1], wide_high, half)
 
     own_grad = pick(out_grad, core)
     both_grad = jnp.concatenate([own_grad, pick(out_grad, 1 - core)], axis=0)
-    grads = [None, None]
-    boundary = [None, None]
-    for section in (1, 0):
-        attn_saved, state = saved[section]
-        mid_grad, ffn_gain_term, wide_term, down_term = ffn_backward(
-            own_grad.astype(f32), both_grad, state, gains[section, 1], ffn_wide[section], half
+    mid_grad, ffn_gain_high, wide_share_high, down_share_high = ffn_backward(
+        own_grad.astype(f32), both_grad, state_high, gains_high[1], wide_high, down_high
+    )
+    stream_grad, attn_gain_high, attn_share_high, down_share_high = attention_backward(
+        mid_grad, attn_saved_high, gains_high[0], attn_high, place, down_share_high
+    )
+    boundary_high = stream_grad.astype(bf16)
+    both_grad = jnp.concatenate([boundary_high, swap_cores(boundary_high)], axis=0)
+    mid_grad, ffn_gain_low, wide_share_low, down_share_low, wide_share_high = ffn_backward(
+        boundary_high.astype(f32),
+        both_grad,
+        state_low,
+        gains_low[1],
+        wide_low,
+        down_low,
+        wide_share_high,
+    )
+    stream_grad, attn_gain_low, attn_share_low, down_share_low, attn_share_high = (
+        attention_backward(
+            mid_grad, attn_saved_low, gains_low[0], attn_low, place, down_share_low, attn_share_high
         )
-        down_share = lax.psum_scatter(down_term, "ctx", scatter_dimension=0, tiled=True)
-        wide_share = lax.psum_scatter(wide_term, "ctx", scatter_dimension=0, tiled=True)
-        stream_grad, attn_gain_term, attn_term = attention_backward(
-            mid_grad, attn_saved, gains[section, 0], attn_wide[section], place
+    )
+    boundary_low = stream_grad.astype(bf16)
+    (out_high,) = ffn_forward_out(state_high, down_high)
+
+    def from_other(low, high):
+        return swap_cores(jnp.where(first, high, low))
+
+    def to_owner(low, high):
+        keep_part = jnp.where(first, low, high)
+        got_part = from_other(low, high)
+        return jnp.where(first, keep_part, got_part), jnp.where(first, got_part, keep_part)
+
+    section_outputs = jnp.stack(to_owner(out_low, out_high))
+    boundary_grads = jnp.stack(to_owner(boundary_low, boundary_high))
+    down_pair = (down_share_low, down_share_high)
+    down_out = down_outputs(core, *down_pair, from_other(*down_pair))
+    wide_pair = (wide_share_low, wide_share_high)
+    gate_out, up_out = wide_outputs(core, *wide_pair, from_other(*wide_pair))
+    attn_full = jnp.concatenate(to_owner(attn_share_low, attn_share_high), axis=0).astype(f32)
+    gains_out = share_gains(
+        jnp.stack(
+            [jnp.stack([attn_gain_low, ffn_gain_low]), jnp.stack([attn_gain_high, ffn_gain_high])]
         )
-        attn_mine, attn_theirs = mine_theirs(attn_term, 1)
-        attn_sum = (attn_mine.astype(f32) + swap_cores(attn_theirs).astype(f32)).astype(bf16)
-        attn_share = lax.psum_scatter(attn_sum, "ctx", scatter_dimension=0, tiled=True)
-        own_grad = stream_grad.astype(bf16)
-        boundary[section] = own_grad
-        if section == 1:
-            both_grad = jnp.concatenate([own_grad, swap_cores(own_grad)], axis=0)
-        grads[section] = (wide_share, down_share, attn_share, attn_gain_term, ffn_gain_term)
-
-    def to_owner(pair):
-        keep_part = jnp.where(first, pair[0], pair[1])
-        got_part = swap_cores(jnp.where(first, pair[1], pair[0]))
-        return jnp.where(first, keep_part, got_part), jnp.where(first, got_part, keep_part)
-
-    section_outputs = jnp.stack(to_owner(outs))
-    boundary_grads = jnp.stack(to_owner(boundary))
-    wide_a, wide_b = to_owner((grads[0][0], grads[1][0]))
-    down_a, down_b = to_owner((grads[0][1], grads[1][1]))
-    attn_full = jnp.concatenate(to_owner((grads[0][2], grads[1][2])), axis=1).astype(f32)
-    gain_terms = jnp.stack([jnp.stack(grads[0][3:]), jnp.stack(grads[1][3:])])
-    gain_sum = pick(lax.psum(gain_terms, ("pipe", "ctx")), core)
-    own_width = attn_gain.shape[1]
-    gain_own = lax.dynamic_slice_in_dim(gain_sum, shard * own_width, own_width, 1)
+    )
     key_at = n_query + n_key
     value_at = key_at + n_key
     return (
         section_outputs[None],
         boundary_grads[None],
-        gain_own[0][None],
+        gains_out[:1],
         attn_full[:, :n_query][None],
         attn_full[:, n_query:key_at][None],
         attn_full[:, key_at:value_at][None],
         attn_full[:, value_at:].T[None],
-        gain_own[1][None],
-        jnp.concatenate([wide_a[:, :half], wide_b[:, :half]], axis=1).astype(f32)[None],
-        jnp.concatenate([wide_a[:, half:], wide_b[:, half:]], axis=1).astype(f32)[None],
-        jnp.concatenate([down_a.T, down_b.T], axis=0).astype(f32)[None],
+        gains_out[1:],
+        gate_out[None],
+        up_out[None],
+        down_out[None],
     )
 
 

time: 1140 us -> 1140 us (level)
  local copies, waits for them, and re-layouts: 57 us -> 163 us
  waiting for transfers between devices: 766 us -> 677 us
  blocking collectives: 48.1 us -> 0 us
  matrix products: 126 us -> 91.9 us
  Pallas kernels: 0 us -> 26.2 us
  starting transfers between devices: 14.6 us -> 39.7 us
  between operations: 17.9 us -> 30.4 us
    ppermute x0 -> x19, waiting for transfers between devices: none -> 122 us  [the longest x2 45 us: ring_gather(): from_back = lax.ppermute(from_back, 'ctx', ahead)]
    psum x7, waiting for transfers between devices: 310 us -> 219 us  [sum_tensor(): return (lax.psum(partial, 'tensor').astype(f32), *others)]
    reduce_scatter x6 -> x4, waiting for transfers between devices: 244 us -> 165 us  [the longest x2 106 us: ffn_backward(): wide_share = lax.psum_scatter(terms, 'ctx', scatter_dimension=0, tiled=True)]
    dynamic_slice x0 -> x6, local copies, waits for them, and re-layouts: none -> 50.9 us  [the longest x2 27.3 us: attention_backward(): mine = lax.dynamic_index_in_dim(terms, core, 1, keepdims=False)]
    all_gather x3 -> x4, waiting for transfers between devices: 173 us -> 124 us  [gather(): return lax.all_gather(shard_part, 'ctx', axis=0, tiled=True)]
    dot_general x8 -> x4, matrix products: 39.7 us -> 7 us  [rows_product(): lax.dot_general(left, right, (((0,), (0,)), ((), ())), preferred_element_...]
    unnamed x251 -> x276, local copies, waits for them, and re-layouts: 31.7 us -> 59.6 us
    psum x1 -> x0, blocking collectives: 27.4 us -> none  [on_device(): gain_sum = pick(lax.psum(gain_terms, ('pipe', 'ctx')), core)]
  transfers between devices with their start and end apart: 35 -> 58, of which waited for: 25 -> 34; matrix products, arithmetic and copies ran while one was open for 13% -> 26% of each run, Pallas kernels for 0% -> 2%
where the time goes in v2:
time: 1140 us; the launch traced here: 1120 us
  waiting for transfers between devices  677 us (59%)
  local copies, waits for them, and re-layouts  163 us (14%)
  other arithmetic  96 us (8%)
  matrix products  91.9 us (8%)
  starting transfers between devices  39.7 us (3%)
  between operations  30.4 us (3%)
  Pallas kernels  26.2 us (2%)
    psum x7, waiting for transfers between devices, sum_tensor(): return (lax.psum(partial, 'tensor').astype(f32), *others)  219 us
    all_gather x4, waiting for transfers between devices, gather(): return lax.all_gather(shard_part, 'ctx', axis=0, tiled=True)  124 us
    reduce_scatter x2, waiting for transfers between devices, ffn_backward(): wide_share = lax.psum_scatter(terms, 'ctx', scatter_dimension=0, tiled=True)  106 us
    unnamed x276, local copies, waits for them, and re-layouts  59.6 us
    reduce_scatter x2, waiting for transfers between devices, ffn_backward(): lax.psum_scatter(token_terms(upstream_both, hidden), 'ctx', scatter_dimen...  58.6 us
    ppermute x2, waiting for transfers between devices, ring_gather(): from_back = lax.ppermute(from_back, 'ctx', ahead)  45 us
    dot_general x8, matrix products, product(): lax.dot_general(left, right, (((1,), (0,)), ((), ())), preferred_element_...  36.4 us
    dot_general x8, matrix products, cols_product(): lax.dot_general(left, right, (((1,), (1,)), ((), ())), preferred_element_...  31.5 us
  transfers between devices with their start and end apart: 58, of which 34 were waited for; matrix products, arithmetic and copies ran while one was open for 26% of the time, Pallas kernels for 2%

profile of v2, /device:TPU:0, one launch (start us, length us, event | category | flops | bytes accessed | tf_op | source)
XLA Modules:
  0.0 1124.8 jit_solution(481794562880390102)
XLA Ops:
  50.7 22.8 %collective-permute-done.1 = bf16[272,1280]{1,0:T(8,128)(2,1)S(1)} collective-permute-done((bf16[272,1280]{1,0:T(8,128)(2,1)S(1)}, bf16[272,1280]{1,0:T(8,128)(2,1)S(1)}, u32[]{:S(2)}, u32[]{:S(2)}) %collective-permute-start.1) | collective-permute-done | bytes 696352 | tf_op jit(solution)/shard_map/ppermute | solution.py:68
  77.4 14.1 %collective-permute-done.3 = bf16[272,640]{1,0:T(8,128)(2,1)S(1)} collective-permute-done((bf16[272,640]{1,0:T(8,128)(2,1)S(1)}, bf16[272,640]{1,0:T(8,128)(2,1)S(1)}, u32[]{:S(2)}, u32[]{:S(2)}) %collective-permute-start.3) | collective-permute-done | bytes 348192 | tf_op jit(solution)/shard_map/ppermute | solution.py:72
  131.9 53.6 %all-reduce.10.cloned.1.call-done = bf16[256,2048]{1,0:T(8,128)(2,1)} async-done(((bf16[256,2048]{1,0:T(8,128)(2,1)}), bf16[256,2048]{1,0:T(8,128)(2,1)}) %all-reduce.10.cloned.1.call-update) | async-done | bytes 1048592 | tf_op jit(solution)/shard_map/psum | solution.py:335
  193.1 22.2 %collective-permute-done.11 = bf16[272,1280]{1,0:T(8,128)(2,1)S(1)} collective-permute-done((bf16[272,1280]{1,0:T(8,128)(2,1)S(1)}, bf16[272,1280]{1,0:T(8,128)(2,1)S(1)}, u32[]{:S(2)}, u32[]{:S(2)}) %collective-permute-start.11) | collective-permute-done | bytes 696352 | tf_op jit(solution)/shard_map/ppermute | solution.py:68
  229.6 21.4 %all-gather.7.cloned.1.call-done = bf16[2048,1024]{1,0:T(8,128)(2,1)} async-done(((bf16[512,1024]{1,0:T(8,128)(2,1)}), bf16[2048,1024]{1,0:T(8,128)(2,1)}) %all-gather.7.cloned.1.call-update) | async-done | bytes 4194320 | tf_op jit(solution)/shard_map/all_gather | solution.py:511
  265.2 46.5 %all-reduce.12.cloned.1.call-done = bf16[256,2048]{1,0:T(8,128)(2,1)} async-done(((bf16[256,2048]{1,0:T(8,128)(2,1)}), bf16[256,2048]{1,0:T(8,128)(2,1)}) %all-reduce.12.cloned.1.call-update) | async-done | bytes 1048592 | tf_op jit(solution)/shard_map/psum | solution.py:335
  342.0 61.3 %all-gather.9.cloned.1.call-done = bf16[2048,2048]{1,0:T(8,128)(2,1)} async-done(((bf16[512,2048]{1,0:T(8,128)(2,1)}), bf16[2048,2048]{1,0:T(8,128)(2,1)}) %all-gather.9.cloned.1.call-update) | async-done | bytes 8388624 | tf_op jit(solution)/shard_map/all_gather | solution.py:511
  404.3 53.6 %all-reduce.14.cloned.1.call-done = bf16[256,2048]{1,0:T(8,128)(2,1)} async-done(((bf16[256,2048]{1,0:T(8,128)(2,1)}), bf16[256,2048]{1,0:T(8,128)(2,1)}) %all-reduce.14.cloned.1.call-update) | async-done | bytes 1048592 | tf_op jit(solution)/shard_map/psum | solution.py:335
  465.0 11.5 %fusion.141 = f32[512,2048]{1,0:T(8,128)} fusion(bf16[2048,2048]{1,0:T(8,128)(2,1)} %all-gather.9.cloned.1.call-done, bf16[256,2048]{1,0:T(8,128)(2,1)S(1)} %collective-permute-done.17, bf16[256,2048]{1,0:T(8,128)(2,1)} %multiply_convert_fusion.5), kind=kOutput, calls=%fused_computation.354 | convolution fusion | flops 4299161600 | bytes 14680064 | tf_op jit(solution)/shard_map/dot_general | solution.py:226
  476.5 36.1 %all-gather.11.cloned.1.call-done = bf16[2048,1024]{1,0:T(8,128)(2,1)} async-done(((bf16[512,1024]{1,0:T(8,128)(2,1)}), bf16[2048,1024]{1,0:T(8,128)(2,1)}) %all-gather.11.cloned.1.call-update) | async-done | bytes 4194320 | tf_op jit(solution)/shard_map/all_gather | solution.py:511
  553.2 30.6 %all-reduce.16.cloned.1.call-done = bf16[256,2048]{1,0:T(8,128)(2,1)} async-done(((bf16[256,2048]{1,0:T(8,128)(2,1)}), bf16[256,2048]{1,0:T(8,128)(2,1)}) %all-reduce.16.cloned.1.call-update) | async-done | bytes 1048592 | tf_op jit(solution)/shard_map/psum | solution.py:335
  614.0 28.2 %reduce-scatter.5.cloned.1.call-done.high_ref = bf16[512,1024]{1,0:T(8,128)(2,1)} async-done(((bf16[2048,1024]{1,0:T(8,128)(2,1)}), bf16[512,1024]{1,0:T(8,128)(2,1)}) %reduce-scatter.5.cloned.1.call-update) | async-done | bytes 1048592 | tf_op jit(solution)/shard_map/reduce_scatter | solution.py:395
  659.4 13.8 %constant_dynamic-slice_fusion.5 = (bf16[4,1,256,1280]{2,1,0,3:T(2,128)(2,1)}, bf16[4,1,256,1280]{2,1,0,3:T(2,128)(2,1)}) fusion(bf16[4,2,256,1280]{2,1,0,3:T(2,128)(2,1)} %reshape.322, s32[]{:T(128)S(6)} %select_n.282, s32[]{:T(128)S(6)} %select_n.324), kind=kLoop, calls=%fused_computation.306 | loop fusion | bytes 10485768 | tf_op jit(solution)/shard_map/jit(dynamic_index_in_dim)/dynamic_slice | solution.py:444
  673.2 11.1 copy.102
  684.3 11.1 copy.126
  719.4 66.4 %reduce-scatter.7.cloned.1.call-done.high_ref = bf16[512,2048]{1,0:T(8,128)(2,1)} async-done(((bf16[2048,2048]{1,0:T(8,128)(2,1)}), bf16[512,2048]{1,0:T(8,128)(2,1)}) %reduce-scatter.7.cloned.1.call-update) | async-done | bytes 2097168 | tf_op jit(solution)/shard_map/reduce_scatter | solution.py:399
  868.6 30.4 %reduce-scatter.9.cloned.1.call-done.low_ref = bf16[512,1024]{1,0:T(8,128)(2,1)} async-done(((bf16[2048,1024]{1,0:T(8,128)(2,1)}), bf16[512,1024]{1,0:T(8,128)(2,1)}) %reduce-scatter.9.cloned.1.call-update) | async-done | bytes 1048592 | tf_op jit(solution)/shard_map/reduce_scatter | solution.py:395
  915.6 13.5 %constant_dynamic-slice_fusion.7 = (bf16[4,1,256,1280]{2,1,0,3:T(2,128)(2,1)}, bf16[4,1,256,1280]{2,1,0,3:T(2,128)(2,1)}) fusion(bf16[4,2,256,1280]{2,1,0,3:T(2,128)(2,1)} %reshape.329, s32[]{:T(128)S(6)} %select_n.282, s32[]{:T(128)S(6)} %select_n.324), kind=kLoop, calls=%fused_computation.308 | loop fusion | bytes 10485768 | tf_op jit(solution)/shard_map/jit(dynamic_index_in_dim)/dynamic_slice | solution.py:444
  929.1 11.2 copy.108
  942.0 11.1 copy.127
  955.8 33.2 %all-reduce.22.cloned.1.call-done = (bf16[256,2048]{1,0:T(8,128)(2,1)}, bf16[256,2048]{1,0:T(8,128)(2,1)}) async-done(((bf16[256,2048]{1,0:T(8,128)(2,1)}, bf16[256,2048]{1,0:T(8,128)(2,1)}), (bf16[256,2048]{1,0:T(8,128)(2,1)}, bf16[256,2048]{1,0:T(8,128)(2,1)})) %all-reduce.22.cloned.1.call-update) | async-done | bytes 2097168 | tf_op jit(solution)/shard_map/psum | solution.py:335
  1010.5 14.3 %collective-permute-done.38 = bf16[256,640]{1,0:T(8,128)(2,1)S(1)} collective-permute-done((bf16[256,640]{1,0:T(8,128)(2,1)S(1)}, bf16[256,640]{1,0:T(8,128)(2,1)S(1)}, u32[]{:S(2)}, u32[]{:S(2)}) %collective-permute-start.38) | collective-permute-done | bytes 327712 | tf_op jit(solution)/shard_map/ppermute | solution.py:87
  1029.9 25.8 %collective-permute-done.39 = bf16[256,1280]{1,0:T(8,128)(2,1)S(1)} collective-permute-done((bf16[256,1280]{1,0:T(8,128)(2,1)S(1)}, bf16[256,1280]{1,0:T(8,128)(2,1)S(1)}, u32[]{:S(2)}, u32[]{:S(2)}) %collective-permute-start.39) | collective-permute-done | bytes 655392 | tf_op jit(solution)/shard_map/ppermute | solution.py:96
  1058.7 39.9 %reduce-scatter.11.cloned.1.call-done.low_ref = bf16[512,2048]{1,0:T(8,128)(2,1)} async-done(((bf16[2048,2048]{1,0:T(8,128)(2,1)}), bf16[512,2048]{1,0:T(8,128)(2,1)}) %reduce-scatter.11.cloned.1.call-update) | async-done | bytes 2097168 | tf_op jit(solution)/shard_map/reduce_scatter | solution.py:399
  (627 shorter events, 410.4 us)
Async XLA Ops:
  7.2 123.5 %all-gather.5.cloned.1.call-start = ((), (), s32[]{:S(2)}) async-start(), calls=%async_computation.4 | async-start | bytes 10485760 | tf_op jit(solution)/shard_map/all_gather | solution.py:511
  21.1 164.4 %all-reduce.10.cloned.1.call-start = ((), (), s32[]{:S(2)}) async-start(), calls=%async_computation.5 | async-start | bytes 2097152 | tf_op jit(solution)/shard_map/psum | solution.py:335
  130.7 120.3 %all-gather.7.cloned.1.call-start = ((), (), s32[]{:S(2)}) async-start(), calls=%async_computation.6 | async-start | bytes 5242880 | tf_op jit(solution)/shard_map/all_gather | solution.py:511
  131.5 180.2 %all-reduce.12.cloned.1.call-start = ((), (), s32[]{:S(2)}) async-start(), calls=%async_computation.7 | async-start | bytes 2097152 | tf_op jit(solution)/shard_map/psum | solution.py:335
  188.3 31.3 %collective-permute-start.9 = (bf16[256,2048]{1,0:T(8,128)(2,1)S(1)}, bf16[256,2048]{1,0:T(8,128)(2,1)S(1)}, u32[]{:S(2)}, u32[]{:S(2)}) collective-permute-start(bf16[256,2048]{1,0:T(8,128)(2,1)S(1)} %multiply_convert_fusion.7), channel_id=1, source_target_pairs={{0,16},{16,0},{1,17},{17,1},{2,18},{18,2},{3,19},{19,3},{4,20},{20... | collective-permute-start | bytes 3145736 | tf_op jit(solution)/shard_map/ppermute | solution.py:22
  216.1 41.5 %collective-permute-start.13 = (bf16[272,640]{1,0:T(8,128)(2,1)}, bf16[272,640]{1,0:T(8,128)(2,1)}, u32[]{:S(2)}, u32[]{:S(2)}) collective-permute-start(bf16[272,640]{1,0:T(8,128)(2,1)} %slice.361), channel_id=1, source_target_pairs={{0,4},{4,12},{12,8},{8,0},{1,5},{5,13},{13,9},{9,1},{2,6},{6,14},{... | collective-permute-start | bytes 1044488 | tf_op jit(solution)/shard_map/ppermute | solution.py:72
  219.4 40.0 %collective-permute-start.14 = (bf16[272,640]{1,0:T(8,128)(2,1)}, bf16[272,640]{1,0:T(8,128)(2,1)}, u32[]{:S(2)}, u32[]{:S(2)}) collective-permute-start(bf16[272,640]{1,0:T(8,128)(2,1)} %slice.362), channel_id=1, source_target_pairs={{4,0},{12,4},{8,12},{0,8},{5,1},{13,5},{9,13},{1,9},{6,2},{14,6},{... | collective-permute-start | bytes 1044488 | tf_op jit(solution)/shard_map/ppermute | solution.py:73
  262.5 140.8 %all-gather.9.cloned.1.call-start = ((), (), s32[]{:S(2)}) async-start(), calls=%async_computation.8 | async-start | bytes 10485760 | tf_op jit(solution)/shard_map/all_gather | solution.py:511
  263.1 194.9 %all-reduce.14.cloned.1.call-start = ((), (), s32[]{:S(2)}) async-start(), calls=%async_computation.9 | async-start | bytes 2097152 | tf_op jit(solution)/shard_map/psum | solution.py:335
  263.1 50.8 %collective-permute-start.15 = (bf16[4,272,1280]{2,1,0:T(8,128)(2,1)}, bf16[4,272,1280]{2,1,0:T(8,128)(2,1)}, u32[]{:S(2)}, u32[]{:S(2)}) collective-permute-start(bf16[4,272,1280]{2,1,0:T(8,128)(2,1)} %bitcast_dynamic-update-slice_fusion.6), channel_id=1, source_target_pairs={{0,16},{16,0},{1,17},{17,1},{2,18},{18,2},{3,19},{19,3},{4,20},{20... | collective-permute-start | bytes 8355848 | tf_op jit(solution)/shard_map/ppermute | solution.py:22
  403.3 109.3 %all-gather.11.cloned.1.call-start = ((), (), s32[]{:S(2)}) async-start(), calls=%async_computation.10 | async-start | bytes 5242880 | tf_op jit(solution)/shard_map/all_gather | solution.py:511
  404.1 179.7 %all-reduce.16.cloned.1.call-start = ((), (), s32[]{:S(2)}) async-start(), calls=%async_computation.11 | async-start | bytes 2097152 | tf_op jit(solution)/shard_map/psum | solution.py:335
  531.9 110.3 %reduce-scatter.5.cloned.1.call-start = ((), (), s32[]{:S(2)}) async-start(), calls=%async_computation.12 | async-start | bytes 5242880 | tf_op jit(solution)/shard_map/reduce_scatter | solution.py:395
  538.6 161.5 %all-reduce.18.cloned.1.call-start = ((), (), s32[]{:S(2)}) async-start(), calls=%async_computation.13 | async-start | bytes 2097152 | tf_op jit(solution)/shard_map/psum | solution.py:335
  642.2 143.6 %reduce-scatter.7.cloned.1.call-start = ((), (), s32[]{:S(2)}) async-start(), calls=%async_computation.14 | async-start | bytes 10485760 | tf_op jit(solution)/shard_map/reduce_scatter | solution.py:399
  643.0 197.6 %all-reduce.20.cloned.1.call-start = ((), (), s32[]{:S(2)}) async-start(), calls=%async_computation.15 | async-start | bytes 2097152 | tf_op jit(solution)/shard_map/psum | solution.py:335
  785.9 113.1 %reduce-scatter.9.cloned.1.call-start = ((), (), s32[]{:S(2)}) async-start(), calls=%async_computation.16 | async-start | bytes 5242880 | tf_op jit(solution)/shard_map/reduce_scatter | solution.py:395
  796.8 192.2 %all-reduce.22.cloned.1.call-start = ((), (), s32[]{:S(2)}) async-start(), calls=%async_computation.18 | async-start | bytes 4194304 | tf_op jit(solution)/shard_map/psum | solution.py:335
  899.0 199.6 %reduce-scatter.11.cloned.1.call-start = ((), (), s32[]{:S(2)}) async-start(), calls=%async_computation.17 | async-start | bytes 10485760 | tf_op jit(solution)/shard_map/reduce_scatter | solution.py:399
  940.4 52.0 %collective-permute-start.30 = (bf16[4,256,1280]{2,1,0:T(8,128)(2,1)}, bf16[4,256,1280]{2,1,0:T(8,128)(2,1)}, u32[]{:S(2)}, u32[]{:S(2)}) collective-permute-start(bf16[4,256,1280]{2,1,0:T(8,128)(2,1)} %bitcast.394), channel_id=1, source_target_pairs={{0,16},{16,0},{1,17},{17,1},{2,18},{18,2},{3,19},{19,3},{4,20},{20... | collective-permute-start | bytes 7864328 | tf_op jit(solution)/shard_map/ppermute | solution.py:22
  992.0 35.4 %collective-permute-start.19 = (bf16[256,2048]{1,0:T(8,128)(2,1)S(1)}, bf16[256,2048]{1,0:T(8,128)(2,1)S(1)}, u32[]{:S(2)}, u32[]{:S(2)}) collective-permute-start(bf16[256,2048]{1,0:T(8,128)(2,1)S(1)} %broadcast_select_fusion.6), channel_id=1, source_target_pairs={{0,16},{16,0},{1,17},{17,1},{2,18},{18,2},{3,19},{19,3},{4,20},{20... | collective-permute-start | bytes 3145736 | tf_op jit(solution)/shard_map/ppermute | solution.py:22
  1000.6 101.0 %collective-permute-start.31 = (bf16[256,2048]{1,0:T(8,128)(2,1)}, bf16[256,2048]{1,0:T(8,128)(2,1)}, u32[]{:S(2)}, u32[]{:S(2)}) collective-permute-start(bf16[256,2048]{1,0:T(8,128)(2,1)} %get-tuple-element.92), channel_id=1, source_target_pairs={{0,16},{16,0},{1,17},{17,1},{2,18},{18,2},{3,19},{19,3},{4,20},{20... | collective-permute-start | bytes 3145736 | tf_op jit(solution)/shard_map/ppermute | solution.py:22
  1026.3 31.0 %collective-permute-start.37 = (bf16[256,1280]{1,0:T(8,128)(2,1)S(1)}, bf16[256,1280]{1,0:T(8,128)(2,1)S(1)}, u32[]{:S(2)}, u32[]{:S(2)}) collective-permute-start(bf16[256,1280]{1,0:T(8,128)(2,1)S(1)} %pad_maximum_fusion.17), channel_id=1, source_target_pairs={{0,4},{4,12},{12,8},{8,0},{1,5},{5,13},{13,9},{9,1},{2,6},{6,14},{... | collective-permute-start | bytes 1966088 | tf_op jit(solution)/shard_map/ppermute | solution.py:95
  1058.7 45.9 %collective-permute-start.40 = (bf16[256,1280]{1,0:T(8,128)(2,1)}, bf16[256,1280]{1,0:T(8,128)(2,1)}, u32[]{:S(2)}, u32[]{:S(2)}) collective-permute-start(bf16[256,1280]{1,0:T(8,128)(2,1)} %get-tuple-element.90), channel_id=1, source_target_pairs={{0,16},{16,0},{1,17},{17,1},{2,18},{18,2},{3,19},{19,3},{4,20},{20... | collective-permute-start | bytes 1966088 | tf_op jit(solution)/shard_map/ppermute | solution.py:22
  (170 other events, 1915.6 us)
Sparse Core Ops, SparseCore 0:
  21.2 109.4 all-gather.4
  133.6 51.7 all-reduce.9
  188.0 62.9 all-gather.6
  262.6 49.0 all-reduce.11
  313.9 89.3 all-gather.8
  406.1 51.8 all-reduce.13
  460.5 52.0 all-gather.10
  532.0 51.8 all-reduce.15
  587.4 54.7 reduce-scatter.4
  645.1 51.8 all-reduce.17
  700.0 85.7 reduce-scatter.6
  788.8 51.7 all-reduce.19
  844.1 54.7 reduce-scatter.8
  902.0 87.0 all-reduce.21
  991.9 106.5 reduce-scatter.10

commit v3 on v2

--- a/solution.py
+++ b/solution.py
@@ -1,3 +1,4 @@
+import functools
 import math
 
 import jax
@@ -128,6 +129,68 @@
         ),
         name="token_terms",
     )(left, right)
+
+
+def attention_terms_kernel(normed_ref, mid_grad_ref, grads_ref, mixed_ref, out_ref):
+    n_grads = grads_ref.shape[1]
+    half = out_ref.shape[1]
+    rows = (((0,), (0,)), ((), ()))
+    inner = lax.dot_general(normed_ref[...], grads_ref[...], rows, preferred_element_type=f32)
+    outer = lax.dot_general(mid_grad_ref[...], mixed_ref[...], rows, preferred_element_type=f32)
+    for part in range(2):
+        part_rows = slice(part * half, (part + 1) * half)
+        out_ref[part, :, :n_grads] = inner[part_rows].astype(bf16)
+        out_ref[part, :, n_grads:] = outer[part_rows].astype(bf16)
+
+
+def attention_terms(normed, mid_grad, grads, mixed, count):
+    tokens, width = normed.shape
+    columns = grads.shape[1] + mixed.shape[1]
+    tile = width // count
+    return pl.pallas_call(
+        attention_terms_kernel,
+        grid=(count,),
+        in_specs=[
+            pl.BlockSpec((tokens, tile), lambda i: (0, i)),
+            pl.BlockSpec((tokens, tile), lambda i: (0, i)),
+            pl.BlockSpec((tokens, grads.shape[1]), lambda i: (0, 0)),
+            pl.BlockSpec((tokens, mixed.shape[1]), lambda i: (0, 0)),
+        ],
+        out_specs=pl.BlockSpec((2, None, tile // 2, columns), lambda i: (0, i, 0, 0)),
+        out_shape=jax.ShapeDtypeStruct((2, count, tile // 2, columns), bf16),
+        compiler_params=pltpu.CompilerParams(vmem_limit_bytes=40 * 2**20),
+        cost_estimate=pl.CostEstimate(
+            flops=2 * tokens * width * columns,
+            bytes_accessed=2 * (width * columns + 2 * tokens * width + tokens * columns),
+            transcendentals=0,
+        ),
+        name="attention_terms",
+    )(normed, mid_grad, grads, mixed)
+
+
+def section_stack_kernel(core_ref, low_ref, high_ref, got_ref, out_ref):
+    keep = jnp.where(core_ref[0] == 0, low_ref[...], high_ref[...])
+    out_ref[...] = jnp.where(core_ref[0] == pl.program_id(0), keep, got_ref[...])
+
+
+def section_stack(core, low, high, got):
+    rows, width = got.shape
+    block = pl.BlockSpec((rows, width), lambda i, core: (0, 0))
+    return pl.pallas_call(
+        section_stack_kernel,
+        grid_spec=pltpu.PrefetchScalarGridSpec(
+            num_scalar_prefetch=1,
+            grid=(2,),
+            in_specs=[block, block, block],
+            out_specs=pl.BlockSpec((None, rows, width), lambda i, core: (i, 0, 0)),
+        ),
+        out_shape=jax.ShapeDtypeStruct((2, rows, width), got.dtype),
+        compiler_params=pltpu.CompilerParams(vmem_limit_bytes=40 * 2**20),
+        cost_estimate=pl.CostEstimate(
+            flops=0, bytes_accessed=5 * rows * width * 2, transcendentals=0
+        ),
+        name="section_stack",
+    )(core.reshape(1), low, high, got)
 
 
 def wide_outputs_kernel(core_ref, low_ref, high_ref, got_ref, gate_ref, up_ref):
@@ -240,29 +303,6 @@
     )
 
 
-def rope_tables(positions_row, width):
-    frequency = jnp.exp(
-        jnp.arange(width // 2, dtype=f32) * (-2.0 * math.log(rope_base) / width)
-    )
-    angles = positions_row.astype(f32)[:, None] * frequency[None, :]
-    cosine_table = jnp.concatenate([jnp.cos(angles), jnp.cos(angles)], axis=1)
-    sine_table = jnp.concatenate([jnp.sin(angles), jnp.sin(angles)], axis=1)
-    return (cosine_table, sine_table)
-
-
-def rotate(values, cosine_table, sine_table):
-    half_width = values.shape[-1] // 2
-    turned = jnp.concatenate([-values[..., half_width:], values[..., :half_width]], axis=-1)
-    return values * cosine_table[:, None, :] + turned * sine_table[:, None, :]
-
-
-def rotate_back(grads_in, cosine_table, sine_table):
-    half_width = grads_in.shape[-1] // 2
-    scaled = grads_in * sine_table[:, None, :]
-    turned = jnp.concatenate([-scaled[..., half_width:], scaled[..., :half_width]], axis=-1)
-    return grads_in * cosine_table[:, None, :] - turned
-
-
 def norm_forward(stream, gain_vector):
     inv_rms = lax.rsqrt(jnp.mean(stream * stream, axis=-1) + epsilon)
     return ((stream * inv_rms[:, None] * gain_vector[None, :]).astype(bf16), inv_rms)
@@ -278,56 +318,6 @@
     return (stream_grad, gain_grad)
 
 
-def scores(query_block, key_block, allowed):
-    raw_scores = jnp.einsum(
-        "qkgd,skd->kgqs", query_block, key_block, preferred_element_type=f32
-    ) * HEAD_DIM ** (-0.5)
-    return jnp.where(allowed[None, None], raw_scores, -1e30)
-
-
-def attend(query_block, key_block, value_block, allowed):
-    masked = scores(query_block, key_block, allowed)
-    row_top = jnp.max(masked, axis=-1, keepdims=True)
-    exponent = jnp.exp(masked - row_top)
-    row_total = jnp.sum(exponent, axis=-1, keepdims=True)
-    weights_block = (exponent / row_total).astype(bf16)
-    mixed_rows = jnp.einsum(
-        "kgqs,skd->qkgd", weights_block, value_block, preferred_element_type=f32
-    )
-    return (mixed_rows, (row_top + jnp.log(row_total))[..., 0])
-
-
-def attend_back(
-    query_block, key_block, value_block, allowed, log_block, mixed_block, grad_block
-):
-    masked = scores(query_block, key_block, allowed)
-    probability = jnp.exp(masked - log_block[..., None])
-    prob_grad = jnp.einsum(
-        "qkgd,skd->kgqs", grad_block, value_block, preferred_element_type=f32
-    )
-    row_delta = jnp.transpose(
-        jnp.sum(grad_block.astype(f32) * mixed_block.astype(f32), axis=-1),
-        (1, 2, 0),
-    )
-    score_grad = (probability * (prob_grad - row_delta[..., None])).astype(bf16)
-    scale_factor = HEAD_DIM ** (-0.5)
-    query_grad = (
-        jnp.einsum("kgqs,skd->qkgd", score_grad, key_block, preferred_element_type=f32)
-        * scale_factor
-    )
-    key_part = (
-        jnp.einsum("kgqs,qkgd->skd", score_grad, query_block, preferred_element_type=f32)
-        * scale_factor
-    )
-    value_part = jnp.einsum(
-        "kgqs,qkgd->skd",
-        probability.astype(bf16),
-        grad_block,
-        preferred_element_type=f32,
-    )
-    return (query_grad, key_part, value_part)
-
-
 def sum_tensor(partial, *others):
     partial = partial.astype(bf16)
     if others:
@@ -340,29 +330,338 @@
     return partial[:rows] + arrived.astype(f32)
 
 
+def half_swap(values):
+    lanes = lax.broadcasted_iota(jnp.int32, values.shape, 1)
+    count = values.shape[1]
+    quarter = HEAD_DIM // 2
+    return jnp.where(
+        lanes % HEAD_DIM < quarter,
+        pltpu.roll(values, count - quarter, 1),
+        pltpu.roll(values, quarter, 1),
+    )
+
+
+def wide_table(table, columns):
+    return jnp.concatenate([table] * (columns // table.shape[1]), axis=1)
+
+
+def rope_tables(positions_row, width):
+    frequency = jnp.exp(
+        jnp.arange(width // 2, dtype=f32) * (-2.0 * math.log(rope_base) / width)
+    )
+    angles = positions_row.astype(f32)[:, None] * frequency[None, :]
+    cosine, sine = jnp.cos(angles), jnp.sin(angles)
+    return (
+        jnp.concatenate([cosine] * 4, axis=1),
+        jnp.concatenate([-sine, sine] * 2, axis=1),
+    )
+
+
+def head_inputs_kernel(sizes, stream_ref, gain_ref, wide_ref, cos_ref, sin_ref,
+                       normed_ref, rms_ref, query_ref, own_ref):
+    n_query, n_key = sizes
+    stream = stream_ref[...].astype(f32)
+    inv_rms = lax.rsqrt(jnp.mean(stream * stream, axis=1, keepdims=True) + epsilon)
+    normed = (stream * inv_rms * gain_ref[...]).astype(bf16)
+    normed_ref[...] = normed
+    rms_ref[...] = inv_rms
+    raw = jnp.dot(normed, wide_ref[...], preferred_element_type=f32)
+    turned = raw[:, : n_query + n_key]
+    cosine = wide_table(cos_ref[...], n_query + n_key)
+    sine = wide_table(sin_ref[...], n_query + n_key)
+    turned = turned * cosine + half_swap(turned) * sine
+    query_ref[...] = turned[:, :n_query].astype(bf16)
+    own_ref[:, :n_key] = turned[:, n_query:].astype(bf16)
+    own_ref[:, n_key:] = raw[:, n_query + n_key :].astype(bf16)
+
+
+def params(megabytes=48):
+    return pltpu.CompilerParams(vmem_limit_bytes=megabytes * 2**20)
+
+
+def cost(flops, bytes_accessed, transcendentals=0):
+    return pl.CostEstimate(
+        flops=flops, bytes_accessed=bytes_accessed, transcendentals=transcendentals
+    )
+
+
+def head_inputs(stream, gain, wide, tables, sizes):
+    n_query, n_key = sizes
+    rows, width = stream.shape
+    columns = n_query + 2 * n_key
+    whole = lambda *shape: pl.BlockSpec(shape, lambda i: (0,) * len(shape))
+    return pl.pallas_call(
+        functools.partial(head_inputs_kernel, sizes),
+        grid=(1,),
+        in_specs=[
+            whole(rows, width),
+            whole(1, width),
+            whole(width, columns),
+            whole(rows, 2 * HEAD_DIM),
+            whole(rows, 2 * HEAD_DIM),
+        ],
+        out_specs=[whole(rows, width), whole(rows, 1), whole(rows, n_query), whole(rows, 2 * n_key)],
+        out_shape=[
+            jax.ShapeDtypeStruct((rows, width), bf16),
+            jax.ShapeDtypeStruct((rows, 1), f32),
+            jax.ShapeDtypeStruct((rows, n_query), bf16),
+            jax.ShapeDtypeStruct((rows, 2 * n_key), bf16),
+        ],
+        compiler_params=params(),
+        cost_estimate=cost(2 * rows * width * columns, 2 * width * (columns + 4 * rows)),
+        name="head_inputs",
+    )(stream, gain[None], wide, *tables)
+
+
+def masked_scores(query, keys, allowed):
+    raw = lax.dot_general(query, keys, (((1,), (1,)), ((), ())), preferred_element_type=f32)
+    return jnp.where(allowed, raw * HEAD_DIM ** (-0.5), -1e30)
+
+
+def allowed_pairs(pos, rows):
+    distance = (
+        lax.broadcasted_iota(jnp.int32, (rows, 2 * rows), 0)
+        - lax.broadcasted_iota(jnp.int32, (rows, 2 * rows), 1)
+        + rows
+    )
+    return (distance >= 0) & (distance <= pos)
+
+
+def head_slice(index):
+    return slice(index * HEAD_DIM, (index + 1) * HEAD_DIM)
+
+
+def mix_kernel(n_key, pos_ref, query_ref, tail_ref, own_ref, wide_ref,
+               mixed_ref, log_ref, partial_ref, window, mixed_all):
+    rows, n_query = query_ref.shape
+
+    @pl.when(pl.program_id(0) == 0)
+    def _():
+        window[:rows] = tail_ref[...]
+        window[rows:] = own_ref[...]
+        allowed = allowed_pairs(pos_ref[...], rows)
+        group = HEADS // KV_HEADS
+        logs, mixed = [], []
+        for head in range(n_query // HEAD_DIM):
+            keys = window[:, head_slice(head // group)]
+            values = window[:, head_slice((n_key // HEAD_DIM) + head // group)]
+            masked = masked_scores(query_ref[:, head_slice(head)], keys, allowed)
+            top = jnp.max(masked, axis=1, keepdims=True)
+            exponent = jnp.exp(masked - top)
+            total = jnp.sum(exponent, axis=1, keepdims=True)
+            weights = (exponent * (1.0 / total)).astype(bf16)
+            mixed.append(jnp.dot(weights, values, preferred_element_type=f32).astype(bf16))
+            logs.append(top + jnp.log(total))
+        everything = jnp.concatenate(mixed, axis=1)
+        mixed_all[...] = everything
+        mixed_ref[...] = everything
+        log_ref[...] = jnp.concatenate(logs, axis=1)
+
+    partial_ref[...] = lax.dot_general(
+        mixed_all[...],
+        wide_ref[:, wide_ref.shape[1] - n_query :],
+        (((1,), (1,)), ((), ())),
+        preferred_element_type=f32,
+    ).astype(bf16)
+
+
+def mix(pos, queries, tail, own, wide, n_key):
+    rows, n_query = queries.shape
+    width, columns = wide.shape
+    tile = 512
+    heads = n_query // HEAD_DIM
+    whole = lambda *shape: pl.BlockSpec(shape, lambda i: (0,) * len(shape))
+    return pl.pallas_call(
+        functools.partial(mix_kernel, n_key),
+        grid=(width // tile,),
+        in_specs=[
+            whole(rows, 1),
+            whole(rows, n_query),
+            whole(rows, 2 * n_key),
+            whole(rows, 2 * n_key),
+            pl.BlockSpec((tile, columns), lambda i: (i, 0)),
+        ],
+        out_specs=[
+            whole(rows, n_query),
+            whole(rows, heads),
+            pl.BlockSpec((rows, tile), lambda i: (0, i)),
+        ],
+        out_shape=[
+            jax.ShapeDtypeStruct((rows, n_query), bf16),
+            jax.ShapeDtypeStruct((rows, heads), f32),
+            jax.ShapeDtypeStruct((rows, width), bf16),
+        ],
+        scratch_shapes=[pltpu.VMEM((2 * rows, 2 * n_key), bf16), pltpu.VMEM((rows, n_query), bf16)],
+        compiler_params=params(),
+        cost_estimate=cost(
+            2 * rows * n_query * (width + 4 * rows), 2 * width * (columns + rows), 2 * rows * rows * heads
+        ),
+        name="mix",
+    )(pos, queries, tail, own, wide)
+
+
+def mix_back_kernel(n_key, pos_ref, query_ref, tail_ref, own_ref, mixed_ref, log_ref, cos_ref, sin_ref,
+                    mid_grad_ref, wide_ref, query_grad_ref, back_ref, own_grad_ref, mid_b_ref,
+                    window, mixed_grad):
+    rows, n_query = query_ref.shape
+    step = pl.program_id(0)
+    mid_b = mid_grad_ref[...].astype(bf16)
+    mid_b_ref[...] = mid_b
+    part = jnp.dot(mid_b, wide_ref[:, wide_ref.shape[1] - n_query :], preferred_element_type=f32)
+
+    @pl.when(step == 0)
+    def _():
+        mixed_grad[...] = part
+
+    @pl.when(step > 0)
+    def _():
+        mixed_grad[...] += part
+
+    @pl.when(step == pl.num_programs(0) - 1)
+    def _():
+        window[:rows] = tail_ref[...]
+        window[rows:] = own_ref[...]
+        allowed = allowed_pairs(pos_ref[...], rows)
+        group = HEADS // KV_HEADS
+        groups = n_key // HEAD_DIM
+        scale = HEAD_DIM ** (-0.5)
+        grads = mixed_grad[...].astype(bf16)
+        over_rows = (((0,), (0,)), ((), ()))
+        over_columns = (((1,), (1,)), ((), ()))
+        query_grads, key_grads, value_grads = [], [None] * groups, [None] * groups
+        for head in range(n_query // HEAD_DIM):
+            at = head // group
+            keys = window[:, head_slice(at)]
+            values = window[:, head_slice(groups + at)]
+            query = query_ref[:, head_slice(head)]
+            grad = grads[:, head_slice(head)]
+            masked = masked_scores(query, keys, allowed)
+            prob = jnp.exp(masked - log_ref[:, head : head + 1])
+            prob_grad = lax.dot_general(grad, values, over_columns, preferred_element_type=f32)
+            delta = jnp.sum(
+                grad.astype(f32) * mixed_ref[:, head_slice(head)].astype(f32), axis=1, keepdims=True
+            )
+            score_grad = (prob * (prob_grad - delta)).astype(bf16)
+            query_grads.append(jnp.dot(score_grad, keys, preferred_element_type=f32))
+            key_part = lax.dot_general(score_grad, query, over_rows, preferred_element_type=f32)
+            value_part = lax.dot_general(
+                prob.astype(bf16), grad, over_rows, preferred_element_type=f32
+            )
+            key_grads[at] = key_part if key_grads[at] is None else key_grads[at] + key_part
+            value_grads[at] = value_part if value_grads[at] is None else value_grads[at] + value_part
+        query_grad = jnp.concatenate(query_grads, axis=1) * scale
+        query_grad = query_grad * wide_table(cos_ref[...], n_query) - half_swap(
+            query_grad
+        ) * wide_table(sin_ref[...], n_query)
+        query_grad_ref[...] = query_grad.astype(bf16)
+        key_grad = jnp.concatenate(key_grads, axis=1) * scale
+        value_grad = jnp.concatenate(value_grads, axis=1)
+        back_ref[:, :n_key] = key_grad[:rows].astype(bf16)
+        back_ref[:, n_key:] = value_grad[:rows].astype(bf16)
+        own_grad_ref[:, :n_key] = key_grad[rows:]
+        own_grad_ref[:, n_key:] = value_grad[rows:]
+
+
+def mix_back(pos, queries, tail, own, mixed, logs, tables, mid_grad, wide, n_key):
+    rows, n_query = queries.shape
+    width, columns = wide.shape
+    tile = 512
+    heads = n_query // HEAD_DIM
+    whole = lambda *shape: pl.BlockSpec(shape, lambda i: (0,) * len(shape))
+    return pl.pallas_call(
+        functools.partial(mix_back_kernel, n_key),
+        grid=(width // tile,),
+        in_specs=[
+            whole(rows, 1),
+            whole(rows, n_query),
+            whole(rows, 2 * n_key),
+            whole(rows, 2 * n_key),
+            whole(rows, n_query),
+            whole(rows, heads),
+            whole(rows, 2 * HEAD_DIM),
+            whole(rows, 2 * HEAD_DIM),
+            pl.BlockSpec((rows, tile), lambda i: (0, i)),
+            pl.BlockSpec((tile, columns), lambda i: (i, 0)),
+        ],
+        out_specs=[
+            whole(rows, n_query),
+            whole(rows, 2 * n_key),
+            whole(rows, 2 * n_key),
+            pl.BlockSpec((rows, tile), lambda i: (0, i)),
+        ],
+        out_shape=[
+            jax.ShapeDtypeStruct((rows, n_query), bf16),
+            jax.ShapeDtypeStruct((rows, 2 * n_key), bf16),
+            jax.ShapeDtypeStruct((rows, 2 * n_key), f32),
+            jax.ShapeDtypeStruct((rows, width), bf16),
+        ],
+        scratch_shapes=[pltpu.VMEM((2 * rows, 2 * n_key), bf16), pltpu.VMEM((rows, n_query), f32)],
+        compiler_params=params(),
+        cost_estimate=cost(
+            2 * rows * n_query * (width + 10 * rows), 2 * width * (columns + 3 * rows), 2 * rows * rows * heads
+        ),
+        name="mix_back",
+    )(pos, queries, tail, own, mixed, logs, *tables, mid_grad, wide)
+
+
+def head_grads_kernel(n_key, query_grad_ref, own_grad_ref, back_ref, cos_ref, sin_ref, wide_ref,
+                      grads_ref, partial_ref, grads):
+    n_query = query_grad_ref.shape[1]
+
+    @pl.when(pl.program_id(0) == 0)
+    def _():
+        own = own_grad_ref[...] + back_ref[...].astype(f32)
+        keys = own[:, :n_key]
+        keys = keys * wide_table(cos_ref[...], n_key) - half_swap(keys) * wide_table(
+            sin_ref[...], n_key
+        )
+        grads[:, :n_query] = query_grad_ref[...]
+        grads[:, n_query : n_query + n_key] = keys.astype(bf16)
+        grads[:, n_query + n_key :] = own[:, n_key:].astype(bf16)
+        grads_ref[...] = grads[...]
+
+    partial_ref[...] = lax.dot_general(
+        grads[...], wide_ref[...], (((1,), (1,)), ((), ())), preferred_element_type=f32
+    ).astype(bf16)
+
+
+def head_grads(query_grad, own_grad, back, tables, wide, n_key):
+    rows, n_query = query_grad.shape
+    width = wide.shape[0]
+    columns = n_query + 2 * n_key
+    tile = 512
+    whole = lambda *shape: pl.BlockSpec(shape, lambda i: (0,) * len(shape))
+    return pl.pallas_call(
+        functools.partial(head_grads_kernel, n_key),
+        grid=(width // tile,),
+        in_specs=[
+            whole(rows, n_query),
+            whole(rows, 2 * n_key),
+            whole(rows, 2 * n_key),
+            whole(rows, 2 * HEAD_DIM),
+            whole(rows, 2 * HEAD_DIM),
+            pl.BlockSpec((tile, columns), lambda i: (i, 0)),
+        ],
+        out_specs=[whole(rows, columns), pl.BlockSpec((rows, tile), lambda i: (0, i))],
+        out_shape=[
+            jax.ShapeDtypeStruct((rows, columns), bf16),
+            jax.ShapeDtypeStruct((rows, width), bf16),
+        ],
+        scratch_shapes=[pltpu.VMEM((rows, columns), bf16)],
+        compiler_params=params(),
+        cost_estimate=cost(2 * rows * width * columns, 2 * width * (columns + rows)),
+        name="head_grads",
+    )(query_grad, own_grad, back, *tables, wide)
+
+
 def attention_forward(stream, gain, wide, place, *others):
-    allowed, cosine, sine, sizes = place
-    n_query, n_key = sizes
-    rows = stream.shape[0]
-    groups = n_key // HEAD_DIM
-    normed, inv_rms = norm_forward(stream, gain)
-    raw = product(normed, wide[:, : n_query + 2 * n_key])
-    queries = rotate(raw[:, :n_query].reshape(rows, -1, HEAD_DIM), cosine, sine).astype(bf16)
-    keys = rotate(
-        raw[:, n_query : n_query + n_key].reshape(rows, -1, HEAD_DIM), cosine, sine
-    ).astype(bf16)
-    values = raw[:, n_query + n_key :].astype(bf16)
-    own = jnp.concatenate([keys.reshape(rows, n_key), values], axis=1)
+    pos, tables, sizes = place
+    normed, inv_rms, queries, own = head_inputs(stream, gain, wide, tables, sizes)
     tail = from_behind(own, "ctx", 1)
-    window = jnp.concatenate([tail, own], axis=0)
-    keys_window = window[:, :n_key].reshape(2 * rows, groups, HEAD_DIM)
-    values_window = window[:, n_key:].reshape(2 * rows, groups, HEAD_DIM)
-    grouped = queries.reshape(rows, groups, HEADS // KV_HEADS, HEAD_DIM)
-    mixed_rows, log_totals = attend(grouped, keys_window, values_window, allowed)
-    mixed = mixed_rows.astype(bf16).reshape(rows, n_query)
-    partial = cols_product(mixed, wide[:, n_query + 2 * n_key :])
+    mixed, logs, partial = mix(pos, queries, tail, own, wide, sizes[1])
     total, *others = sum_tensor(partial, *others)
-    saved = (stream, inv_rms, normed, grouped, keys_window, values_window, log_totals, mixed)
+    stream = stream.astype(f32)
+    saved = (stream, inv_rms[:, 0], normed, queries, tail, own, mixed, logs)
     return stream + total, saved, *others
 
 
@@ -401,51 +700,25 @@
     return upstream + mid_part, gain_term, wide_share, down_share, *others
 
 
-def attention_backward(mid_grad, saved, gain, wide, place, *others):
-    allowed, cosine, sine, sizes = place
-    n_query, n_key = sizes
-    stream, inv_rms, normed, grouped, keys_window, values_window, log_totals, mixed = saved
-    rows = stream.shape[0]
-    mid_grad_b = mid_grad.astype(bf16)
-    mixed_grad = product(mid_grad_b, wide[:, n_query + 2 * n_key :]).astype(bf16)
-    query_grads, key_grads, value_grads = attend_back(
-        grouped,
-        keys_window,
-        values_window,
-        allowed,
-        log_totals,
-        mixed.reshape(grouped.shape),
-        mixed_grad.reshape(grouped.shape),
-    )
-    both = jnp.concatenate(
-        [key_grads.reshape(2 * rows, n_key), value_grads.reshape(2 * rows, n_key)], axis=1
-    )
-    back = from_behind(both[:rows].astype(bf16), "ctx", -1)
-    own = both[rows:] + back.astype(f32)
-    query_grad_b = rotate_back(query_grads.reshape(rows, -1, HEAD_DIM), cosine, sine)
-    key_grad_b = rotate_back(own[:, :n_key].reshape(rows, -1, HEAD_DIM), cosine, sine)
-    grads = jnp.concatenate(
-        [
-            query_grad_b.reshape(rows, n_query).astype(bf16),
-            key_grad_b.reshape(rows, n_key).astype(bf16),
-            own[:, n_key:].astype(bf16),
-        ],
-        axis=1,
-    )
-    partial = cols_product(grads, wide[:, : n_query + 2 * n_key])
+def attention_backward(mid_grad, saved, wide, place, *others):
+    pos, tables, sizes = place
+    _, _, normed, queries, tail, own, mixed, logs = saved
+    query_grad, back, own_grad, mid_grad_b = mix_back(
+        pos, queries, tail, own, mixed, logs, tables, mid_grad, wide, sizes[1]
+    )
+    back = from_behind(back, "ctx", -1)
+    grads, partial = head_grads(query_grad, own_grad, back, tables, wide, sizes[1])
     normed_grad, *others = sum_tensor(partial, *others)
-    terms = jnp.concatenate(
-        [rows_product(normed, grads).astype(bf16), rows_product(mid_grad_b, mixed).astype(bf16)],
-        axis=1,
-    )
-    count = lax.axis_size("ctx")
-    terms = terms.reshape(count, 2, -1, terms.shape[1])
+    terms = attention_terms(normed, mid_grad_b, grads, mixed, lax.axis_size("ctx"))
     core = lax.axis_index("pipe")
-    mine = lax.dynamic_index_in_dim(terms, core, 1, keepdims=False)
-    theirs = lax.dynamic_index_in_dim(terms, 1 - core, 1, keepdims=False)
-    normed_grad, summed = pin(normed_grad, add_bf16(mine, swap_cores(theirs)))
-    part, gain_term = norm_backward(stream, inv_rms, gain, normed_grad)
-    return mid_grad + part, gain_term, ring_scatter(summed).astype(bf16), *others
+    mine = lax.dynamic_index_in_dim(terms, core, 0, keepdims=False)
+    theirs = lax.dynamic_index_in_dim(terms, 1 - core, 0, keepdims=False)
+    return normed_grad, add_bf16(mine, swap_cores(theirs)), *others
+
+
+def attention_backward_out(mid_grad, normed_grad, saved, gain):
+    part, gain_term = norm_backward(saved[0], saved[1], gain, normed_grad)
+    return (mid_grad + part).astype(bf16), gain_term
 
 
 def on_device(
@@ -513,7 +786,7 @@
     attn_parts = for_sections(attn_keep, attn_got)
     wide_parts = for_sections(wide_keep, wide_got)
     down_parts = for_sections(down_keep, down_got)
-    wide_low = gather(wide_parts[0])
+    wide_low = lax.all_gather(wide_parts[0], ("pipe", "ctx"), axis=0, tiled=True)
     attn_pieces, attn_parts[1], wide_parts[1], *down_parts = pin(
         ring_gather(attn_parts[0]), attn_parts[1], wide_parts[1], *down_parts
     )
@@ -523,22 +796,18 @@
     down_high = gather(down_parts[1])
 
     pos_row = pick(positions, core)
-    cosine, sine = rope_tables(pos_row, HEAD_DIM)
-    query_index = jnp.arange(rows, dtype=jnp.int32)
-    key_index = jnp.arange(2 * rows, dtype=jnp.int32) - rows
-    distance = query_index[:, None] - key_index[None, :]
-    allowed = (distance >= 0) & (distance <= pos_row[:, None])
-    place = (allowed, cosine, sine, (n_query, n_key))
+    place = (pos_row[:, None], rope_tables(pos_row, HEAD_DIM), (n_query, n_key))
 
     stream = pick(inputs, core)
     middle, attn_saved_low, wide_low, attn_part_high = attention_forward(
-        stream.astype(f32), gains_low[0], attn_low, place, wide_low, attn_parts[1]
-    )
+        stream, gains_low[0], attn_low, place, wide_low, attn_parts[1]
+    )
+    wide_low = pick(wide_low.reshape(2, width, -1), core)
     state_low = ffn_forward_in(middle, gains_low[1], wide_low, half)
     out_low, attn_pieces = ffn_forward_out(state_low, down_low, ring_gather(attn_part_high))
     attn_high, gains_high = attn_weights(attn_pieces)
     middle, attn_saved_high, wide_high = attention_forward(
-        out_low.astype(f32), gains_high[0], attn_high, place, wide_high
+        out_low, gains_high[0], attn_high, place, wide_high
     )
     state_high = ffn_forward_in(middle, gains_high[1], wide_high, half)
 
@@ -547,10 +816,14 @@
     mid_grad, ffn_gain_high, wide_share_high, down_share_high = ffn_backward(
         own_grad.astype(f32), both_grad, state_high, gains_high[1], wide_high, down_high
     )
-    stream_grad, attn_gain_high, attn_share_high, down_share_high = attention_backward(
-        mid_grad, attn_saved_high, gains_high[0], attn_high, place, down_share_high
-    )
-    boundary_high = stream_grad.astype(bf16)
+    normed_grad, summed, down_share_high = attention_backward(
+        mid_grad, attn_saved_high, attn_high, place, down_share_high
+    )
+    normed_grad, summed = pin(normed_grad, summed)
+    attn_share_high = ring_scatter(summed).astype(bf16)
+    boundary_high, attn_gain_high = attention_backward_out(
+        mid_grad, normed_grad, attn_saved_high, gains_high[0]
+    )
     both_grad = jnp.concatenate([boundary_high, swap_cores(boundary_high)], axis=0)
     mid_grad, ffn_gain_low, wide_share_low, down_share_low, wide_share_high = ffn_backward(
         boundary_high.astype(f32),
@@ -561,12 +834,9 @@
         down_low,
         wide_share_high,
     )
-    stream_grad, attn_gain_low, attn_share_low, down_share_low, attn_share_high = (
-        attention_backward(
-            mid_grad, attn_saved_low, gains_low[0], attn_low, place, down_share_low, attn_share_high
-        )
-    )
-    boundary_low = stream_grad.astype(bf16)
+    normed_grad, summed, down_share_low, attn_share_high = attention_backward(
+        mid_grad, attn_saved_low, attn_low, place, down_share_low, attn_share_high
+    )
     (out_high,) = ffn_forward_out(state_high, down_high)
 
     def from_other(low, high):
@@ -577,13 +847,21 @@
         got_part = from_other(low, high)
         return jnp.where(first, keep_part, got_part), jnp.where(first, got_part, keep_part)
 
-    section_outputs = jnp.stack(to_owner(out_low, out_high))
-    boundary_grads = jnp.stack(to_owner(boundary_low, boundary_high))
     down_pair = (down_share_low, down_share_high)
     down_out = down_outputs(core, *down_pair, from_other(*down_pair))
+    attn_share_low = ring_scatter(summed).astype(bf16)
+    attn_full = jnp.concatenate(to_owner(attn_share_low, attn_share_high), axis=0).astype(f32)
+    normed_grad, down_out, attn_full = pin(normed_grad, down_out, attn_full)
+
+    boundary_low, attn_gain_low = attention_backward_out(
+        mid_grad, normed_grad, attn_saved_low, gains_low[0]
+    )
+    outs = (out_low, out_high)
+    section_outputs = section_stack(core, *outs, from_other(*outs))
+    boundary = (boundary_low, boundary_high)
+    boundary_grads = section_stack(core, *boundary, from_other(*boundary))
     wide_pair = (wide_share_low, wide_share_high)
     gate_out, up_out = wide_outputs(core, *wide_pair, from_other(*wide_pair))
-    attn_full = jnp.concatenate(to_owner(attn_share_low, attn_share_high), axis=0).astype(f32)
     gains_out = share_gains(
         jnp.stack(
             [jnp.stack([attn_gain_low, ffn_gain_low]), jnp.stack([attn_gain_high, ffn_gain_high])]

time: 1140 us -> 819 us (0.72)
  waiting for transfers between devices: 677 us -> 428 us
  local copies, waits for them, and re-layouts: 163 us -> 85.9 us
  Pallas kernels: 26.2 us -> 86.7 us
  matrix products: 91.9 us -> 55.3 us
    all_gather x4 -> x3, waiting for transfers between devices: 124 us -> 7.58 us  [gather(): return lax.all_gather(shard_part, 'ctx', axis=0, tiled=True)]
    reduce_scatter x2, waiting for transfers between devices: 106 us -> 11.8 us  [ffn_backward(): wide_share = lax.psum_scatter(terms, 'ctx', scatter_dimension=0, tiled=True)]
    pallas_call x0 -> x12, Pallas kernels: none -> 59 us  [the longest x2 18.3 us: mix_back(): pl.pallas_call(functools.partial(mix_back_kernel, n_key), grid=(width //...]
    reduce_scatter x2, waiting for transfers between devices: 58.6 us -> 0.01 us  [ffn_backward(): lax.psum_scatter(token_terms(upstream_both, hidden), 'ctx', scatter_dimen...]
    psum x7, waiting for transfers between devices: 219 us -> 272 us  [sum_tensor(): return (lax.psum(partial, 'tensor').astype(f32), *others)]
    dynamic_slice x5 -> x0, local copies, waits for them, and re-layouts: 49.7 us -> none  [the longest x2 27.3 us: attention_backward(): mine = lax.dynamic_index_in_dim(terms, core, 1, keepdims=False)]
    ppermute x2, waiting for transfers between devices: 31 us -> 0.01 us  [ring_scatter(): to_back = lax.ppermute(back, 'ctx', behind)]
    dot_general x16 -> x0, matrix products: 24 us -> none  [the longest x2 8.16 us: attend_back(): jnp.einsum('qkgd,skd->kgqs', grad_block, value_block, preferred_element_t...]
  transfers between devices with their start and end apart: 58 -> 58, of which waited for: 34 -> 29; matrix products, arithmetic and copies ran while one was open for 26% -> 18% of each run, Pallas kernels for 2% -> 10%
where the time goes in v3:
time: 819 us; the launch traced here: 809 us
  waiting for transfers between devices  428 us (52%)
  Pallas kernels  86.7 us (11%)
  other arithmetic  86.1 us (11%)
  local copies, waits for them, and re-layouts  85.9 us (10%)
  matrix products  55.3 us (7%)
  starting transfers between devices  35.7 us (4%)
  between operations  31.4 us (4%)
    psum x7, waiting for transfers between devices, sum_tensor(): return (lax.psum(partial, 'tensor').astype(f32), *others)  272 us
    unnamed x238, local copies, waits for them, and re-layouts  54.1 us
    ppermute x2, waiting for transfers between devices, ring_gather(): from_back = lax.ppermute(from_back, 'ctx', ahead)  35.7 us
    dot_general x4, matrix products, product(): lax.dot_general(left, right, (((1,), (0,)), ((), ())), preferred_element_...  31.6 us
    ppermute x2, waiting for transfers between devices, ring_scatter(): to_back = lax.ppermute(far[:, half:], 'ctx', behind)  28.5 us
    ppermute x4, waiting for transfers between devices, from_behind(): return lax.ppermute(block, axis, route)  25.3 us
    ppermute x20, waiting for transfers between devices, swap_cores(): return lax.ppermute(block, 'pipe', [(0, 1), (1, 0)])  25 us
    dot_general x4, matrix products, cols_product(): lax.dot_general(left, right, (((1,), (1,)), ((), ())), preferred_element_...  23.7 us
  transfers between devices with their start and end apart: 58, of which 29 were waited for; matrix products, arithmetic and copies ran while one was open for 18% of the time, Pallas kernels for 10%

profile of v3, /device:TPU:0, one launch (start us, length us, event | category | flops | bytes accessed | tf_op | source)
XLA Modules:
  0.0 809.0 jit_solution(6493581013764103089)
XLA Ops:
  51.4 22.8 %collective-permute-done.1 = bf16[272,1280]{1,0:T(8,128)(2,1)S(1)} collective-permute-done((bf16[272,1280]{1,0:T(8,128)(2,1)S(1)}, bf16[272,1280]{1,0:T(8,128)(2,1)S(1)}, u32[]{:S(2)}, u32[]{:S(2)}) %collective-permute-start.1) | collective-permute-done | bytes 696352 | tf_op jit(solution)/shard_map/ppermute | solution.py:69
  78.2 14.1 %collective-permute-done.3 = bf16[272,640]{1,0:T(8,128)(2,1)S(1)} collective-permute-done((bf16[272,640]{1,0:T(8,128)(2,1)S(1)}, bf16[272,640]{1,0:T(8,128)(2,1)S(1)}, u32[]{:S(2)}, u32[]{:S(2)}) %collective-permute-start.3) | collective-permute-done | bytes 348192 | tf_op jit(solution)/shard_map/ppermute | solution.py:73
  118.5 8.6 %mix.2 = (bf16[256,512]{1,0:T(8,128)(2,1)S(1)}, f32[256,8]{1,0:T(8,128)S(1)}, bf16[256,2048]{1,0:T(8,128)(2,1)}) custom-call(s32[256,1]{1,0:T(8,128)S(1)} %copy.101.pos_ref, bf16[256,512]{1,0:T(8,128)(2,1)S(1)} %get-tuple-element.68.query_ref, bf16[256,256]{1,0:T(8,128)(2,1)S(1)} %collective-permute-done.8.tail_ref, ...), custom_call_target="tpu_custom_call" | custom-call | flops 805306368 | bytes 6291456 | tf_op jit(solution)/shard_map/mix/pallas_call | solution.py:474
  133.8 53.9 %all-reduce.10.cloned.1.call-done = bf16[256,2048]{1,0:T(8,128)(2,1)} async-done(((bf16[256,2048]{1,0:T(8,128)(2,1)}), bf16[256,2048]{1,0:T(8,128)(2,1)}) %all-reduce.10.cloned.1.call-update) | async-done | bytes 1048592 | tf_op jit(solution)/shard_map/psum | solution.py:325
  195.2 12.9 %collective-permute-done.11 = bf16[272,1280]{1,0:T(8,128)(2,1)S(1)} collective-permute-done((bf16[272,1280]{1,0:T(8,128)(2,1)S(1)}, bf16[272,1280]{1,0:T(8,128)(2,1)S(1)}, u32[]{:S(2)}, u32[]{:S(2)}) %collective-permute-start.11) | collective-permute-done | bytes 696352 | tf_op jit(solution)/shard_map/ppermute | solution.py:69
  211.8 7.3 fusion.2
  235.4 48.8 %all-reduce.12.cloned.1.call-done = bf16[256,2048]{1,0:T(8,128)(2,1)} async-done(((bf16[256,2048]{1,0:T(8,128)(2,1)}), bf16[256,2048]{1,0:T(8,128)(2,1)}) %all-reduce.12.cloned.1.call-update) | async-done | bytes 1048592 | tf_op jit(solution)/shard_map/psum | solution.py:325
  299.7 6.3 collective-permute-done.16.tail_ref
  306.0 7.6 mix.3
  317.9 7.5 all-gather.9.cloned.1.call-done
  327.0 50.4 %all-reduce.14.cloned.1.call-done = bf16[256,2048]{1,0:T(8,128)(2,1)} async-done(((bf16[256,2048]{1,0:T(8,128)(2,1)}), bf16[256,2048]{1,0:T(8,128)(2,1)}) %all-reduce.14.cloned.1.call-update) | async-done | bytes 1048592 | tf_op jit(solution)/shard_map/psum | solution.py:325
  384.4 10.5 %fusion.60 = f32[512,2048]{1,0:T(8,128)} fusion(bf16[2048,2048]{1,0:T(8,128)(2,1)} %all-gather.9.cloned.1.call-done, bf16[256,2048]{1,0:T(8,128)(2,1)} %collective-permute-done.17, bf16[256,2048]{1,0:T(8,128)(2,1)} %multiply_convert_fusion.5), kind=kOutput, calls=%fused_computation.207 | convolution fusion | flops 4299161600 | bytes 14680064 | tf_op jit(solution)/shard_map/dot_general | solution.py:289
  394.9 8.1 multiply_convert_fusion.3
  404.0 6.9 fusion.58
  435.6 31.0 %all-reduce.16.cloned.1.call-done = bf16[256,2048]{1,0:T(8,128)(2,1)} async-done(((bf16[256,2048]{1,0:T(8,128)(2,1)}), bf16[256,2048]{1,0:T(8,128)(2,1)}) %all-reduce.16.cloned.1.call-update) | async-done | bytes 1048592 | tf_op jit(solution)/shard_map/psum | solution.py:325
  470.7 9.2 %mix_back.2 = (bf16[256,512]{1,0:T(8,128)(2,1)S(1)}, bf16[256,256]{1,0:T(8,128)(2,1)S(1)}, f32[256,256]{1,0:T(8,128)S(1)}, bf16[256,2048]{1,0:T(8,128)(2,1)S(1)}) custom-call(s32[256,1]{1,0:T(8,128)S(1)} %copy.101.pos_ref, bf16[256,512]{1,0:T(8,128)(2,1)S(1)} %copy-done.29, bf16[256,256]{1,0:T(8,128)(2,1)S(1)} %copy-done.40, ...), custom_call_target="tpu_custom_call" | custom-call | flops 1207959552 | bytes 8388608 | tf_op jit(solution)/shard_map/mix_back/pallas_call | solution.py:571
  514.1 30.8 %all-reduce.18.cloned.1.call-done = bf16[256,2048]{1,0:T(8,128)(2,1)} async-done(((bf16[256,2048]{1,0:T(8,128)(2,1)}), bf16[256,2048]{1,0:T(8,128)(2,1)}) %all-reduce.18.cloned.1.call-update) | async-done | bytes 1048592 | tf_op jit(solution)/shard_map/psum | solution.py:325
  561.5 6.9 fusion
  572.6 10.5 %reduce-scatter.7.cloned.1.call-done.high_ref = bf16[512,2048]{1,0:T(8,128)(2,1)} async-done(((bf16[2048,2048]{1,0:T(8,128)(2,1)}), bf16[512,2048]{1,0:T(8,128)(2,1)}) %reduce-scatter.7.cloned.1.call-update) | async-done | bytes 2097168 | tf_op jit(solution)/shard_map/reduce_scatter | solution.py:698
  601.5 13.4 %collective-permute-done.28 = bf16[256,640]{1,0:T(8,128)(2,1)S(1)} collective-permute-done((bf16[256,640]{1,0:T(8,128)(2,1)S(1)}, bf16[256,640]{1,0:T(8,128)(2,1)S(1)}, u32[]{:S(2)}, u32[]{:S(2)}) %collective-permute-start.28) | collective-permute-done | bytes 327712 | tf_op jit(solution)/shard_map/ppermute | solution.py:88
  639.9 9.1 %mix_back.3 = (bf16[256,512]{1,0:T(8,128)(2,1)S(1)}, bf16[256,256]{1,0:T(8,128)(2,1)S(1)}, f32[256,256]{1,0:T(8,128)S(1)}, bf16[256,2048]{1,0:T(8,128)(2,1)S(1)}) custom-call(s32[256,1]{1,0:T(8,128)S(1)} %copy.101.pos_ref, bf16[256,512]{1,0:T(8,128)(2,1)S(1)} %copy-done.24, bf16[256,256]{1,0:T(8,128)(2,1)S(1)} %copy-done.36, ...), custom_call_target="tpu_custom_call" | custom-call | flops 1207959552 | bytes 8388608 | tf_op jit(solution)/shard_map/mix_back/pallas_call | solution.py:571
  653.9 6.7 collective-permute-done.25.back_ref
  681.5 15.1 %collective-permute-done.34 = bf16[256,640]{1,0:T(8,128)(2,1)S(1)} collective-permute-done((bf16[256,640]{1,0:T(8,128)(2,1)S(1)}, bf16[256,640]{1,0:T(8,128)(2,1)S(1)}, u32[]{:S(2)}, u32[]{:S(2)}) %collective-permute-start.34) | collective-permute-done | bytes 327712 | tf_op jit(solution)/shard_map/ppermute | solution.py:88
  701.9 50.9 %all-reduce.22.cloned.1.call-done = (bf16[256,2048]{1,0:T(8,128)(2,1)}, bf16[256,2048]{1,0:T(8,128)(2,1)}) async-done(((bf16[256,2048]{1,0:T(8,128)(2,1)}, bf16[256,2048]{1,0:T(8,128)(2,1)}), (bf16[256,2048]{1,0:T(8,128)(2,1)}, bf16[256,2048]{1,0:T(8,128)(2,1)})) %all-reduce.22.cloned.1.call-update) | async-done | bytes 2097168 | tf_op jit(solution)/shard_map/psum | solution.py:325
  (495 shorter events, 327.8 us)
Async XLA Ops:
  8.0 125.0 %all-gather.5.cloned.1.call-start = ((), (), s32[]{:S(2)}) async-start(), calls=%async_computation.4 | async-start | bytes 18874368 | tf_op jit(solution)/shard_map/all_gather | solution.py:789
  21.8 165.9 %all-reduce.10.cloned.1.call-start = ((), (), s32[]{:S(2)}) async-start(), calls=%async_computation.5 | async-start | bytes 2097152 | tf_op jit(solution)/shard_map/psum | solution.py:325
  26.5 22.2 %collective-permute-start.6 = (bf16[512,1024]{1,0:T(8,128)(2,1)}, bf16[512,1024]{1,0:T(8,128)(2,1)}, u32[]{:S(2)}, u32[]{:S(2)}) collective-permute-start(bf16[512,1024]{1,0:T(8,128)(2,1)} %bitcast.210), channel_id=1, source_target_pairs={{0,16},{16,0},{1,17},{17,1},{2,18},{18,2},{3,19},{19,3},{4,20},{20... | collective-permute-start | bytes 3145736 | tf_op jit(solution)/shard_map/ppermute | solution.py:23
  45.1 29.1 %collective-permute-start.1 = (bf16[272,1280]{1,0:T(8,128)(2,1)S(1)}, bf16[272,1280]{1,0:T(8,128)(2,1)S(1)}, u32[]{:S(2)}, u32[]{:S(2)}) collective-permute-start(bf16[272,1280]{1,0:T(8,128)(2,1)S(1)} %get-tuple-element.184), channel_id=1, source_target_pairs={{0,4},{4,12},{12,8},{8,0},{1,5},{5,13},{13,9},{9,1},{2,6},{6,14},{... | collective-permute-start | bytes 2088968 | tf_op jit(solution)/shard_map/ppermute | solution.py:69
  47.7 26.6 %collective-permute-start.2 = (bf16[272,1280]{1,0:T(8,128)(2,1)S(1)}, bf16[272,1280]{1,0:T(8,128)(2,1)S(1)}, u32[]{:S(2)}, u32[]{:S(2)}) collective-permute-start(bf16[272,1280]{1,0:T(8,128)(2,1)S(1)} %get-tuple-element.184), channel_id=1, source_target_pairs={{4,0},{12,4},{8,12},{0,8},{5,1},{13,5},{9,13},{1,9},{6,2},{14,6},{... | collective-permute-start | bytes 2088968 | tf_op jit(solution)/shard_map/ppermute | solution.py:70
  133.0 88.9 %all-gather.7.cloned.1.call-start = ((), (), s32[]{:S(2)}) async-start(), calls=%async_computation.6 | async-start | bytes 5242880 | tf_op jit(solution)/shard_map/all_gather | solution.py:784
  133.6 150.6 %all-reduce.12.cloned.1.call-start = ((), (), s32[]{:S(2)}) async-start(), calls=%async_computation.7 | async-start | bytes 2097152 | tf_op jit(solution)/shard_map/psum | solution.py:325
  232.7 92.8 %all-gather.9.cloned.1.call-start = ((), (), s32[]{:S(2)}) async-start(), calls=%async_computation.8 | async-start | bytes 10485760 | tf_op jit(solution)/shard_map/all_gather | solution.py:784
  233.3 144.2 %all-reduce.14.cloned.1.call-start = ((), (), s32[]{:S(2)}) async-start(), calls=%async_computation.9 | async-start | bytes 2097152 | tf_op jit(solution)/shard_map/psum | solution.py:325
  233.3 52.9 %collective-permute-start.15 = (bf16[4,272,1280]{2,1,0:T(8,128)(2,1)}, bf16[4,272,1280]{2,1,0:T(8,128)(2,1)}, u32[]{:S(2)}, u32[]{:S(2)}) collective-permute-start(bf16[4,272,1280]{2,1,0:T(8,128)(2,1)} %bitcast_dynamic-update-slice_fusion.6), channel_id=1, source_target_pairs={{0,16},{16,0},{1,17},{17,1},{2,18},{18,2},{3,19},{19,3},{4,20},{20... | collective-permute-start | bytes 8355848 | tf_op jit(solution)/shard_map/ppermute | solution.py:23
  325.5 69.5 %all-gather.11.cloned.1.call-start = ((), (), s32[]{:S(2)}) async-start(), calls=%async_computation.10 | async-start | bytes 5242880 | tf_op jit(solution)/shard_map/all_gather | solution.py:784
  326.1 140.5 %all-reduce.16.cloned.1.call-start = ((), (), s32[]{:S(2)}) async-start(), calls=%async_computation.11 | async-start | bytes 2097152 | tf_op jit(solution)/shard_map/psum | solution.py:325
  415.2 78.5 %reduce-scatter.5.cloned.1.call-start = ((), (), s32[]{:S(2)}) async-start(), calls=%async_computation.12 | async-start | bytes 5242880 | tf_op jit(solution)/shard_map/reduce_scatter | solution.py:694
  422.0 123.0 %all-reduce.18.cloned.1.call-start = ((), (), s32[]{:S(2)}) async-start(), calls=%async_computation.13 | async-start | bytes 2097152 | tf_op jit(solution)/shard_map/psum | solution.py:325
  493.7 89.4 %reduce-scatter.7.cloned.1.call-start = ((), (), s32[]{:S(2)}) async-start(), calls=%async_computation.14 | async-start | bytes 10485760 | tf_op jit(solution)/shard_map/reduce_scatter | solution.py:698
  494.5 140.6 %all-reduce.20.cloned.1.call-start = ((), (), s32[]{:S(2)}) async-start(), calls=%async_computation.15 | async-start | bytes 2097152 | tf_op jit(solution)/shard_map/psum | solution.py:325
  583.1 82.9 %reduce-scatter.9.cloned.1.call-start = ((), (), s32[]{:S(2)}) async-start(), calls=%async_computation.16 | async-start | bytes 5242880 | tf_op jit(solution)/shard_map/reduce_scatter | solution.py:694
  589.5 163.3 %all-reduce.22.cloned.1.call-start = ((), (), s32[]{:S(2)}) async-start(), calls=%async_computation.18 | async-start | bytes 4194304 | tf_op jit(solution)/shard_map/psum | solution.py:325
  615.9 35.4 %collective-permute-start.29 = (bf16[256,1280]{1,0:T(8,128)(2,1)}, bf16[256,1280]{1,0:T(8,128)(2,1)}, u32[]{:S(2)}, u32[]{:S(2)}) collective-permute-start(bf16[256,1280]{1,0:T(8,128)(2,1)} %pad_maximum_fusion.14), channel_id=1, source_target_pairs={{4,0},{12,4},{8,12},{0,8},{5,1},{13,5},{9,13},{1,9},{6,2},{14,6},{... | collective-permute-start | bytes 1966088 | tf_op jit(solution)/shard_map/ppermute | solution.py:97
  618.3 33.0 %collective-permute-start.27 = (bf16[256,1280]{1,0:T(8,128)(2,1)}, bf16[256,1280]{1,0:T(8,128)(2,1)}, u32[]{:S(2)}, u32[]{:S(2)}) collective-permute-start(bf16[256,1280]{1,0:T(8,128)(2,1)} %pad_maximum_fusion.13), channel_id=1, source_target_pairs={{0,4},{4,12},{12,8},{8,0},{1,5},{5,13},{13,9},{9,1},{2,6},{6,14},{... | collective-permute-start | bytes 1966088 | tf_op jit(solution)/shard_map/ppermute | solution.py:96
  666.1 110.4 %reduce-scatter.11.cloned.1.call-start = ((), (), s32[]{:S(2)}) async-start(), calls=%async_computation.17 | async-start | bytes 10485760 | tf_op jit(solution)/shard_map/reduce_scatter | solution.py:698
  697.6 58.6 %collective-permute-start.35 = (bf16[256,1280]{1,0:T(8,128)(2,1)}, bf16[256,1280]{1,0:T(8,128)(2,1)}, u32[]{:S(2)}, u32[]{:S(2)}) collective-permute-start(bf16[256,1280]{1,0:T(8,128)(2,1)} %pad_maximum_fusion.16), channel_id=1, source_target_pairs={{4,0},{12,4},{8,12},{0,8},{5,1},{13,5},{9,13},{1,9},{6,2},{14,6},{... | collective-permute-start | bytes 1966088 | tf_op jit(solution)/shard_map/ppermute | solution.py:97
  700.0 56.1 %collective-permute-start.33 = (bf16[256,1280]{1,0:T(8,128)(2,1)}, bf16[256,1280]{1,0:T(8,128)(2,1)}, u32[]{:S(2)}, u32[]{:S(2)}) collective-permute-start(bf16[256,1280]{1,0:T(8,128)(2,1)} %pad_maximum_fusion.15), channel_id=1, source_target_pairs={{0,4},{4,12},{12,8},{8,0},{1,5},{5,13},{13,9},{9,1},{2,6},{6,14},{... | collective-permute-start | bytes 1966088 | tf_op jit(solution)/shard_map/ppermute | solution.py:96
  701.9 57.9 %collective-permute-start.30 = (bf16[512,1024]{1,0:T(8,128)(2,1)}, bf16[512,1024]{1,0:T(8,128)(2,1)}, u32[]{:S(2)}, u32[]{:S(2)}) collective-permute-start(bf16[512,1024]{1,0:T(8,128)(2,1)} %broadcast_select_fusion.5), channel_id=1, source_target_pairs={{0,16},{16,0},{1,17},{17,1},{2,18},{18,2},{3,19},{19,3},{4,20},{20... | collective-permute-start | bytes 3145736 | tf_op jit(solution)/shard_map/ppermute | solution.py:23
  (148 other events, 928.2 us)
Sparse Core Ops, SparseCore 0:
  21.9 110.9 all-gather.4
  135.9 51.7 all-reduce.9
  232.8 51.3 all-reduce.11
  325.6 51.7 all-reduce.13
  415.3 51.2 all-reduce.15
  493.9 51.0 all-reduce.17
  583.2 51.7 all-reduce.19
  666.2 86.6 all-reduce.21
Sparse Core Ops, SparseCore 1:
  136.0 52.5 all-gather.6
  235.7 89.7 all-gather.8
  328.5 52.5 all-gather.10
  422.0 51.9 reduce-scatter.4
  497.6 85.5 reduce-scatter.6
  589.6 72.5 reduce-scatter.8
  669.6 106.9 reduce-scatter.10

commit v4 on v3

--- a/solution.py
+++ b/solution.py
@@ -55,80 +55,115 @@
     return count, ahead, behind, device_at
 
 
-def ring_gather(block):
+def ring_gather_start(block):
+    count, ahead, behind, _ = ring_tools()
+    from_back, from_front = [block], [block]
+    for _ in range(1, count // 2):
+        from_back.append(lax.ppermute(from_back[-1], "ctx", ahead))
+        from_front.append(lax.ppermute(from_front[-1], "ctx", behind))
+    return from_back, from_front
+
+
+def ring_gather(from_back, from_front):
     count, ahead, behind, device_at = ring_tools()
+    block = from_back[0]
     half = block.shape[1] // 2
+    left = lax.ppermute(from_back[-1][:, :half], "ctx", ahead)
+    right = lax.ppermute(from_front[-1][:, half:], "ctx", behind)
     out = jnp.zeros((count,) + block.shape, block.dtype)
 
     def put(out, piece, distance, column=0):
         return lax.dynamic_update_slice(out, piece[None], (device_at(distance), 0, column))
 
     out = put(out, block, 0)
-    from_back, from_front = block, block
     for distance in range(1, count // 2):
-        from_back = lax.ppermute(from_back, "ctx", ahead)
-        from_front = lax.ppermute(from_front, "ctx", behind)
-        out = put(out, from_back, -distance)
-        out = put(out, from_front, distance)
-    left = lax.ppermute(from_back[:, :half], "ctx", ahead)
-    right = lax.ppermute(from_front[:, half:], "ctx", behind)
+        out = put(out, from_back[distance], -distance)
+        out = put(out, from_front[distance], distance)
     out = put(out, left, count // 2)
     return put(out, right, count // 2, half)
 
 
-def ring_scatter(terms):
-    count, ahead, behind, device_at = ring_tools()
+def ring_term(terms, distance):
+    return lax.dynamic_index_in_dim(terms, ring_tools()[3](distance), 0, keepdims=False)
+
+
+def ring_scatter_start(terms):
+    count, ahead, behind, _ = ring_tools()
     half = terms.shape[2] // 2
-
-    def term(distance):
-        return lax.dynamic_index_in_dim(terms, device_at(distance), 0, keepdims=False)
-
-    far = term(count // 2)
+    far = ring_term(terms, count // 2)
     to_front = lax.ppermute(far[:, :half], "ctx", ahead)
     to_back = lax.ppermute(far[:, half:], "ctx", behind)
     for distance in range(count // 2 - 1, 0, -1):
-        front, back = term(distance), term(-distance)
+        front, back = ring_term(terms, distance), ring_term(terms, -distance)
         if distance == count // 2 - 1:
             front = jnp.concatenate([add_bf16(front[:, :half], to_front), front[:, half:]], axis=1)
             back = jnp.concatenate([back[:, :half], add_bf16(back[:, half:], to_back)], axis=1)
         else:
             front, back = add_bf16(front, to_front), add_bf16(back, to_back)
-        to_front = lax.ppermute(front, "ctx", ahead)
-        to_back = lax.ppermute(back, "ctx", behind)
-    return term(0).astype(f32) + to_front.astype(f32) + to_back.astype(f32)
+        if distance > 1:
+            front = lax.ppermute(front, "ctx", ahead)
+            back = lax.ppermute(back, "ctx", behind)
+        to_front, to_back = front, back
+    return ring_term(terms, 0), to_front, to_back
+
+
+def ring_scatter(own, to_front, to_back):
+    _, ahead, behind, _ = ring_tools()
+    from_back = lax.ppermute(to_front, "ctx", ahead)
+    from_front = lax.ppermute(to_back, "ctx", behind)
+    return (own.astype(f32) + from_back.astype(f32) + from_front.astype(f32)).astype(bf16)
 
 
 def add_bf16(a, b):
     return (a.astype(f32) + b.astype(f32)).astype(bf16)
 
 
-def token_terms_kernel(left_ref, right_ref, out_ref):
-    out_ref[...] = lax.dot_general(
-        left_ref[...], right_ref[...], (((0,), (0,)), ((), ())), preferred_element_type=f32
-    ).astype(bf16)
-
-
-def token_terms(left, right):
-    tokens, width = left.shape
-    units = right.shape[1]
-    tile, column = min(width, 1024), min(units, 1024)
+def params(megabytes=24):
+    return pltpu.CompilerParams(vmem_limit_bytes=megabytes * 2**20)
+
+
+def cost(flops, bytes_accessed, transcendentals=0):
+    return pl.CostEstimate(
+        flops=flops, bytes_accessed=bytes_accessed, transcendentals=transcendentals
+    )
+
+
+def token_terms_kernel(plan, *refs):
+    out_ref = refs[-1]
+    lefts, rights = refs[: -1 - len(plan)], refs[-1 - len(plan) : -1]
+    rows = (((0,), (0,)), ((), ()))
+    column = 0
+    for left, right_ref in zip(plan, rights):
+        own, got = lefts[2 * left], lefts[2 * left + 1]
+        half, columns = own.shape[0], right_ref.shape[1]
+        total = lax.dot_general(own[...], right_ref[:half], rows, preferred_element_type=f32)
+        total += lax.dot_general(got[...], right_ref[half:], rows, preferred_element_type=f32)
+        out_ref[:, column : column + columns] = total.astype(bf16)
+        column += columns
+
+
+def token_terms(lefts, rights):
+    tokens, width = lefts[0][0].shape
+    tile = 512
+    columns = sum(right[2] for right in rights)
+    side = pl.BlockSpec((tokens, tile), lambda i: (0, i))
+
+    def right_spec(right):
+        return pl.BlockSpec((2 * tokens, right[2]), lambda i: (0, right[3]))
+
     return pl.pallas_call(
-        token_terms_kernel,
-        grid=(units // column, width // tile),
-        in_specs=[
-            pl.BlockSpec((tokens, tile), lambda j, i: (0, i)),
-            pl.BlockSpec((tokens, column), lambda j, i: (0, j)),
-        ],
-        out_specs=pl.BlockSpec((tile, column), lambda j, i: (i, j)),
-        out_shape=jax.ShapeDtypeStruct((width, units), bf16),
-        compiler_params=pltpu.CompilerParams(vmem_limit_bytes=40 * 2**20),
-        cost_estimate=pl.CostEstimate(
-            flops=2 * tokens * width * units,
-            bytes_accessed=2 * (width * units + tokens * width + tokens * units),
-            transcendentals=0,
+        functools.partial(token_terms_kernel, [right[0] for right in rights]),
+        grid=(width // tile,),
+        in_specs=[side] * (2 * len(lefts)) + [right_spec(right) for right in rights],
+        out_specs=pl.BlockSpec((tile, columns), lambda i: (i, 0)),
+        out_shape=jax.ShapeDtypeStruct((width, columns), bf16),
+        compiler_params=params(),
+        cost_estimate=cost(
+            4 * tokens * width * columns,
+            2 * (width * columns + 2 * tokens * width * len(lefts) + 2 * tokens * columns),
         ),
         name="token_terms",
-    )(left, right)
+    )(*(array for pair in lefts for array in pair), *(right[1] for right in rights))
 
 
 def attention_terms_kernel(normed_ref, mid_grad_ref, grads_ref, mixed_ref, out_ref):
@@ -158,7 +193,7 @@
         ],
         out_specs=pl.BlockSpec((2, None, tile // 2, columns), lambda i: (0, i, 0, 0)),
         out_shape=jax.ShapeDtypeStruct((2, count, tile // 2, columns), bf16),
-        compiler_params=pltpu.CompilerParams(vmem_limit_bytes=40 * 2**20),
+        compiler_params=params(),
         cost_estimate=pl.CostEstimate(
             flops=2 * tokens * width * columns,
             bytes_accessed=2 * (width * columns + 2 * tokens * width + tokens * columns),
@@ -168,99 +203,96 @@
     )(normed, mid_grad, grads, mixed)
 
 
-def section_stack_kernel(core_ref, low_ref, high_ref, got_ref, out_ref):
-    keep = jnp.where(core_ref[0] == 0, low_ref[...], high_ref[...])
-    out_ref[...] = jnp.where(core_ref[0] == pl.program_id(0), keep, got_ref[...])
-
-
-def section_stack(core, low, high, got):
-    rows, width = got.shape
+def section_stack_kernel(core_ref, low_ref, high_ref, got_low_ref, got_high_ref, out_ref):
+    first = core_ref[0] == 0
+    keep = jnp.where(first, low_ref[...], high_ref[...])
+    got = jnp.where(first, got_low_ref[...], got_high_ref[...])
+    out_ref[...] = jnp.where(core_ref[0] == pl.program_id(0), keep, got)
+
+
+def section_stack(core, low, high, got_low, got_high):
+    rows, width = low.shape
     block = pl.BlockSpec((rows, width), lambda i, core: (0, 0))
     return pl.pallas_call(
         section_stack_kernel,
         grid_spec=pltpu.PrefetchScalarGridSpec(
             num_scalar_prefetch=1,
             grid=(2,),
-            in_specs=[block, block, block],
+            in_specs=[block] * 4,
             out_specs=pl.BlockSpec((None, rows, width), lambda i, core: (i, 0, 0)),
         ),
-        out_shape=jax.ShapeDtypeStruct((2, rows, width), got.dtype),
-        compiler_params=pltpu.CompilerParams(vmem_limit_bytes=40 * 2**20),
-        cost_estimate=pl.CostEstimate(
-            flops=0, bytes_accessed=5 * rows * width * 2, transcendentals=0
+        out_shape=jax.ShapeDtypeStruct((2, rows, width), low.dtype),
+        compiler_params=params(),
+        cost_estimate=cost(0, 6 * rows * width * 2),
+        name="section_stack",
+    )(core.reshape(1), low, high, got_low, got_high)
+
+
+def wide_outputs_kernel(core_ref, *refs):
+    first = core_ref[0] == 0
+    gate_ref, up_ref = refs[8:]
+    parts = []
+    for shares in (refs[:4], refs[4:8]):
+        keep = jnp.where(first, shares[0][...], shares[1][...])
+        got = jnp.where(first, shares[2][...], shares[3][...])
+        parts.append([jnp.where(first == (side == 0), keep, got).astype(f32) for side in range(2)])
+    quarter = parts[0][0].shape[1]
+    units = parts[1][0].shape[1] - quarter
+    for side in range(2):
+        at = side * units
+        gate_ref[:, at : at + quarter] = parts[0][side]
+        gate_ref[:, at + quarter : at + units] = parts[1][side][:, :quarter]
+        up_ref[:, at : at + units] = parts[1][side][:, quarter:]
+
+
+def wide_outputs(core, early, late):
+    rows, columns = early[0].shape
+    quarter = columns // 3
+    units = 2 * quarter
+    tile = 128
+    return pl.pallas_call(
+        wide_outputs_kernel,
+        grid_spec=pltpu.PrefetchScalarGridSpec(
+            num_scalar_prefetch=1,
+            grid=(rows // tile,),
+            in_specs=[pl.BlockSpec((tile, quarter), lambda i, core: (i, 2))] * 4
+            + [pl.BlockSpec((tile, columns), lambda i, core: (i, 0))] * 4,
+            out_specs=[pl.BlockSpec((tile, 2 * units), lambda i, core: (i, 0))] * 2,
         ),
-        name="section_stack",
-    )(core.reshape(1), low, high, got)
-
-
-def wide_outputs_kernel(core_ref, low_ref, high_ref, got_ref, gate_ref, up_ref):
+        out_shape=[jax.ShapeDtypeStruct((rows, 2 * units), f32)] * 2,
+        compiler_params=params(),
+        cost_estimate=cost(0, rows * (32 * quarter + 4 * 4 * units)),
+        name="wide_outputs",
+    )(core.reshape(1), *early, *late)
+
+
+def down_outputs_kernel(core_ref, low_ref, high_ref, got_low_ref, got_high_ref, down_ref):
     first = core_ref[0] == 0
-    units = got_ref.shape[1] // 2
+    units = low_ref.shape[1]
     keep = jnp.where(first, low_ref[...], high_ref[...])
-    got = got_ref[...]
-    for side in range(2):
-        part = jnp.where(first == (side == 0), keep, got).astype(f32)
-        gate_ref[:, side * units : (side + 1) * units] = part[:, :units]
-        up_ref[:, side * units : (side + 1) * units] = part[:, units:]
-
-
-def down_outputs_kernel(core_ref, low_ref, high_ref, got_ref, down_ref):
-    first = core_ref[0] == 0
-    units = got_ref.shape[1]
-    keep = jnp.where(first, low_ref[...], high_ref[...])
-    got = got_ref[...]
+    got = jnp.where(first, got_low_ref[...], got_high_ref[...])
     for side in range(2):
         part = jnp.where(first == (side == 0), keep, got).astype(f32)
         down_ref[side * units : (side + 1) * units, :] = part.T
 
 
-def section_outputs_call(kernel, core, low, high, got, specs, shapes, name):
-    rows, wide = got.shape
+def down_outputs(core, early):
+    rows, columns = early[0].shape
+    units = 2 * columns // 3
     tile = 128
-    block = pl.BlockSpec((tile, wide), lambda i, core: (i, 0))
     return pl.pallas_call(
-        kernel,
+        down_outputs_kernel,
         grid_spec=pltpu.PrefetchScalarGridSpec(
             num_scalar_prefetch=1,
             grid=(rows // tile,),
-            in_specs=[block, block, block],
-            out_specs=specs(tile),
+            in_specs=[pl.BlockSpec((tile, units), lambda i, core: (i, 0))] * 4,
+            out_specs=pl.BlockSpec((2 * units, tile), lambda i, core: (0, i)),
         ),
-        out_shape=shapes,
-        compiler_params=pltpu.CompilerParams(vmem_limit_bytes=40 * 2**20),
-        cost_estimate=pl.CostEstimate(
-            flops=0, bytes_accessed=3 * rows * wide * 2 + 2 * rows * wide * 4, transcendentals=0
-        ),
-        name=name,
-    )(core.reshape(1), low, high, got)
-
-
-def wide_outputs(core, low, high, got):
-    rows, units = got.shape[0], got.shape[1] // 2
-    return section_outputs_call(
-        wide_outputs_kernel,
-        core,
-        low,
-        high,
-        got,
-        lambda tile: [pl.BlockSpec((tile, 2 * units), lambda i, core: (i, 0))] * 2,
-        [jax.ShapeDtypeStruct((rows, 2 * units), f32)] * 2,
-        "wide_outputs",
-    )
-
-
-def down_outputs(core, low, high, got):
-    rows, units = got.shape
-    return section_outputs_call(
-        down_outputs_kernel,
-        core,
-        low,
-        high,
-        got,
-        lambda tile: pl.BlockSpec((2 * units, tile), lambda i, core: (0, i)),
-        jax.ShapeDtypeStruct((2 * units, rows), f32),
-        "down_outputs",
-    )
+        out_shape=jax.ShapeDtypeStruct((2 * units, rows), f32),
+        compiler_params=params(),
+        cost_estimate=cost(0, rows * units * 16),
+        name="down_outputs",
+    )(core.reshape(1), *early)
 
 
 def pin(value, *others):
@@ -322,7 +354,7 @@
     partial = partial.astype(bf16)
     if others:
         partial, *others = pin(partial, *others)
-    return lax.psum(partial, "tensor").astype(f32), *others
+    return lax.psum(partial, "tensor"), *others
 
 
 def own_share(partial, rows):
@@ -373,16 +405,6 @@
     query_ref[...] = turned[:, :n_query].astype(bf16)
     own_ref[:, :n_key] = turned[:, n_query:].astype(bf16)
     own_ref[:, n_key:] = raw[:, n_query + n_key :].astype(bf16)
-
-
-def params(megabytes=48):
-    return pltpu.CompilerParams(vmem_limit_bytes=megabytes * 2**20)
-
-
-def cost(flops, bytes_accessed, transcendentals=0):
-    return pl.CostEstimate(
-        flops=flops, bytes_accessed=bytes_accessed, transcendentals=transcendentals
-    )
 
 
 def head_inputs(stream, gain, wide, tables, sizes):
@@ -660,44 +682,45 @@
     tail = from_behind(own, "ctx", 1)
     mixed, logs, partial = mix(pos, queries, tail, own, wide, sizes[1])
     total, *others = sum_tensor(partial, *others)
-    stream = stream.astype(f32)
-    saved = (stream, inv_rms[:, 0], normed, queries, tail, own, mixed, logs)
-    return stream + total, saved, *others
+    return total, (stream.astype(f32), inv_rms[:, 0], normed, queries, tail, own, mixed, logs), *others
 
 
 def ffn_forward_in(middle, gain, wide, hidden_width):
     normed, inv_rms = norm_forward(middle, gain)
-    both = jnp.concatenate([normed, swap_cores(normed)], axis=0)
-    gate_up = product(both, wide)
+    got = swap_cores(normed)
+    gate_up = product(jnp.concatenate([normed, got], axis=0), wide)
     gate = gate_up[:, :hidden_width]
     up = gate_up[:, hidden_width:]
     hidden = (jax.nn.silu(gate) * up).astype(bf16)
-    return (middle, inv_rms, both, gate, up, hidden)
-
-
-def ffn_forward_out(state, down, *others):
+    return (middle, inv_rms, normed, got, gate, up, hidden)
+
+
+def ffn_share(state, down):
     middle, hidden = state[0], state[-1]
-    partial = own_share(cols_product(hidden, down), middle.shape[0])
-    total, *others = sum_tensor(partial, *others)
-    return (middle + total).astype(bf16), *others
-
-
-def ffn_backward(upstream, upstream_both, state, gain, wide, down, *others):
-    middle, inv_rms, both, gate, up, hidden = state
-    hidden_grad = product(upstream_both, down)
+    return own_share(cols_product(hidden, down), middle.shape[0]).astype(bf16)
+
+
+def ffn_backward(own_grad, other_grad, state, wide, down, *others):
+    middle, _, normed, got, gate, up, hidden = state
+    hidden_grad = product(jnp.concatenate([own_grad, other_grad], axis=0), down)
     sigmoid_gate = jax.nn.sigmoid(gate)
     gate_grad = (hidden_grad * up * sigmoid_gate * (1.0 + gate * (1.0 - sigmoid_gate))).astype(bf16)
     up_grad = (hidden_grad * gate * sigmoid_gate).astype(bf16)
-    grads = jnp.concatenate([gate_grad, up_grad], axis=1)
-    partial = own_share(cols_product(grads, wide), middle.shape[0])
-    normed_grad, *others = sum_tensor(partial, *others)
-    down_share = lax.psum_scatter(
-        token_terms(upstream_both, hidden), "ctx", scatter_dimension=0, tiled=True
-    )
-    normed_grad, terms = pin(normed_grad, token_terms(both, grads))
-    wide_share = lax.psum_scatter(terms, "ctx", scatter_dimension=0, tiled=True)
-    mid_part, gain_term = norm_backward(middle, inv_rms, gain, normed_grad)
-    return upstream + mid_part, gain_term, wide_share, down_share, *others
+    units = gate.shape[1]
+    partial = cols_product(jnp.concatenate([gate_grad, up_grad], axis=1), wide)
+    normed_grad, *others = sum_tensor(own_share(partial, middle.shape[0]), *others)
+    own_sides, norm_sides = (own_grad, other_grad), (normed, got)
+    early = token_terms(
+        [own_sides, norm_sides], [(0, hidden, units, 0), (1, gate_grad, units // 2, 0)]
+    )
+    early = lax.psum_scatter(early, "ctx", scatter_dimension=0, tiled=True)
+    late = token_terms([norm_sides], [(0, gate_grad, units // 2, 1), (0, up_grad, units, 0)])
+    return normed_grad, early, late, *others
+
+
+def ffn_backward_out(upstream, normed_grad, state, gain):
+    mid_part, gain_term = norm_backward(state[0], state[1], gain, normed_grad.astype(f32))
+    return upstream.astype(f32) + mid_part, gain_term
 
 
 def attention_backward(mid_grad, saved, wide, place, *others):
@@ -717,7 +740,7 @@
 
 
 def attention_backward_out(mid_grad, normed_grad, saved, gain):
-    part, gain_term = norm_backward(saved[0], saved[1], gain, normed_grad)
+    part, gain_term = norm_backward(saved[0], saved[1], gain, normed_grad.astype(f32))
     return (mid_grad + part).astype(bf16), gain_term
 
 
@@ -788,7 +811,7 @@
     down_parts = for_sections(down_keep, down_got)
     wide_low = lax.all_gather(wide_parts[0], ("pipe", "ctx"), axis=0, tiled=True)
     attn_pieces, attn_parts[1], wide_parts[1], *down_parts = pin(
-        ring_gather(attn_parts[0]), attn_parts[1], wide_parts[1], *down_parts
+        ring_gather(*ring_gather_start(attn_parts[0])), attn_parts[1], wide_parts[1], *down_parts
     )
     attn_low, gains_low = attn_weights(attn_pieces)
     down_low = gather(down_parts[0])
@@ -798,85 +821,110 @@
     pos_row = pick(positions, core)
     place = (pos_row[:, None], rope_tables(pos_row, HEAD_DIM), (n_query, n_key))
 
+    def scatter(terms):
+        return lax.psum_scatter(terms, "ctx", scatter_dimension=0, tiled=True)
+
+    def give_low(share):
+        return lax.ppermute(share, "pipe", [(1, 0)])
+
+    def give_high(share):
+        return lax.ppermute(share, "pipe", [(0, 1)])
+
     stream = pick(inputs, core)
-    middle, attn_saved_low, wide_low, attn_part_high = attention_forward(
+    total, attn_saved_low, wide_low, attn_part_high = attention_forward(
         stream, gains_low[0], attn_low, place, wide_low, attn_parts[1]
     )
     wide_low = pick(wide_low.reshape(2, width, -1), core)
+    total, wide_low, attn_ring = pin(total, wide_low, ring_gather_start(attn_part_high))
+    middle = attn_saved_low[0] + total.astype(f32)
     state_low = ffn_forward_in(middle, gains_low[1], wide_low, half)
-    out_low, attn_pieces = ffn_forward_out(state_low, down_low, ring_gather(attn_part_high))
-    attn_high, gains_high = attn_weights(attn_pieces)
-    middle, attn_saved_high, wide_high = attention_forward(
+    own_grad, other_grad = pick(out_grad, core), pick(out_grad, 1 - core)
+    (total,) = sum_tensor(ffn_share(state_low, down_low))
+    total, own_grad, other_grad, (attn_high, gains_high) = pin(
+        total, own_grad, other_grad, attn_weights(ring_gather(*attn_ring))
+    )
+    out_low = (middle + total.astype(f32)).astype(bf16)
+    total, attn_saved_high, wide_high = attention_forward(
         out_low, gains_high[0], attn_high, place, wide_high
     )
+    total, got_out_low = pin(total, swap_cores(out_low))
+    middle = attn_saved_high[0] + total.astype(f32)
     state_high = ffn_forward_in(middle, gains_high[1], wide_high, half)
 
-    own_grad = pick(out_grad, core)
-    both_grad = jnp.concatenate([own_grad, pick(out_grad, 1 - core)], axis=0)
-    mid_grad, ffn_gain_high, wide_share_high, down_share_high = ffn_backward(
-        own_grad.astype(f32), both_grad, state_high, gains_high[1], wide_high, down_high
-    )
-    normed_grad, summed, down_share_high = attention_backward(
-        mid_grad, attn_saved_high, attn_high, place, down_share_high
-    )
-    normed_grad, summed = pin(normed_grad, summed)
-    attn_share_high = ring_scatter(summed).astype(bf16)
+    normed_grad, early_high, late_high = ffn_backward(
+        own_grad, other_grad, state_high, wide_high, down_high
+    )
+    normed_grad, late_high = pin(normed_grad, late_high)
+    mid_grad, ffn_gain_high = ffn_backward_out(own_grad, normed_grad, state_high, gains_high[1])
+    late_high = scatter(late_high)
+    normed_grad, summed, early_high = attention_backward(
+        mid_grad, attn_saved_high, attn_high, place, early_high
+    )
+    normed_grad, attn_ring, out_share = pin(
+        normed_grad, ring_scatter_start(summed), ffn_share(state_high, down_high)
+    )
     boundary_high, attn_gain_high = attention_backward_out(
         mid_grad, normed_grad, attn_saved_high, gains_high[0]
     )
-    both_grad = jnp.concatenate([boundary_high, swap_cores(boundary_high)], axis=0)
-    mid_grad, ffn_gain_low, wide_share_low, down_share_low, wide_share_high = ffn_backward(
-        boundary_high.astype(f32),
-        both_grad,
-        state_low,
-        gains_low[1],
-        wide_low,
-        down_low,
-        wide_share_high,
-    )
-    normed_grad, summed, down_share_low, attn_share_high = attention_backward(
-        mid_grad, attn_saved_low, attn_low, place, down_share_low, attn_share_high
-    )
-    (out_high,) = ffn_forward_out(state_high, down_high)
-
-    def from_other(low, high):
-        return swap_cores(jnp.where(first, high, low))
+    got_boundary_high = swap_cores(boundary_high)
+    normed_grad, early_low, late_low, late_high = ffn_backward(
+        boundary_high, got_boundary_high, state_low, wide_low, down_low, late_high
+    )
+    normed_grad, late_low, attn_share_high = pin(normed_grad, late_low, ring_scatter(*attn_ring))
+    mid_grad, ffn_gain_low = ffn_backward_out(
+        boundary_high, normed_grad, state_low, gains_low[1]
+    )
+    late_low = scatter(late_low)
+    normed_grad, summed, early_low = attention_backward(
+        mid_grad, attn_saved_low, attn_low, place, early_low
+    )
+    (total,) = sum_tensor(out_share)
 
     def to_owner(low, high):
         keep_part = jnp.where(first, low, high)
-        got_part = from_other(low, high)
+        got_part = swap_cores(jnp.where(first, high, low))
         return jnp.where(first, keep_part, got_part), jnp.where(first, got_part, keep_part)
 
-    down_pair = (down_share_low, down_share_high)
-    down_out = down_outputs(core, *down_pair, from_other(*down_pair))
-    attn_share_low = ring_scatter(summed).astype(bf16)
+    early = (early_low, early_high, give_low(early_low), give_high(early_high))
+    down_out = down_outputs(core, early)
+    attn_share_low = ring_scatter(*ring_scatter_start(summed))
     attn_full = jnp.concatenate(to_owner(attn_share_low, attn_share_high), axis=0).astype(f32)
-    normed_grad, down_out, attn_full = pin(normed_grad, down_out, attn_full)
+    key_at = n_query + n_key
+    value_at = key_at + n_key
+    attn_outs = (
+        attn_full[:, :n_query],
+        attn_full[:, n_query:key_at],
+        attn_full[:, key_at:value_at],
+        attn_full[:, value_at:].T,
+    )
+    normed_grad, down_out, attn_outs, got_late_high = pin(
+        normed_grad, down_out, attn_outs, give_high(late_high)
+    )
+    out_high = (middle + total.astype(f32)).astype(bf16)
+    section_outputs = section_stack(core, out_low, out_high, got_out_low, swap_cores(out_high))
 
     boundary_low, attn_gain_low = attention_backward_out(
         mid_grad, normed_grad, attn_saved_low, gains_low[0]
     )
-    outs = (out_low, out_high)
-    section_outputs = section_stack(core, *outs, from_other(*outs))
-    boundary = (boundary_low, boundary_high)
-    boundary_grads = section_stack(core, *boundary, from_other(*boundary))
-    wide_pair = (wide_share_low, wide_share_high)
-    gate_out, up_out = wide_outputs(core, *wide_pair, from_other(*wide_pair))
+    boundary_grads = section_stack(
+        core, boundary_low, boundary_high, swap_cores(boundary_low), got_boundary_high
+    )
+    late = (late_low, late_high, give_low(late_low), got_late_high)
+    gate_out, up_out = wide_outputs(core, early, late)
     gains_out = share_gains(
         jnp.stack(
             [jnp.stack([attn_gain_low, ffn_gain_low]), jnp.stack([attn_gain_high, ffn_gain_high])]
         )
     )
-    key_at = n_query + n_key
-    value_at = key_at + n_key
+    query_out, key_out, value_out, attn_out = attn_outs
     return (
         section_outputs[None],
         boundary_grads[None],
         gains_out[:1],
-        attn_full[:, :n_query][None],
-        attn_full[:, n_query:key_at][None],
-        attn_full[:, key_at:value_at][None],
-        attn_full[:, value_at:].T[None],
+        query_out[None],
+        key_out[None],
+        value_out[None],
+        attn_out[None],
         gains_out[1:],
         gate_out[None],
         up_out[None],

time: 819 us -> 795 us (0.971)
  waiting for transfers between devices: 428 us -> 382 us
  local copies, waits for them, and re-layouts: 85.9 us -> 117 us
  other arithmetic: 86.1 us -> 70.8 us
  Pallas kernels: 86.7 us -> 71.9 us
  starting transfers between devices: 35.7 us -> 49.5 us
  between operations: 31.4 us -> 41.1 us
    psum x7, waiting for transfers between devices: 272 us -> 136 us  [sum_tensor(): return (lax.psum(partial, 'tensor'), *others)]
    ppermute x16 -> x20, waiting for transfers between devices: 78.7 us -> 139 us  [the longest x2 52.5 us: ring_scatter(): from_front = lax.ppermute(to_back, 'ctx', behind)]
    unnamed x238 -> x261, local copies, waits for them, and re-layouts: 54.1 us -> 76.9 us
    ppermute x16 -> x20, starting transfers between devices: 17.6 us -> 29.9 us  [the longest x2 9.11 us: give_high(): return lax.ppermute(share, 'pipe', [(0, 1)])]
    select_n x5 -> x1, other arithmetic: 12.6 us -> 1.4 us  [to_owner(): got_part = swap_cores(jnp.where(first, high, low))]
    ppermute x20 -> x19, waiting for transfers between devices: 25 us -> 34.9 us  [swap_cores(): return lax.ppermute(block, 'pipe', [(0, 1), (1, 0)])]
    concatenate x10 -> x4, other arithmetic: 10.9 us -> 1.9 us  [the longest x2 0.95 us: ring_scatter_start(): jnp.concatenate([add_bf16(front[:, :half], to_front), front[:, half:]], a...]
  transfers between devices with their start and end apart: 58 -> 61, of which waited for: 29 -> 42; matrix products, arithmetic and copies ran while one was open for 18% -> 17% of each run, Pallas kernels for 10% -> 8%
where the time goes in v4:
time: 795 us; the launch traced here: 784 us
  waiting for transfers between devices  382 us (48%)
  local copies, waits for them, and re-layouts  117 us (15%)
  Pallas kernels  71.9 us (9%)
  other arithmetic  70.8 us (9%)
  matrix products  52.6 us (7%)
  starting transfers between devices  49.5 us (6%)
  between operations  41.1 us (5%)
    psum x7, waiting for transfers between devices, sum_tensor(): return (lax.psum(partial, 'tensor'), *others)  136 us
    unnamed x261, local copies, waits for them, and re-layouts  76.9 us
    ppermute x2, waiting for transfers between devices, ring_scatter(): from_front = lax.ppermute(to_back, 'ctx', behind)  52.5 us
    ppermute x19, waiting for transfers between devices, swap_cores(): return lax.ppermute(block, 'pipe', [(0, 1), (1, 0)])  34.9 us
    ppermute x2, waiting for transfers between devices, ring_gather_start(): from_back.append(lax.ppermute(from_back[-1], 'ctx', ahead))  33.5 us
    dot_general x4, matrix products, product(): lax.dot_general(left, right, (((1,), (0,)), ((), ())), preferred_element_...  30.3 us
    ppermute x4, waiting for transfers between devices, from_behind(): return lax.ppermute(block, axis, route)  30.2 us
    dot_general x4, matrix products, cols_product(): lax.dot_general(left, right, (((1,), (1,)), ((), ())), preferred_element_...  22.3 us
  transfers between devices with their start and end apart: 61, of which 42 were waited for; matrix products, arithmetic and copies ran while one was open for 17% of the time, Pallas kernels for 8%

profile of v4, /device:TPU:0, one launch (start us, length us, event | category | flops | bytes accessed | tf_op | source)
XLA Modules:
  0.0 784.2 jit_solution(9331194202703600024)
XLA Ops:
  53.1 22.0 %collective-permute-done.1 = bf16[272,1280]{1,0:T(8,128)(2,1)S(1)} collective-permute-done((bf16[272,1280]{1,0:T(8,128)(2,1)S(1)}, bf16[272,1280]{1,0:T(8,128)(2,1)S(1)}, u32[]{:S(2)}, u32[]{:S(2)}) %collective-permute-start.1) | collective-permute-done | bytes 696352 | tf_op jit(solution)/shard_map/ppermute | solution.py:62
  79.2 14.2 %collective-permute-done.3 = bf16[272,640]{1,0:T(8,128)(2,1)S(1)} collective-permute-done((bf16[272,640]{1,0:T(8,128)(2,1)S(1)}, bf16[272,640]{1,0:T(8,128)(2,1)S(1)}, u32[]{:S(2)}, u32[]{:S(2)}) %collective-permute-start.3) | collective-permute-done | bytes 348192 | tf_op jit(solution)/shard_map/ppermute | solution.py:71
  110.9 6.2 collective-permute-done.8.tail_ref
  133.6 8.8 %dynamic-slice_bitcast_fusion = bf16[2048,2048]{1,0:T(8,128)(2,1)} fusion(bf16[2,2048,2048]{2,1,0:T(8,128)(2,1)} %bitcast.208, s32[]{:T(128)S(6)} %select_n.236), kind=kLoop, calls=%fused_computation | loop fusion | bytes 16777220 | tf_op jit(solution)/shard_map/jit(dynamic_index_in_dim)/squeeze | solution.py:771
  142.5 11.5 %collective-permute-done.9 = bf16[272,1280]{1,0:T(8,128)(2,1)S(1)} collective-permute-done((bf16[272,1280]{1,0:T(8,128)(2,1)S(1)}, bf16[272,1280]{1,0:T(8,128)(2,1)S(1)}, u32[]{:S(2)}, u32[]{:S(2)}) %collective-permute-start.9) | collective-permute-done | bytes 696352 | tf_op jit(solution)/shard_map/ppermute | solution.py:62
  155.3 30.6 %all-reduce.10.cloned.1.call-done = bf16[256,2048]{1,0:T(8,128)(2,1)} async-done(((bf16[256,2048]{1,0:T(8,128)(2,1)}), bf16[256,2048]{1,0:T(8,128)(2,1)}) %all-reduce.10.cloned.1.call-update) | async-done | bytes 1048592 | tf_op jit(solution)/shard_map/psum | solution.py:357
  190.9 7.3 fusion.34
  236.9 25.4 %all-reduce.12.cloned.1.call-done = bf16[256,2048]{1,0:T(8,128)(2,1)} async-done(((bf16[256,2048]{1,0:T(8,128)(2,1)}), bf16[256,2048]{1,0:T(8,128)(2,1)}) %all-reduce.12.cloned.1.call-update) | async-done | bytes 1048592 | tf_op jit(solution)/shard_map/psum | solution.py:357
  290.0 13.6 %all-gather.9.cloned.1.call-done = bf16[2048,2048]{1,0:T(8,128)(2,1)} async-done(((bf16[512,2048]{1,0:T(8,128)(2,1)}), bf16[2048,2048]{1,0:T(8,128)(2,1)}) %all-gather.9.cloned.1.call-update) | async-done | bytes 8388624 | tf_op jit(solution)/shard_map/all_gather | solution.py:807
  308.0 47.6 %all-reduce.14.cloned.1.call-done = bf16[256,2048]{1,0:T(8,128)(2,1)} async-done(((bf16[256,2048]{1,0:T(8,128)(2,1)}), bf16[256,2048]{1,0:T(8,128)(2,1)}) %all-reduce.14.cloned.1.call-update) | async-done | bytes 1048592 | tf_op jit(solution)/shard_map/psum | solution.py:357
  361.2 10.1 %fusion.42 = f32[512,2048]{1,0:T(8,128)} fusion(bf16[2048,2048]{1,0:T(8,128)(2,1)} %all-gather.9.cloned.1.call-done, bf16[256,2048]{1,0:T(8,128)(2,1)S(1)} %collective-permute-done.18.refs_1_.refs_3_, bf16[256,2048]{1,0:T(8,128)(2,1)S(1)} %multiply_convert_fusion.5.refs_0_.refs_2_), kind=kOutput, calls=%fused_computation.77 | convolution fusion | flops 4299161600 | bytes 14680064 | tf_op jit(solution)/shard_map/dot_general | solution.py:321
  373.2 7.3 multiply_convert_fusion.4
  380.5 7.7 fusion.46
  415.6 28.2 %all-reduce.16.cloned.1.call-done = bf16[256,2048]{1,0:T(8,128)(2,1)} async-done(((bf16[256,2048]{1,0:T(8,128)(2,1)}), bf16[256,2048]{1,0:T(8,128)(2,1)}) %all-reduce.16.cloned.1.call-update) | async-done | bytes 1048592 | tf_op jit(solution)/shard_map/psum | solution.py:357
  451.8 6.5 mix_back.2
  460.6 9.4 %collective-permute-done.20.back_ref = bf16[256,256]{1,0:T(8,128)(2,1)S(1)} collective-permute-done((bf16[256,256]{1,0:T(8,128)(2,1)S(1)}, bf16[256,256]{1,0:T(8,128)(2,1)S(1)}, u32[]{:S(2)}, u32[]{:S(2)}) %collective-permute-start.20) | collective-permute-done | bytes 131104 | tf_op jit(solution)/shard_map/ppermute | solution.py:29
  508.3 13.7 %collective-permute-done.22 = bf16[256,640]{1,0:T(8,128)(2,1)S(1)} collective-permute-done((bf16[256,640]{1,0:T(8,128)(2,1)S(1)}, bf16[256,640]{1,0:T(8,128)(2,1)S(1)}, u32[]{:S(2)}, u32[]{:S(2)}) %collective-permute-start.22) | collective-permute-done | bytes 327712 | tf_op jit(solution)/shard_map/ppermute | solution.py:94
  572.5 23.6 %collective-permute-done.29 = bf16[256,1280]{1,0:T(8,128)(2,1)S(1)} collective-permute-done((bf16[256,1280]{1,0:T(8,128)(2,1)}, bf16[256,1280]{1,0:T(8,128)(2,1)S(1)}, u32[]{:S(2)}, u32[]{:S(2)}) %collective-permute-start.29) | collective-permute-done | bytes 655392 | tf_op jit(solution)/shard_map/ppermute | solution.py:113
  618.6 6.5 mix_back.3
  627.4 8.4 %collective-permute-done.30.back_ref = bf16[256,256]{1,0:T(8,128)(2,1)S(1)} collective-permute-done((bf16[256,256]{1,0:T(8,128)(2,1)S(1)}, bf16[256,256]{1,0:T(8,128)(2,1)S(1)}, u32[]{:S(2)}, u32[]{:S(2)}) %collective-permute-start.30) | collective-permute-done | bytes 131104 | tf_op jit(solution)/shard_map/ppermute | solution.py:29
  639.6 11.8 %reduce-scatter.9.cloned.1.call-done.low_ref.refs_0_ = bf16[512,1536]{1,0:T(8,128)(2,1)} async-done(((bf16[2048,1536]{1,0:T(8,128)(2,1)}), bf16[512,1536]{1,0:T(8,128)(2,1)}) %reduce-scatter.9.cloned.1.call-update) | async-done | bytes 1572880 | tf_op jit(solution)/shard_map/reduce_scatter | solution.py:716
  667.0 15.2 %collective-permute-done.36 = bf16[256,640]{1,0:T(8,128)(2,1)S(1)} collective-permute-done((bf16[256,640]{1,0:T(8,128)(2,1)S(1)}, bf16[256,640]{1,0:T(8,128)(2,1)S(1)}, u32[]{:S(2)}, u32[]{:S(2)}) %collective-permute-start.36) | collective-permute-done | bytes 327712 | tf_op jit(solution)/shard_map/ppermute | solution.py:95
  684.7 28.9 %collective-permute-done.37 = bf16[256,1280]{1,0:T(8,128)(2,1)S(1)} collective-permute-done((bf16[256,1280]{1,0:T(8,128)(2,1)S(1)}, bf16[256,1280]{1,0:T(8,128)(2,1)S(1)}, u32[]{:S(2)}, u32[]{:S(2)}) %collective-permute-start.37) | collective-permute-done | bytes 655392 | tf_op jit(solution)/shard_map/ppermute | solution.py:113
  770.1 6.2 wide_outputs.1
  (514 shorter events, 372.5 us)
Async XLA Ops:
  8.0 122.7 %all-gather.5.cloned.1.call-start = ((), (), s32[]{:S(2)}) async-start(), calls=%async_computation.4 | async-start | bytes 18874368 | tf_op jit(solution)/shard_map/all_gather | solution.py:812
  21.8 164.1 %all-reduce.10.cloned.1.call-start = ((), (), s32[]{:S(2)}) async-start(), calls=%async_computation.5 | async-start | bytes 2097152 | tf_op jit(solution)/shard_map/psum | solution.py:357
  25.8 25.7 %collective-permute-start.6 = (bf16[512,1024]{0,1:T(8,128)(2,1)}, bf16[512,1024]{0,1:T(8,128)(2,1)S(1)}, u32[]{:S(2)}, u32[]{:S(2)}) collective-permute-start(bf16[512,1024]{0,1:T(8,128)(2,1)} %dynamic-slice_bitcast_fusion.5), channel_id=1, source_target_pairs={{0,16},{16,0},{1,17},{17,1},{2,18},{18,2},{3,19},{19,3},{4,20},{20... | collective-permute-start | bytes 3145736 | tf_op jit(solution)/shard_map/ppermute | solution.py:23
  47.7 27.4 %collective-permute-start.1 = (bf16[272,1280]{1,0:T(8,128)(2,1)S(1)}, bf16[272,1280]{1,0:T(8,128)(2,1)S(1)}, u32[]{:S(2)}, u32[]{:S(2)}) collective-permute-start(bf16[272,1280]{1,0:T(8,128)(2,1)S(1)} %get-tuple-element.214), channel_id=1, source_target_pairs={{0,4},{4,12},{12,8},{8,0},{1,5},{5,13},{13,9},{9,1},{2,6},{6,14},{... | collective-permute-start | bytes 2088968 | tf_op jit(solution)/shard_map/ppermute | solution.py:62
  50.4 24.9 %collective-permute-start.2 = (bf16[272,1280]{1,0:T(8,128)(2,1)S(1)}, bf16[272,1280]{1,0:T(8,128)(2,1)S(1)}, u32[]{:S(2)}, u32[]{:S(2)}) collective-permute-start(bf16[272,1280]{1,0:T(8,128)(2,1)S(1)} %get-tuple-element.214), channel_id=1, source_target_pairs={{4,0},{12,4},{8,12},{0,8},{5,1},{13,5},{9,13},{1,9},{6,2},{14,6},{... | collective-permute-start | bytes 2088968 | tf_op jit(solution)/shard_map/ppermute | solution.py:63
  130.8 71.1 %all-gather.7.cloned.1.call-start = ((), (), s32[]{:S(2)}) async-start(), calls=%async_computation.6 | async-start | bytes 5242880 | tf_op jit(solution)/shard_map/all_gather | solution.py:807
  131.3 131.0 %all-reduce.12.cloned.1.call-start = ((), (), s32[]{:S(2)}) async-start(), calls=%async_computation.7 | async-start | bytes 2097152 | tf_op jit(solution)/shard_map/psum | solution.py:357
  210.9 92.7 %all-gather.9.cloned.1.call-start = ((), (), s32[]{:S(2)}) async-start(), calls=%async_computation.8 | async-start | bytes 10485760 | tf_op jit(solution)/shard_map/all_gather | solution.py:807
  211.5 144.1 %all-reduce.14.cloned.1.call-start = ((), (), s32[]{:S(2)}) async-start(), calls=%async_computation.9 | async-start | bytes 2097152 | tf_op jit(solution)/shard_map/psum | solution.py:357
  303.7 69.5 %all-gather.11.cloned.1.call-start = ((), (), s32[]{:S(2)}) async-start(), calls=%async_computation.10 | async-start | bytes 5242880 | tf_op jit(solution)/shard_map/all_gather | solution.py:807
  304.2 139.5 %all-reduce.16.cloned.1.call-start = ((), (), s32[]{:S(2)}) async-start(), calls=%async_computation.11 | async-start | bytes 2097152 | tf_op jit(solution)/shard_map/psum | solution.py:357
  392.4 84.4 %reduce-scatter.5.cloned.1.call-start = ((), (), s32[]{:S(2)}) async-start(), calls=%async_computation.12 | async-start | bytes 7864320 | tf_op jit(solution)/shard_map/reduce_scatter | solution.py:716
  404.6 124.2 %all-reduce.18.cloned.1.call-start = ((), (), s32[]{:S(2)}) async-start(), calls=%async_computation.13 | async-start | bytes 2097152 | tf_op jit(solution)/shard_map/psum | solution.py:357
  476.8 81.2 %reduce-scatter.7.cloned.1.call-start = ((), (), s32[]{:S(2)}) async-start(), calls=%async_computation.14 | async-start | bytes 7864320 | tf_op jit(solution)/shard_map/reduce_scatter | solution.py:825
  477.6 133.0 %all-reduce.20.cloned.1.call-start = ((), (), s32[]{:S(2)}) async-start(), calls=%async_computation.15 | async-start | bytes 2097152 | tf_op jit(solution)/shard_map/psum | solution.py:357
  558.0 93.4 %reduce-scatter.9.cloned.1.call-start = ((), (), s32[]{:S(2)}) async-start(), calls=%async_computation.16 | async-start | bytes 7864320 | tf_op jit(solution)/shard_map/reduce_scatter | solution.py:716
  570.2 167.8 %all-reduce.22.cloned.1.call-start = ((), (), s32[]{:S(2)}) async-start(), calls=%async_computation.18 | async-start | bytes 4194304 | tf_op jit(solution)/shard_map/psum | solution.py:357
  570.2 25.8 %collective-permute-start.29 = (bf16[256,1280]{1,0:T(8,128)(2,1)}, bf16[256,1280]{1,0:T(8,128)(2,1)S(1)}, u32[]{:S(2)}, u32[]{:S(2)}) collective-permute-start(bf16[256,1280]{1,0:T(8,128)(2,1)} %pad_maximum_fusion.8), channel_id=1, source_target_pairs={{4,0},{12,4},{8,12},{0,8},{5,1},{13,5},{9,13},{1,9},{6,2},{14,6},{... | collective-permute-start | bytes 1966088 | tf_op jit(solution)/shard_map/ppermute | solution.py:113
  571.6 27.2 %collective-permute-start.28 = (bf16[256,1280]{1,0:T(8,128)(2,1)}, bf16[256,1280]{1,0:T(8,128)(2,1)S(1)}, u32[]{:S(2)}, u32[]{:S(2)}) collective-permute-start(bf16[256,1280]{1,0:T(8,128)(2,1)} %pad_maximum_fusion.7), channel_id=1, source_target_pairs={{0,4},{4,12},{12,8},{8,0},{1,5},{5,13},{13,9},{9,1},{2,6},{6,14},{... | collective-permute-start | bytes 1966088 | tf_op jit(solution)/shard_map/ppermute | solution.py:112
  651.4 94.2 %reduce-scatter.11.cloned.1.call-start = ((), (), s32[]{:S(2)}) async-start(), calls=%async_computation.17 | async-start | bytes 7864320 | tf_op jit(solution)/shard_map/reduce_scatter | solution.py:825
  682.4 31.2 %collective-permute-start.37 = (bf16[256,1280]{1,0:T(8,128)(2,1)S(1)}, bf16[256,1280]{1,0:T(8,128)(2,1)S(1)}, u32[]{:S(2)}, u32[]{:S(2)}) collective-permute-start(bf16[256,1280]{1,0:T(8,128)(2,1)S(1)} %pad_maximum_fusion.10), channel_id=1, source_target_pairs={{4,0},{12,4},{8,12},{0,8},{5,1},{13,5},{9,13},{1,9},{6,2},{14,6},{... | collective-permute-start | bytes 1966088 | tf_op jit(solution)/shard_map/ppermute | solution.py:113
  683.8 31.0 %collective-permute-start.35 = (bf16[256,1280]{1,0:T(8,128)(2,1)S(1)}, bf16[256,1280]{1,0:T(8,128)(2,1)S(1)}, u32[]{:S(2)}, u32[]{:S(2)}) collective-permute-start(bf16[256,1280]{1,0:T(8,128)(2,1)S(1)} %pad_maximum_fusion.9), channel_id=1, source_target_pairs={{0,4},{4,12},{12,8},{8,0},{1,5},{5,13},{13,9},{9,1},{2,6},{6,14},{... | collective-permute-start | bytes 1966088 | tf_op jit(solution)/shard_map/ppermute | solution.py:112
  741.2 25.5 %collective-permute-start.25 = (bf16[256,2048]{1,0:T(8,128)(2,1)}, bf16[256,2048]{1,0:T(8,128)(2,1)}, u32[]{:S(2)}, u32[]{:S(2)}) collective-permute-start(bf16[256,2048]{1,0:T(8,128)(2,1)} %add_convert_fusion.high_ref), channel_id=1, source_target_pairs={{0,16},{16,0},{1,17},{17,1},{2,18},{18,2},{3,19},{19,3},{4,20},{20... | collective-permute-start | bytes 3145736 | tf_op jit(solution)/shard_map/ppermute | solution.py:23
  745.7 24.5 %collective-permute-start.45 = (bf16[512,1536]{1,0:T(8,128)(2,1)}, bf16[512,1536]{1,0:T(8,128)(2,1)}, u32[]{:S(2)}, u32[]{:S(2)}) collective-permute-start(bf16[512,1536]{1,0:T(8,128)(2,1)} %reduce-scatter.11.cloned.1.call-done.refs_4_), channel_id=1, source_target_pairs={{16,0},{17,1},{18,2},{19,3},{20,4},{21,5},{22,6},{23,7},{24,8},{25... | collective-permute-start | bytes 4718600 | tf_op jit(solution)/shard_map/ppermute | solution.py:828
  (164 other events, 1306.2 us)
Sparse Core Ops, SparseCore 0:
  21.9 108.7 all-gather.4
  133.7 52.1 all-reduce.9
  211.1 51.1 all-reduce.11
  303.8 51.7 all-reduce.13
  392.5 51.1 all-reduce.15
  476.9 51.8 all-reduce.17
  558.1 51.8 all-reduce.19
  651.5 86.4 all-reduce.21
Sparse Core Ops, SparseCore 1:
  133.8 58.5 all-gather.6
  214.0 89.6 all-gather.8
  306.7 52.4 all-gather.10
  404.7 72.1 reduce-scatter.4
  480.9 77.1 reduce-scatter.6
  570.2 81.1 reduce-scatter.8
  655.2 90.5 reduce-scatter.10

commit v5 on v4

--- a/solution.py
+++ b/solution.py
@@ -133,11 +133,11 @@
     lefts, rights = refs[: -1 - len(plan)], refs[-1 - len(plan) : -1]
     rows = (((0,), (0,)), ((), ()))
     column = 0
-    for left, right_ref in zip(plan, rights):
+    for (left, start, columns), right_ref in zip(plan, rights):
         own, got = lefts[2 * left], lefts[2 * left + 1]
-        half, columns = own.shape[0], right_ref.shape[1]
-        total = lax.dot_general(own[...], right_ref[:half], rows, preferred_element_type=f32)
-        total += lax.dot_general(got[...], right_ref[half:], rows, preferred_element_type=f32)
+        half, part = own.shape[0], slice(start, start + columns)
+        total = lax.dot_general(own[...], right_ref[:half, part], rows, preferred_element_type=f32)
+        total += lax.dot_general(got[...], right_ref[half:, part], rows, preferred_element_type=f32)
         out_ref[:, column : column + columns] = total.astype(bf16)
         column += columns
 
@@ -145,16 +145,15 @@
 def token_terms(lefts, rights):
     tokens, width = lefts[0][0].shape
     tile = 512
-    columns = sum(right[2] for right in rights)
+    columns = sum(right[3] for right in rights)
     side = pl.BlockSpec((tokens, tile), lambda i: (0, i))
-
-    def right_spec(right):
-        return pl.BlockSpec((2 * tokens, right[2]), lambda i: (0, right[3]))
-
+    arrays = [right[1] for right in rights]
+    plan = [(right[0], right[2], right[3]) for right in rights]
     return pl.pallas_call(
-        functools.partial(token_terms_kernel, [right[0] for right in rights]),
+        functools.partial(token_terms_kernel, plan),
         grid=(width // tile,),
-        in_specs=[side] * (2 * len(lefts)) + [right_spec(right) for right in rights],
+        in_specs=[side] * (2 * len(lefts))
+        + [pl.BlockSpec(array.shape, lambda i: (0, 0)) for array in arrays],
         out_specs=pl.BlockSpec((tile, columns), lambda i: (i, 0)),
         out_shape=jax.ShapeDtypeStruct((width, columns), bf16),
         compiler_params=params(),
@@ -163,7 +162,7 @@
             2 * (width * columns + 2 * tokens * width * len(lefts) + 2 * tokens * columns),
         ),
         name="token_terms",
-    )(*(array for pair in lefts for array in pair), *(right[1] for right in rights))
+    )(*(array for pair in lefts for array in pair), *arrays)
 
 
 def attention_terms_kernel(normed_ref, mid_grad_ref, grads_ref, mixed_ref, out_ref):
@@ -203,65 +202,104 @@
     )(normed, mid_grad, grads, mixed)
 
 
-def section_stack_kernel(core_ref, low_ref, high_ref, got_low_ref, got_high_ref, out_ref):
+def section_stacks_kernel(core_ref, *refs):
     first = core_ref[0] == 0
-    keep = jnp.where(first, low_ref[...], high_ref[...])
-    got = jnp.where(first, got_low_ref[...], got_high_ref[...])
-    out_ref[...] = jnp.where(core_ref[0] == pl.program_id(0), keep, got)
-
-
-def section_stack(core, low, high, got_low, got_high):
-    rows, width = low.shape
+    for sources, target in ((refs[:4], refs[8]), (refs[4:8], refs[9])):
+        low, high, got_low, got_high = (source[...] for source in sources)
+        keep, got = jnp.where(first, low, high), jnp.where(first, got_low, got_high)
+        target[...] = jnp.where(core_ref[0] == pl.program_id(0), keep, got)
+
+
+def section_stacks(core, *sources):
+    rows, width = sources[0].shape
     block = pl.BlockSpec((rows, width), lambda i, core: (0, 0))
     return pl.pallas_call(
-        section_stack_kernel,
+        section_stacks_kernel,
         grid_spec=pltpu.PrefetchScalarGridSpec(
             num_scalar_prefetch=1,
             grid=(2,),
-            in_specs=[block] * 4,
-            out_specs=pl.BlockSpec((None, rows, width), lambda i, core: (i, 0, 0)),
+            in_specs=[block] * 8,
+            out_specs=[pl.BlockSpec((None, rows, width), lambda i, core: (i, 0, 0))] * 2,
         ),
-        out_shape=jax.ShapeDtypeStruct((2, rows, width), low.dtype),
+        out_shape=[jax.ShapeDtypeStruct((2, rows, width), bf16)] * 2,
+        compiler_params=params(40),
+        cost_estimate=cost(0, 12 * rows * width * 2),
+        name="section_stacks",
+    )(core.reshape(1), *sources)
+
+
+def attention_outputs_kernel(core_ref, low_ref, high_ref, got_ref, query_ref, key_ref, value_ref, out_ref):
+    first = core_ref[0] == 0
+    keep = jnp.where(first, low_ref[...], high_ref[...])
+    got = got_ref[...]
+    parts = [jnp.where(first == (side == 0), keep, got).astype(f32) for side in range(2)]
+    whole = jnp.concatenate(parts, axis=0)
+    column = 0
+    for ref in (query_ref, key_ref, value_ref):
+        ref[...] = whole[:, column : column + ref.shape[1]]
+        column += ref.shape[1]
+    out_ref[...] = whole[:, column:].T
+
+
+def attention_outputs(core, low, high, got, sizes):
+    n_query, n_key = sizes
+    rows, columns = got.shape
+    whole = lambda *shape: pl.BlockSpec(shape, lambda i, core: (0, 0))
+    shapes = [(2 * rows, n_query), (2 * rows, n_key), (2 * rows, n_key), (n_query, 2 * rows)]
+    return pl.pallas_call(
+        attention_outputs_kernel,
+        grid_spec=pltpu.PrefetchScalarGridSpec(
+            num_scalar_prefetch=1,
+            grid=(1,),
+            in_specs=[whole(rows, columns)] * 3,
+            out_specs=[whole(*shape) for shape in shapes],
+        ),
+        out_shape=[jax.ShapeDtypeStruct(shape, f32) for shape in shapes],
         compiler_params=params(),
-        cost_estimate=cost(0, 6 * rows * width * 2),
-        name="section_stack",
-    )(core.reshape(1), low, high, got_low, got_high)
-
-
-def wide_outputs_kernel(core_ref, *refs):
+        cost_estimate=cost(0, rows * columns * 14),
+        name="attention_outputs",
+    )(core.reshape(1), low, high, got)
+
+
+def wide_outputs_kernel(columns, core_ref, *refs):
     first = core_ref[0] == 0
     gate_ref, up_ref = refs[8:]
-    parts = []
-    for shares in (refs[:4], refs[4:8]):
-        keep = jnp.where(first, shares[0][...], shares[1][...])
-        got = jnp.where(first, shares[2][...], shares[3][...])
-        parts.append([jnp.where(first == (side == 0), keep, got).astype(f32) for side in range(2)])
-    quarter = parts[0][0].shape[1]
-    units = parts[1][0].shape[1] - quarter
-    for side in range(2):
-        at = side * units
-        gate_ref[:, at : at + quarter] = parts[0][side]
-        gate_ref[:, at + quarter : at + units] = parts[1][side][:, :quarter]
-        up_ref[:, at : at + units] = parts[1][side][:, quarter:]
-
-
-def wide_outputs(core, early, late):
-    rows, columns = early[0].shape
-    quarter = columns // 3
-    units = 2 * quarter
+    sections = []
+    for place in range(4):
+        early, late = refs[place][...], refs[4 + place][...]
+        head = columns[place % 2]
+        rest = gate_ref.shape[1] // 2 - head
+        gate = jnp.concatenate([early, late[:, :rest]], axis=1)
+        sections.append((gate, late[:, rest:]))
+    low, high, got_low, got_high = sections
+    for target, part in ((gate_ref, 0), (up_ref, 1)):
+        units = target.shape[1] // 2
+        keep = jnp.where(first, low[part], high[part])
+        got = jnp.where(first, got_low[part], got_high[part])
+        target[:, :units] = jnp.where(first, keep, got).astype(f32)
+        target[:, units:] = jnp.where(first, got, keep).astype(f32)
+
+
+def wide_outputs(core, early, late, units):
+    rows = early[0].shape[0]
+    columns = [share.shape[1] - units for share in early[:2]]
     tile = 128
+
+    def early_spec(head):
+        return pl.BlockSpec((tile, head), lambda i, core: (i, units // head))
+
     return pl.pallas_call(
-        wide_outputs_kernel,
+        functools.partial(wide_outputs_kernel, columns),
         grid_spec=pltpu.PrefetchScalarGridSpec(
             num_scalar_prefetch=1,
             grid=(rows // tile,),
-            in_specs=[pl.BlockSpec((tile, quarter), lambda i, core: (i, 2))] * 4
-            + [pl.BlockSpec((tile, columns), lambda i, core: (i, 0))] * 4,
+            in_specs=[early_spec(head) for head in columns * 2]
+            + [pl.BlockSpec((tile, share.shape[1]), lambda i, core: (i, 0)) for share in late],
             out_specs=[pl.BlockSpec((tile, 2 * units), lambda i, core: (i, 0))] * 2,
         ),
         out_shape=[jax.ShapeDtypeStruct((rows, 2 * units), f32)] * 2,
         compiler_params=params(),
-        cost_estimate=cost(0, rows * (32 * quarter + 4 * 4 * units)),
+        cost_estimate=cost(0, rows * 32 * units),
         name="wide_outputs",
     )(core.reshape(1), *early, *late)
 
@@ -276,9 +314,8 @@
         down_ref[side * units : (side + 1) * units, :] = part.T
 
 
-def down_outputs(core, early):
-    rows, columns = early[0].shape
-    units = 2 * columns // 3
+def down_outputs(core, early, units):
+    rows = early[0].shape[0]
     tile = 128
     return pl.pallas_call(
         down_outputs_kernel,
@@ -481,7 +518,7 @@
 
     partial_ref[...] = lax.dot_general(
         mixed_all[...],
-        wide_ref[:, wide_ref.shape[1] - n_query :],
+        wide_ref[...],
         (((1,), (1,)), ((), ())),
         preferred_element_type=f32,
     ).astype(bf16)
@@ -529,7 +566,7 @@
     step = pl.program_id(0)
     mid_b = mid_grad_ref[...].astype(bf16)
     mid_b_ref[...] = mid_b
-    part = jnp.dot(mid_b, wide_ref[:, wide_ref.shape[1] - n_query :], preferred_element_type=f32)
+    part = jnp.dot(mid_b, wide_ref[...], preferred_element_type=f32)
 
     @pl.when(step == 0)
     def _():
@@ -678,9 +715,9 @@
 
 def attention_forward(stream, gain, wide, place, *others):
     pos, tables, sizes = place
-    normed, inv_rms, queries, own = head_inputs(stream, gain, wide, tables, sizes)
+    normed, inv_rms, queries, own = head_inputs(stream, gain, wide[0], tables, sizes)
     tail = from_behind(own, "ctx", 1)
-    mixed, logs, partial = mix(pos, queries, tail, own, wide, sizes[1])
+    mixed, logs, partial = mix(pos, queries, tail, own, wide[1], sizes[1])
     total, *others = sum_tensor(partial, *others)
     return total, (stream.astype(f32), inv_rms[:, 0], normed, queries, tail, own, mixed, logs), *others
 
@@ -700,7 +737,7 @@
     return own_share(cols_product(hidden, down), middle.shape[0]).astype(bf16)
 
 
-def ffn_backward(own_grad, other_grad, state, wide, down, *others):
+def ffn_backward(own_grad, other_grad, state, wide, down, head, *others):
     middle, _, normed, got, gate, up, hidden = state
     hidden_grad = product(jnp.concatenate([own_grad, other_grad], axis=0), down)
     sigmoid_gate = jax.nn.sigmoid(gate)
@@ -710,11 +747,9 @@
     partial = cols_product(jnp.concatenate([gate_grad, up_grad], axis=1), wide)
     normed_grad, *others = sum_tensor(own_share(partial, middle.shape[0]), *others)
     own_sides, norm_sides = (own_grad, other_grad), (normed, got)
-    early = token_terms(
-        [own_sides, norm_sides], [(0, hidden, units, 0), (1, gate_grad, units // 2, 0)]
-    )
+    early = token_terms([own_sides, norm_sides], [(0, hidden, 0, units), (1, gate_grad, 0, head)])
     early = lax.psum_scatter(early, "ctx", scatter_dimension=0, tiled=True)
-    late = token_terms([norm_sides], [(0, gate_grad, units // 2, 1), (0, up_grad, units, 0)])
+    late = token_terms([norm_sides], [(0, gate_grad, head, units - head), (0, up_grad, 0, units)])
     return normed_grad, early, late, *others
 
 
@@ -727,10 +762,10 @@
     pos, tables, sizes = place
     _, _, normed, queries, tail, own, mixed, logs = saved
     query_grad, back, own_grad, mid_grad_b = mix_back(
-        pos, queries, tail, own, mixed, logs, tables, mid_grad, wide, sizes[1]
+        pos, queries, tail, own, mixed, logs, tables, mid_grad, wide[1], sizes[1]
     )
     back = from_behind(back, "ctx", -1)
-    grads, partial = head_grads(query_grad, own_grad, back, tables, wide, sizes[1])
+    grads, partial = head_grads(query_grad, own_grad, back, tables, wide[0], sizes[1])
     normed_grad, *others = sum_tensor(partial, *others)
     terms = attention_terms(normed, mid_grad_b, grads, mixed, lax.axis_size("ctx"))
     core = lax.axis_index("pipe")
@@ -785,11 +820,14 @@
     attn_keep = jnp.concatenate([rows_mine, gain_rows], axis=0)
     attn_got = swap_cores(jnp.concatenate([rows_theirs, gain_rows], axis=0))
 
+    inner_columns = n_query + 2 * n_key
+
     def attn_weights(pieces):
         got = swap_cores(pieces)
         both = jnp.stack([jnp.where(first, pieces, got), jnp.where(first, got, pieces)], axis=1)
         part_rows = attn_shard.shape[0] // 2
         wide = both[:, :, :part_rows].reshape(width, wide_columns)
+        wide = (wide[:, :inner_columns], wide[:, inner_columns:])
         row = pieces[:, part_rows, : gain_row.shape[1]].astype(f32)
         return wide, row.reshape(count, 2, -1).transpose(1, 0, 2).reshape(2, width)
 
@@ -852,7 +890,7 @@
     state_high = ffn_forward_in(middle, gains_high[1], wide_high, half)
 
     normed_grad, early_high, late_high = ffn_backward(
-        own_grad, other_grad, state_high, wide_high, down_high
+        own_grad, other_grad, state_high, wide_high, down_high, half // 2
     )
     normed_grad, late_high = pin(normed_grad, late_high)
     mid_grad, ffn_gain_high = ffn_backward_out(own_grad, normed_grad, state_high, gains_high[1])
@@ -868,7 +906,7 @@
     )
     got_boundary_high = swap_cores(boundary_high)
     normed_grad, early_low, late_low, late_high = ffn_backward(
-        boundary_high, got_boundary_high, state_low, wide_low, down_low, late_high
+        boundary_high, got_boundary_high, state_low, wide_low, down_low, half // 4, late_high
     )
     normed_grad, late_low, attn_share_high = pin(normed_grad, late_low, ring_scatter(*attn_ring))
     mid_grad, ffn_gain_low = ffn_backward_out(
@@ -878,44 +916,35 @@
     normed_grad, summed, early_low = attention_backward(
         mid_grad, attn_saved_low, attn_low, place, early_low
     )
+    def from_other(low, high):
+        return swap_cores(jnp.where(first, high, low))
+
     (total,) = sum_tensor(out_share)
-
-    def to_owner(low, high):
-        keep_part = jnp.where(first, low, high)
-        got_part = swap_cores(jnp.where(first, high, low))
-        return jnp.where(first, keep_part, got_part), jnp.where(first, got_part, keep_part)
-
+    attn_pair = (ring_scatter(*ring_scatter_start(summed)), attn_share_high)
+    attn_outs = attention_outputs(core, *attn_pair, from_other(*attn_pair), (n_query, n_key))
     early = (early_low, early_high, give_low(early_low), give_high(early_high))
-    down_out = down_outputs(core, early)
-    attn_share_low = ring_scatter(*ring_scatter_start(summed))
-    attn_full = jnp.concatenate(to_owner(attn_share_low, attn_share_high), axis=0).astype(f32)
-    key_at = n_query + n_key
-    value_at = key_at + n_key
-    attn_outs = (
-        attn_full[:, :n_query],
-        attn_full[:, n_query:key_at],
-        attn_full[:, key_at:value_at],
-        attn_full[:, value_at:].T,
-    )
+    down_out = down_outputs(core, early, half)
     normed_grad, down_out, attn_outs, got_late_high = pin(
         normed_grad, down_out, attn_outs, give_high(late_high)
     )
     out_high = (middle + total.astype(f32)).astype(bf16)
-    section_outputs = section_stack(core, out_low, out_high, got_out_low, swap_cores(out_high))
 
     boundary_low, attn_gain_low = attention_backward_out(
         mid_grad, normed_grad, attn_saved_low, gains_low[0]
     )
-    boundary_grads = section_stack(
-        core, boundary_low, boundary_high, swap_cores(boundary_low), got_boundary_high
-    )
-    late = (late_low, late_high, give_low(late_low), got_late_high)
-    gate_out, up_out = wide_outputs(core, early, late)
     gains_out = share_gains(
         jnp.stack(
             [jnp.stack([attn_gain_low, ffn_gain_low]), jnp.stack([attn_gain_high, ffn_gain_high])]
         )
     )
+    late_low, gains_out, got_out_high, got_boundary_low = pin(
+        late_low, gains_out, swap_cores(out_high), swap_cores(boundary_low)
+    )
+    outs = (out_low, out_high, got_out_low, got_out_high)
+    boundaries = (boundary_low, boundary_high, got_boundary_low, got_boundary_high)
+    section_outputs, boundary_grads = section_stacks(core, *outs, *boundaries)
+    late = (late_low, late_high, give_low(late_low), got_late_high)
+    gate_out, up_out = wide_outputs(core, early, late, half)
     query_out, key_out, value_out, attn_out = attn_outs
     return (
         section_outputs[None],

time: 795 us -> 782 us (0.984)
    unnamed x261 -> x262, local copies, waits for them, and re-layouts: 76.9 us -> 70 us
  transfers between devices with their start and end apart: 61 -> 61, of which waited for: 42 -> 44; matrix products, arithmetic and copies ran while one was open for 17% -> 17% of each run, Pallas kernels for 8% -> 9%
where the time goes in v5:
time: 782 us; the launch traced here: 770 us
  waiting for transfers between devices  382 us (49%)
  local copies, waits for them, and re-layouts  113 us (14%)
  Pallas kernels  72 us (9%)
  other arithmetic  67.5 us (9%)
  matrix products  52.5 us (7%)
  starting transfers between devices  42.9 us (5%)
  between operations  41.1 us (5%)
    psum x7, waiting for transfers between devices, sum_tensor(): return (lax.psum(partial, 'tensor'), *others)  144 us
    unnamed x262, local copies, waits for them, and re-layouts  70 us
    ppermute x2, waiting for transfers between devices, ring_scatter(): from_front = lax.ppermute(to_back, 'ctx', behind)  45.9 us
    ppermute x19, waiting for transfers between devices, swap_cores(): return lax.ppermute(block, 'pipe', [(0, 1), (1, 0)])  37.2 us
    ppermute x2, waiting for transfers between devices, ring_gather_start(): from_back.append(lax.ppermute(from_back[-1], 'ctx', ahead))  33.9 us
    dot_general x4, matrix products, product(): lax.dot_general(left, right, (((1,), (0,)), ((), ())), preferred_element_...  30.3 us
    ppermute x4, waiting for transfers between devices, from_behind(): return lax.ppermute(block, axis, route)  29.3 us
    dot_general x4, matrix products, cols_product(): lax.dot_general(left, right, (((1,), (1,)), ((), ())), preferred_element_...  22.3 us
  transfers between devices with their start and end apart: 61, of which 44 were waited for; matrix products, arithmetic and copies ran while one was open for 17% of the time, Pallas kernels for 9%

profile of v5, /device:TPU:0, one launch (start us, length us, event | category | flops | bytes accessed | tf_op | source)
XLA Modules:
  0.0 770.4 jit_solution(8843800546480977716)
XLA Ops:
  53.2 22.0 %collective-permute-done.1 = bf16[272,1280]{1,0:T(8,128)(2,1)S(1)} collective-permute-done((bf16[272,1280]{1,0:T(8,128)(2,1)S(1)}, bf16[272,1280]{1,0:T(8,128)(2,1)S(1)}, u32[]{:S(2)}, u32[]{:S(2)}) %collective-permute-start.1) | collective-permute-done | bytes 696352 | tf_op jit(solution)/shard_map/ppermute | solution.py:62
  79.2 14.2 %collective-permute-done.3 = bf16[272,640]{1,0:T(8,128)(2,1)S(1)} collective-permute-done((bf16[272,640]{1,0:T(8,128)(2,1)S(1)}, bf16[272,640]{1,0:T(8,128)(2,1)S(1)}, u32[]{:S(2)}, u32[]{:S(2)}) %collective-permute-start.3) | collective-permute-done | bytes 348192 | tf_op jit(solution)/shard_map/ppermute | solution.py:71
  118.9 6.2 mix.2
  133.6 8.8 %dynamic-slice_bitcast_fusion = bf16[2048,2048]{1,0:T(8,128)(2,1)} fusion(bf16[2,2048,2048]{2,1,0:T(8,128)(2,1)} %bitcast.203, s32[]{:T(128)S(6)} %select_n.224), kind=kLoop, calls=%fused_computation | loop fusion | bytes 16777220 | tf_op jit(solution)/shard_map/jit(dynamic_index_in_dim)/squeeze | solution.py:806
  142.5 11.9 %collective-permute-done.9 = bf16[272,1280]{1,0:T(8,128)(2,1)S(1)} collective-permute-done((bf16[272,1280]{1,0:T(8,128)(2,1)}, bf16[272,1280]{1,0:T(8,128)(2,1)S(1)}, u32[]{:S(2)}, u32[]{:S(2)}) %collective-permute-start.9) | collective-permute-done | bytes 696352 | tf_op jit(solution)/shard_map/ppermute | solution.py:62
  155.8 30.1 %all-reduce.10.cloned.1.call-done = bf16[256,2048]{1,0:T(8,128)(2,1)} async-done(((bf16[256,2048]{1,0:T(8,128)(2,1)}), bf16[256,2048]{1,0:T(8,128)(2,1)}) %all-reduce.10.cloned.1.call-update) | async-done | bytes 1048592 | tf_op jit(solution)/shard_map/psum | solution.py:394
  190.9 7.3 fusion.34
  237.9 24.4 %all-reduce.12.cloned.1.call-done = bf16[256,2048]{1,0:T(8,128)(2,1)} async-done(((bf16[256,2048]{1,0:T(8,128)(2,1)}), bf16[256,2048]{1,0:T(8,128)(2,1)}) %all-reduce.12.cloned.1.call-update) | async-done | bytes 1048592 | tf_op jit(solution)/shard_map/psum | solution.py:394
  288.0 15.6 %all-gather.9.cloned.1.call-done = bf16[2048,2048]{1,0:T(8,128)(2,1)} async-done(((bf16[512,2048]{1,0:T(8,128)(2,1)}), bf16[2048,2048]{1,0:T(8,128)(2,1)}) %all-gather.9.cloned.1.call-update) | async-done | bytes 8388624 | tf_op jit(solution)/shard_map/all_gather | solution.py:845
  308.0 47.7 %all-reduce.14.cloned.1.call-done = bf16[256,2048]{1,0:T(8,128)(2,1)} async-done(((bf16[256,2048]{1,0:T(8,128)(2,1)}), bf16[256,2048]{1,0:T(8,128)(2,1)}) %all-reduce.14.cloned.1.call-update) | async-done | bytes 1048592 | tf_op jit(solution)/shard_map/psum | solution.py:394
  361.2 10.0 %fusion.42 = f32[512,2048]{1,0:T(8,128)} fusion(bf16[2048,2048]{1,0:T(8,128)(2,1)} %all-gather.9.cloned.1.call-done, bf16[256,2048]{1,0:T(8,128)(2,1)S(1)} %collective-permute-done.18.refs_1_.refs_3_, bf16[256,2048]{1,0:T(8,128)(2,1)S(1)} %multiply_convert_fusion.5.refs_0_.refs_2_), kind=kOutput, calls=%fused_computation.77 | convolution fusion | flops 4299161600 | bytes 14680064 | tf_op jit(solution)/shard_map/dot_general | solution.py:358
  373.2 7.3 multiply_convert_fusion.4
  380.5 7.7 fusion.46
  415.4 28.4 %all-reduce.16.cloned.1.call-done = bf16[256,2048]{1,0:T(8,128)(2,1)} async-done(((bf16[256,2048]{1,0:T(8,128)(2,1)}), bf16[256,2048]{1,0:T(8,128)(2,1)}) %all-reduce.16.cloned.1.call-update) | async-done | bytes 1048592 | tf_op jit(solution)/shard_map/psum | solution.py:394
  449.4 6.5 mix_back.2
  458.2 9.4 %collective-permute-done.20.back_ref = bf16[256,256]{1,0:T(8,128)(2,1)S(1)} collective-permute-done((bf16[256,256]{1,0:T(8,128)(2,1)S(1)}, bf16[256,256]{1,0:T(8,128)(2,1)S(1)}, u32[]{:S(2)}, u32[]{:S(2)}) %collective-permute-start.20) | collective-permute-done | bytes 131104 | tf_op jit(solution)/shard_map/ppermute | solution.py:29
  508.1 13.7 %collective-permute-done.22 = bf16[256,640]{1,0:T(8,128)(2,1)S(1)} collective-permute-done((bf16[256,640]{1,0:T(8,128)(2,1)S(1)}, bf16[256,640]{1,0:T(8,128)(2,1)S(1)}, u32[]{:S(2)}, u32[]{:S(2)}) %collective-permute-start.22) | collective-permute-done | bytes 327712 | tf_op jit(solution)/shard_map/ppermute | solution.py:94
  571.5 23.6 %collective-permute-done.28 = bf16[256,1280]{1,0:T(8,128)(2,1)S(1)} collective-permute-done((bf16[256,1280]{1,0:T(8,128)(2,1)}, bf16[256,1280]{1,0:T(8,128)(2,1)S(1)}, u32[]{:S(2)}, u32[]{:S(2)}) %collective-permute-start.28) | collective-permute-done | bytes 655392 | tf_op jit(solution)/shard_map/ppermute | solution.py:113
  615.9 6.5 mix_back.3
  624.7 9.3 %collective-permute-done.29.back_ref = bf16[256,256]{1,0:T(8,128)(2,1)S(1)} collective-permute-done((bf16[256,256]{1,0:T(8,128)(2,1)S(1)}, bf16[256,256]{1,0:T(8,128)(2,1)S(1)}, u32[]{:S(2)}, u32[]{:S(2)}) %collective-permute-start.29) | collective-permute-done | bytes 131104 | tf_op jit(solution)/shard_map/ppermute | solution.py:29
  657.8 15.1 %collective-permute-done.35 = bf16[256,640]{1,0:T(8,128)(2,1)S(1)} collective-permute-done((bf16[256,640]{1,0:T(8,128)(2,1)S(1)}, bf16[256,640]{1,0:T(8,128)(2,1)S(1)}, u32[]{:S(2)}, u32[]{:S(2)}) %collective-permute-start.35) | collective-permute-done | bytes 327712 | tf_op jit(solution)/shard_map/ppermute | solution.py:95
  681.9 22.3 %collective-permute-done.36 = bf16[256,1280]{1,0:T(8,128)(2,1)S(1)} collective-permute-done((bf16[256,1280]{1,0:T(8,128)(2,1)S(1)}, bf16[256,1280]{1,0:T(8,128)(2,1)S(1)}, u32[]{:S(2)}, u32[]{:S(2)}) %collective-permute-start.36) | collective-permute-done | bytes 655392 | tf_op jit(solution)/shard_map/ppermute | solution.py:113
  719.7 9.9 %all-reduce.22.cloned.1.call-done = (bf16[256,2048]{1,0:T(8,128)(2,1)}, bf16[256,2048]{1,0:T(8,128)(2,1)}) async-done(((bf16[256,2048]{1,0:T(8,128)(2,1)}, bf16[256,2048]{1,0:T(8,128)(2,1)}), (bf16[256,2048]{1,0:T(8,128)(2,1)}, bf16[256,2048]{1,0:T(8,128)(2,1)})) %all-reduce.22.cloned.1.call-update) | async-done | bytes 2097168 | tf_op jit(solution)/shard_map/psum | solution.py:394
  756.4 6.1 wide_outputs.1
  (514 shorter events, 365.1 us)
Async XLA Ops:
  8.0 122.7 %all-gather.5.cloned.1.call-start = ((), (), s32[]{:S(2)}) async-start(), calls=%async_computation.4 | async-start | bytes 18874368 | tf_op jit(solution)/shard_map/all_gather | solution.py:850
  21.8 164.1 %all-reduce.10.cloned.1.call-start = ((), (), s32[]{:S(2)}) async-start(), calls=%async_computation.5 | async-start | bytes 2097152 | tf_op jit(solution)/shard_map/psum | solution.py:394
  25.8 25.7 %collective-permute-start.6 = (bf16[512,1024]{0,1:T(8,128)(2,1)}, bf16[512,1024]{0,1:T(8,128)(2,1)S(1)}, u32[]{:S(2)}, u32[]{:S(2)}) collective-permute-start(bf16[512,1024]{0,1:T(8,128)(2,1)} %dynamic-slice_bitcast_fusion.5), channel_id=1, source_target_pairs={{0,16},{16,0},{1,17},{17,1},{2,18},{18,2},{3,19},{19,3},{4,20},{20... | collective-permute-start | bytes 3145736 | tf_op jit(solution)/shard_map/ppermute | solution.py:23
  47.8 27.4 %collective-permute-start.1 = (bf16[272,1280]{1,0:T(8,128)(2,1)S(1)}, bf16[272,1280]{1,0:T(8,128)(2,1)S(1)}, u32[]{:S(2)}, u32[]{:S(2)}) collective-permute-start(bf16[272,1280]{1,0:T(8,128)(2,1)S(1)} %get-tuple-element.192), channel_id=1, source_target_pairs={{0,4},{4,12},{12,8},{8,0},{1,5},{5,13},{13,9},{9,1},{2,6},{6,14},{... | collective-permute-start | bytes 2088968 | tf_op jit(solution)/shard_map/ppermute | solution.py:62
  130.8 71.1 %all-gather.7.cloned.1.call-start = ((), (), s32[]{:S(2)}) async-start(), calls=%async_computation.6 | async-start | bytes 5242880 | tf_op jit(solution)/shard_map/all_gather | solution.py:845
  131.3 131.0 %all-reduce.12.cloned.1.call-start = ((), (), s32[]{:S(2)}) async-start(), calls=%async_computation.7 | async-start | bytes 2097152 | tf_op jit(solution)/shard_map/psum | solution.py:394
  211.0 92.7 %all-gather.9.cloned.1.call-start = ((), (), s32[]{:S(2)}) async-start(), calls=%async_computation.8 | async-start | bytes 10485760 | tf_op jit(solution)/shard_map/all_gather | solution.py:845
  211.6 144.1 %all-reduce.14.cloned.1.call-start = ((), (), s32[]{:S(2)}) async-start(), calls=%async_computation.9 | async-start | bytes 2097152 | tf_op jit(solution)/shard_map/psum | solution.py:394
  303.7 69.5 %all-gather.11.cloned.1.call-start = ((), (), s32[]{:S(2)}) async-start(), calls=%async_computation.10 | async-start | bytes 5242880 | tf_op jit(solution)/shard_map/all_gather | solution.py:845
  304.3 139.5 %all-reduce.16.cloned.1.call-start = ((), (), s32[]{:S(2)}) async-start(), calls=%async_computation.11 | async-start | bytes 2097152 | tf_op jit(solution)/shard_map/psum | solution.py:394
  392.4 84.2 %reduce-scatter.5.cloned.1.call-start = ((), (), s32[]{:S(2)}) async-start(), calls=%async_computation.12 | async-start | bytes 7864320 | tf_op jit(solution)/shard_map/reduce_scatter | solution.py:751
  404.5 124.2 %all-reduce.18.cloned.1.call-start = ((), (), s32[]{:S(2)}) async-start(), calls=%async_computation.13 | async-start | bytes 2097152 | tf_op jit(solution)/shard_map/psum | solution.py:394
  476.7 81.2 %reduce-scatter.7.cloned.1.call-start = ((), (), s32[]{:S(2)}) async-start(), calls=%async_computation.14 | async-start | bytes 7864320 | tf_op jit(solution)/shard_map/reduce_scatter | solution.py:863
  477.4 132.8 %all-reduce.20.cloned.1.call-start = ((), (), s32[]{:S(2)}) async-start(), calls=%async_computation.15 | async-start | bytes 2097152 | tf_op jit(solution)/shard_map/psum | solution.py:394
  557.9 84.6 %reduce-scatter.11.cloned.1.call-start = ((), (), s32[]{:S(2)}) async-start(), calls=%async_computation.17 | async-start | bytes 6553600 | tf_op jit(solution)/shard_map/reduce_scatter | solution.py:751
  569.1 160.5 %all-reduce.22.cloned.1.call-start = ((), (), s32[]{:S(2)}) async-start(), calls=%async_computation.18 | async-start | bytes 4194304 | tf_op jit(solution)/shard_map/psum | solution.py:394
  569.2 25.8 %collective-permute-start.28 = (bf16[256,1280]{1,0:T(8,128)(2,1)}, bf16[256,1280]{1,0:T(8,128)(2,1)S(1)}, u32[]{:S(2)}, u32[]{:S(2)}) collective-permute-start(bf16[256,1280]{1,0:T(8,128)(2,1)} %pad_maximum_fusion.8), channel_id=1, source_target_pairs={{4,0},{12,4},{8,12},{0,8},{5,1},{13,5},{9,13},{1,9},{6,2},{14,6},{... | collective-permute-start | bytes 1966088 | tf_op jit(solution)/shard_map/ppermute | solution.py:113
  570.6 27.2 %collective-permute-start.27 = (bf16[256,1280]{1,0:T(8,128)(2,1)}, bf16[256,1280]{1,0:T(8,128)(2,1)S(1)}, u32[]{:S(2)}, u32[]{:S(2)}) collective-permute-start(bf16[256,1280]{1,0:T(8,128)(2,1)} %pad_maximum_fusion.7), channel_id=1, source_target_pairs={{0,4},{4,12},{12,8},{8,0},{1,5},{5,13},{13,9},{9,1},{2,6},{6,14},{... | collective-permute-start | bytes 1966088 | tf_op jit(solution)/shard_map/ppermute | solution.py:112
  642.5 104.0 %reduce-scatter.9.cloned.1.call-start = ((), (), s32[]{:S(2)}) async-start(), calls=%async_computation.16 | async-start | bytes 9175040 | tf_op jit(solution)/shard_map/reduce_scatter | solution.py:863
  673.1 31.1 %collective-permute-start.36 = (bf16[256,1280]{1,0:T(8,128)(2,1)S(1)}, bf16[256,1280]{1,0:T(8,128)(2,1)S(1)}, u32[]{:S(2)}, u32[]{:S(2)}) collective-permute-start(bf16[256,1280]{1,0:T(8,128)(2,1)S(1)} %pad_maximum_fusion.10), channel_id=1, source_target_pairs={{4,0},{12,4},{8,12},{0,8},{5,1},{13,5},{9,13},{1,9},{6,2},{14,6},{... | collective-permute-start | bytes 1966088 | tf_op jit(solution)/shard_map/ppermute | solution.py:113
  674.8 31.0 %collective-permute-start.34 = (bf16[256,1280]{1,0:T(8,128)(2,1)S(1)}, bf16[256,1280]{1,0:T(8,128)(2,1)S(1)}, u32[]{:S(2)}, u32[]{:S(2)}) collective-permute-start(bf16[256,1280]{1,0:T(8,128)(2,1)S(1)} %pad_maximum_fusion.9), channel_id=1, source_target_pairs={{0,4},{4,12},{12,8},{8,0},{1,5},{5,13},{13,9},{9,1},{2,6},{6,14},{... | collective-permute-start | bytes 1966088 | tf_op jit(solution)/shard_map/ppermute | solution.py:112
  675.4 39.3 %collective-permute-start.31 = (bf16[512,1536]{1,0:T(8,128)(2,1)}, bf16[512,1536]{1,0:T(8,128)(2,1)}, u32[]{:S(2)}, u32[]{:S(2)}) collective-permute-start(bf16[512,1536]{1,0:T(8,128)(2,1)} %reduce-scatter.5.cloned.1.call-done.high_ref.refs_1_), channel_id=1, source_target_pairs={{0,16},{1,17},{2,18},{3,19},{4,20},{5,21},{6,22},{7,23},{8,24},{9,... | collective-permute-start | bytes 4718600 | tf_op jit(solution)/shard_map/ppermute | solution.py:869
  677.9 41.8 %collective-permute-start.38 = (bf16[512,1536]{1,0:T(8,128)(2,1)}, bf16[512,1536]{1,0:T(8,128)(2,1)}, u32[]{:S(2)}, u32[]{:S(2)}) collective-permute-start(bf16[512,1536]{1,0:T(8,128)(2,1)} %reduce-scatter.7.cloned.1.call-done.refs_5_), channel_id=1, source_target_pairs={{0,16},{1,17},{2,18},{3,19},{4,20},{5,21},{6,22},{7,23},{8,24},{9,... | collective-permute-start | bytes 4718600 | tf_op jit(solution)/shard_map/ppermute | solution.py:869
  680.4 34.4 %collective-permute-start.30 = (bf16[512,1280]{1,0:T(8,128)(2,1)}, bf16[512,1280]{1,0:T(8,128)(2,1)}, u32[]{:S(2)}, u32[]{:S(2)}) collective-permute-start(bf16[512,1280]{1,0:T(8,128)(2,1)} %reduce-scatter.11.cloned.1.call-done.low_ref.refs_0_), channel_id=1, source_target_pairs={{16,0},{17,1},{18,2},{19,3},{20,4},{21,5},{22,6},{23,7},{24,8},{25... | collective-permute-start | bytes 3932168 | tf_op jit(solution)/shard_map/ppermute | solution.py:866
  (165 other events, 1292.6 us)
Sparse Core Ops, SparseCore 0:
  21.9 108.7 all-gather.4
  133.7 52.1 all-reduce.9
  211.1 51.1 all-reduce.11
  303.8 51.8 all-reduce.13
  392.5 51.1 all-reduce.15
  476.8 51.8 all-reduce.17
  558.0 51.8 all-reduce.19
  642.6 87.0 all-reduce.21
Sparse Core Ops, SparseCore 1:
  133.8 58.8 all-gather.6
  214.0 89.6 all-gather.8
  306.7 52.4 all-gather.10
  404.5 72.1 reduce-scatter.4
  480.7 77.0 reduce-scatter.6
  569.2 73.2 reduce-scatter.10
  646.2 99.9 reduce-scatter.8

commit v6 on v5

--- a/solution.py
+++ b/solution.py
@@ -40,17 +40,25 @@
     return [y * across + x for y, x in walk]
 
 
+def take(array, index, axis=0):
+    return lax.dynamic_index_in_dim(
+        array, index, axis, keepdims=False, allow_negative_indices=False
+    )
+
+
 def ring_tools():
     count = lax.axis_size("ctx")
     order = ring_order(count)
-    place = [order.index(device) for device in range(count)]
     ahead = [(order[i], order[(i + 1) % count]) for i in range(count)]
     behind = [(b, a) for a, b in ahead]
-    at = jnp.asarray(place, jnp.int32)[lax.axis_index("ctx")]
-    table = jnp.asarray(order * 2, jnp.int32)
+    device = lax.axis_index("ctx")
 
     def device_at(distance):
-        return table[at + distance % count]
+        if order == [0, 1, 3, 2]:
+            place = ((device ^ (device >> 1)) + distance % count) & 3
+            return place ^ (place >> 1)
+        place = jnp.asarray([order.index(i) for i in range(count)], jnp.int32)
+        return take(jnp.asarray(order * 2, jnp.int32), take(place, device) + distance % count)
 
     return count, ahead, behind, device_at
 
@@ -73,7 +81,9 @@
     out = jnp.zeros((count,) + block.shape, block.dtype)
 
     def put(out, piece, distance, column=0):
-        return lax.dynamic_update_slice(out, piece[None], (device_at(distance), 0, column))
+        return lax.dynamic_update_slice(
+            out, piece[None], (device_at(distance), 0, column), allow_negative_indices=False
+        )
 
     out = put(out, block, 0)
     for distance in range(1, count // 2):
@@ -84,7 +94,7 @@
 
 
 def ring_term(terms, distance):
-    return lax.dynamic_index_in_dim(terms, ring_tools()[3](distance), 0, keepdims=False)
+    return take(terms, ring_tools()[3](distance))
 
 
 def ring_scatter_start(terms):
@@ -339,13 +349,13 @@
 def share_gains(terms):
     core, shard = lax.axis_index("pipe"), lax.axis_index("ctx")
     count = lax.axis_size("ctx")
-    own = lax.dynamic_index_in_dim(terms, core, 0, keepdims=False)
-    other = lax.dynamic_index_in_dim(terms, 1 - core, 0, keepdims=False)
+    own = take(terms, core)
+    other = take(terms, 1 - core)
     total = own + swap_cores(other)
     blocks = total.reshape(2, count, -1)
 
     def block(index):
-        return lax.dynamic_index_in_dim(blocks, index, 1, keepdims=False)
+        return take(blocks, index, 1)
 
     result = block(shard)
     for step in range(1, count):
@@ -722,12 +732,13 @@
     return total, (stream.astype(f32), inv_rms[:, 0], normed, queries, tail, own, mixed, logs), *others
 
 
-def ffn_forward_in(middle, gain, wide, hidden_width):
+def ffn_forward_in(middle, gain, wides, hidden_width):
     normed, inv_rms = norm_forward(middle, gain)
     got = swap_cores(normed)
-    gate_up = product(jnp.concatenate([normed, got], axis=0), wide)
-    gate = gate_up[:, :hidden_width]
-    up = gate_up[:, hidden_width:]
+    both = jnp.concatenate([normed, got], axis=0)
+    gate_up = [product(both, wide) for wide in wides]
+    gate = gate_up[0][:, :hidden_width]
+    up = jnp.concatenate([gate_up[0][:, hidden_width:], *gate_up[1:]], axis=1)
     hidden = (jax.nn.silu(gate) * up).astype(bf16)
     return (middle, inv_rms, normed, got, gate, up, hidden)
 
@@ -769,8 +780,8 @@
     normed_grad, *others = sum_tensor(partial, *others)
     terms = attention_terms(normed, mid_grad_b, grads, mixed, lax.axis_size("ctx"))
     core = lax.axis_index("pipe")
-    mine = lax.dynamic_index_in_dim(terms, core, 0, keepdims=False)
-    theirs = lax.dynamic_index_in_dim(terms, 1 - core, 0, keepdims=False)
+    mine = take(terms, core)
+    theirs = take(terms, 1 - core)
     return normed_grad, add_bf16(mine, swap_cores(theirs)), *others
 
 
@@ -803,12 +814,16 @@
     half = w_gate.shape[2] // 2
 
     def pick(pair, index):
-        return lax.dynamic_index_in_dim(pair, index, 0, keepdims=False)
+        return take(pair, index)
 
     def mine_theirs(array, axis):
         size = array.shape[axis] // 2
-        mine = lax.dynamic_slice_in_dim(array, core * size, size, axis)
-        theirs = lax.dynamic_slice_in_dim(array, (1 - core) * size, size, axis)
+        mine = lax.dynamic_slice_in_dim(
+            array, core * size, size, axis, allow_negative_indices=False
+        )
+        theirs = lax.dynamic_slice_in_dim(
+            array, (1 - core) * size, size, axis, allow_negative_indices=False
+        )
         return mine, theirs
 
     count = lax.axis_size("ctx")
@@ -847,13 +862,18 @@
     attn_parts = for_sections(attn_keep, attn_got)
     wide_parts = for_sections(wide_keep, wide_got)
     down_parts = for_sections(down_keep, down_got)
-    wide_low = lax.all_gather(wide_parts[0], ("pipe", "ctx"), axis=0, tiled=True)
+    tail_columns = half // 4
+    wide_low = lax.all_gather(
+        wide_parts[0][:, :-tail_columns], ("pipe", "ctx"), axis=0, tiled=True
+    )
+    down_parts[0] = jnp.concatenate([down_parts[0], wide_parts[0][:, -tail_columns:]], axis=1)
     attn_pieces, attn_parts[1], wide_parts[1], *down_parts = pin(
         ring_gather(*ring_gather_start(attn_parts[0])), attn_parts[1], wide_parts[1], *down_parts
     )
     attn_low, gains_low = attn_weights(attn_pieces)
-    down_low = gather(down_parts[0])
-    wide_high = gather(wide_parts[1])
+    down_and_tail = gather(down_parts[0])
+    ring_columns = wide_parts[1].shape[1] // 4
+    wide_high = gather(wide_parts[1][:, :-ring_columns])
     down_high = gather(down_parts[1])
 
     pos_row = pick(positions, core)
@@ -875,19 +895,25 @@
     wide_low = pick(wide_low.reshape(2, width, -1), core)
     total, wide_low, attn_ring = pin(total, wide_low, ring_gather_start(attn_part_high))
     middle = attn_saved_low[0] + total.astype(f32)
-    state_low = ffn_forward_in(middle, gains_low[1], wide_low, half)
+    down_low, wide_tail = down_and_tail[:, :half], down_and_tail[:, half:]
+    state_low = ffn_forward_in(middle, gains_low[1], [wide_low, wide_tail], half)
     own_grad, other_grad = pick(out_grad, core), pick(out_grad, 1 - core)
     (total,) = sum_tensor(ffn_share(state_low, down_low))
-    total, own_grad, other_grad, (attn_high, gains_high) = pin(
-        total, own_grad, other_grad, attn_weights(ring_gather(*attn_ring))
+    wide_low = jnp.concatenate([wide_low, wide_tail], axis=1)
+    total, own_grad, other_grad, (attn_high, gains_high), wide_low = pin(
+        total, own_grad, other_grad, attn_weights(ring_gather(*attn_ring)), wide_low
     )
     out_low = (middle + total.astype(f32)).astype(bf16)
-    total, attn_saved_high, wide_high = attention_forward(
-        out_low, gains_high[0], attn_high, place, wide_high
-    )
-    total, got_out_low = pin(total, swap_cores(out_low))
+    total, attn_saved_high, wide_high, wide_part_high = attention_forward(
+        out_low, gains_high[0], attn_high, place, wide_high, wide_parts[1][:, -ring_columns:]
+    )
+    wide_ring = ring_gather_start(wide_part_high)
+    wide_high = jnp.concatenate(
+        [wide_high, ring_gather(*wide_ring).reshape(width, ring_columns)], axis=1
+    )
+    total, got_out_low, wide_high = pin(total, swap_cores(out_low), wide_high)
     middle = attn_saved_high[0] + total.astype(f32)
-    state_high = ffn_forward_in(middle, gains_high[1], wide_high, half)
+    state_high = ffn_forward_in(middle, gains_high[1], [wide_high], half)
 
     normed_grad, early_high, late_high = ffn_backward(
         own_grad, other_grad, state_high, wide_high, down_high, half // 2

time: 782 us -> 762 us (0.974)
  between operations: 41.1 us -> 17.6 us
  waiting for transfers between devices: 382 us -> 361 us
  other arithmetic: 67.5 us -> 79.1 us
  starting transfers between devices: 42.9 us -> 51.8 us
    psum x7, waiting for transfers between devices: 144 us -> 112 us  [sum_tensor(): return (lax.psum(partial, 'tensor'), *others)]
    ppermute x2 -> x3, waiting for transfers between devices: 33.9 us -> 51.9 us  [ring_gather_start(): from_back.append(lax.ppermute(from_back[-1], 'ctx', ahead))]
    all_gather x3, waiting for transfers between devices: 15.7 us -> 0.19 us  [gather(): return lax.all_gather(shard_part, 'ctx', axis=0, tiled=True)]
    concatenate x0 -> x3, other arithmetic: none -> 13.3 us  [the longest x1 8.22 us: on_device(): jnp.concatenate([wide_high, ring_gather(*wide_ring).reshape(width, ring_c...]
    slice x1 -> x8, local copies, waits for them, and re-layouts: 0.62 us -> 9.25 us  [the longest x1 1.89 us: on_device(): wide_parts[1][:, -ring_columns:]]
    ppermute x2 -> x3, waiting for transfers between devices: 14.5 us -> 19.8 us  [ring_gather(): left = lax.ppermute(from_back[-1][:, :half], 'ctx', ahead)]
    dot_general x4 -> x5, matrix products: 30.3 us -> 32.6 us  [product(): lax.dot_general(left, right, (((1,), (0,)), ((), ())), preferred_element_...]
    unnamed x262 -> x274, local copies, waits for them, and re-layouts: 70 us -> 67.8 us
  transfers between devices with their start and end apart: 61 -> 65, of which waited for: 44 -> 46; matrix products, arithmetic and copies ran while one was open for 17% -> 19% of each run, Pallas kernels for 9% -> 9%
where the time goes in v6:
time: 762 us; the launch traced here: 750 us
  waiting for transfers between devices  361 us (47%)
  local copies, waits for them, and re-layouts  115 us (15%)
  other arithmetic  79.1 us (10%)
  Pallas kernels  72.4 us (10%)
  matrix products  52.2 us (7%)
  starting transfers between devices  51.8 us (7%)
  between operations  17.6 us (2%)
    psum x7, waiting for transfers between devices, sum_tensor(): return (lax.psum(partial, 'tensor'), *others)  112 us
    unnamed x274, local copies, waits for them, and re-layouts  67.8 us
    ppermute x3, waiting for transfers between devices, ring_gather_start(): from_back.append(lax.ppermute(from_back[-1], 'ctx', ahead))  51.9 us
    ppermute x2, waiting for transfers between devices, ring_scatter(): from_front = lax.ppermute(to_back, 'ctx', behind)  46 us
    ppermute x19, waiting for transfers between devices, swap_cores(): return lax.ppermute(block, 'pipe', [(0, 1), (1, 0)])  33.2 us
    dot_general x5, matrix products, product(): lax.dot_general(left, right, (((1,), (0,)), ((), ())), preferred_element_...  32.6 us
    ppermute x4, waiting for transfers between devices, from_behind(): return lax.ppermute(block, axis, route)  27.6 us
    ppermute x3, waiting for transfers between devices, ring_gather(): left = lax.ppermute(from_back[-1][:, :half], 'ctx', ahead)  19.8 us
  transfers between devices with their start and end apart: 65, of which 46 were waited for; matrix products, arithmetic and copies ran while one was open for 19% of the time, Pallas kernels for 9%

profile of v6, /device:TPU:0, one launch (start us, length us, event | category | flops | bytes accessed | tf_op | source)
XLA Modules:
  0.0 750.1 jit_solution(786543807334865428)
XLA Ops:
  39.1 25.6 %collective-permute-done.1 = bf16[272,1280]{1,0:T(8,128)(2,1)S(1)} collective-permute-done((bf16[272,1280]{1,0:T(8,128)(2,1)S(1)}, bf16[272,1280]{1,0:T(8,128)(2,1)S(1)}, u32[]{:S(2)}, u32[]{:S(2)}) %collective-permute-start.1) | collective-permute-done | bytes 696352 | tf_op jit(solution)/shard_map/ppermute | solution.py:70
  69.4 8.5 %collective-permute-done.3 = bf16[272,640]{1,0:T(8,128)(2,1)S(1)} collective-permute-done((bf16[272,640]{1,0:T(8,128)(2,1)S(1)}, bf16[272,640]{1,0:T(8,128)(2,1)S(1)}, u32[]{:S(2)}, u32[]{:S(2)}) %collective-permute-start.3) | collective-permute-done | bytes 348192 | tf_op jit(solution)/shard_map/ppermute | solution.py:79
  117.3 8.9 %all-gather.5.cloned.1.call-done = bf16[4096,1792]{1,0:T(8,128)(2,1)} async-done(((bf16[512,1792]{1,0:T(8,128)(2,1)}), bf16[4096,1792]{1,0:T(8,128)(2,1)}) %all-gather.5.cloned.1.call-update) | async-done | bytes 14680080 | tf_op jit(solution)/shard_map/all_gather | solution.py:866
  129.3 6.8 dynamic-slice_bitcast_fusion
  136.0 13.8 %collective-permute-done.9 = bf16[272,1280]{1,0:T(8,128)(2,1)S(1)} collective-permute-done((bf16[272,1280]{1,0:T(8,128)(2,1)}, bf16[272,1280]{1,0:T(8,128)(2,1)S(1)}, u32[]{:S(2)}, u32[]{:S(2)}) %collective-permute-start.9) | collective-permute-done | bytes 696352 | tf_op jit(solution)/shard_map/ppermute | solution.py:70
  151.6 29.4 %all-reduce.10.cloned.1.call-done = bf16[256,2048]{1,0:T(8,128)(2,1)} async-done(((bf16[256,2048]{1,0:T(8,128)(2,1)}), bf16[256,2048]{1,0:T(8,128)(2,1)}) %all-reduce.10.cloned.1.call-update) | async-done | bytes 1048592 | tf_op jit(solution)/shard_map/psum | solution.py:404
  186.0 7.4 fusion.58
  235.0 25.3 %all-reduce.12.cloned.1.call-done = bf16[256,2048]{1,0:T(8,128)(2,1)} async-done(((bf16[256,2048]{1,0:T(8,128)(2,1)}), bf16[256,2048]{1,0:T(8,128)(2,1)}) %all-reduce.12.cloned.1.call-update) | async-done | bytes 1048592 | tf_op jit(solution)/shard_map/psum | solution.py:404
  290.5 12.4 %collective-permute-done.18 = bf16[512,512]{1,0:T(8,128)(2,1)S(1)} collective-permute-done((bf16[512,512]{1,0:T(8,128)(2,1)}, bf16[512,512]{1,0:T(8,128)(2,1)S(1)}, u32[]{:S(2)}, u32[]{:S(2)}) %collective-permute-start.18) | collective-permute-done | bytes 524320 | tf_op jit(solution)/shard_map/ppermute | solution.py:70
  308.9 7.6 %collective-permute-done.20 = bf16[512,256]{1,0:T(8,128)(2,1)S(1)} collective-permute-done((bf16[512,256]{1,0:T(8,128)(2,1)S(1)}, bf16[512,256]{1,0:T(8,128)(2,1)S(1)}, u32[]{:S(2)}, u32[]{:S(2)}) %collective-permute-start.20) | collective-permute-done | bytes 262176 | tf_op jit(solution)/shard_map/ppermute | solution.py:79
  317.9 8.2 %pad_maximum_fusion.1 = bf16[2048,2048]{1,0:T(8,128)(2,1)} fusion(bf16[2048,512]{1,0:T(8,128)(2,1)} %bitcast.46, bf16[2048,1536]{1,0:T(8,128)(2,1)} %all-gather.9.cloned.1.call-done), kind=kLoop, calls=%fused_computation.1 | loop fusion | flops 16777216 | bytes 16777216 | tf_op jit(solution)/shard_map/concatenate | solution.py:911
  326.1 10.2 %all-reduce.14.cloned.1.call-done = bf16[256,2048]{1,0:T(8,128)(2,1)} async-done(((bf16[256,2048]{1,0:T(8,128)(2,1)}), bf16[256,2048]{1,0:T(8,128)(2,1)}) %all-reduce.14.cloned.1.call-update) | async-done | bytes 1048592 | tf_op jit(solution)/shard_map/psum | solution.py:404
  341.9 10.0 %fusion.42 = f32[512,2048]{1,0:T(8,128)} fusion(bf16[2048,2048]{1,0:T(8,128)(2,1)} %pad_maximum_fusion.1, bf16[256,2048]{1,0:T(8,128)(2,1)S(1)} %collective-permute-done.22.refs_1_.refs_3_, bf16[256,2048]{1,0:T(8,128)(2,1)S(1)} %multiply_convert_fusion.5.refs_0_.refs_2_), kind=kOutput, calls=%fused_computation.81 | convolution fusion | flops 4299161600 | bytes 14680064 | tf_op jit(solution)/shard_map/dot_general | solution.py:368
  353.9 7.4 multiply_convert_fusion.4
  361.3 7.7 %fusion.46 = f32[512,2048]{1,0:T(8,128)S(1)} fusion(bf16[2048,2048]{1,0:T(8,128)(2,1)} %pad_maximum_fusion.1, bf16[512,1024]{1,0:T(8,128)(2,1)S(1)} %get-tuple-element.200.refs_3_, bf16[512,1024]{1,0:T(8,128)(2,1)S(1)} %get-tuple-element.199.refs_2_.refs_5_), kind=kOutput, calls=%fused_computation.85 | convolution fusion | flops 4299161600 | bytes 14680064 | tf_op jit(solution)/shard_map/dot_general | solution.py:380
  396.1 28.5 %all-reduce.16.cloned.1.call-done = bf16[256,2048]{1,0:T(8,128)(2,1)} async-done(((bf16[256,2048]{1,0:T(8,128)(2,1)}), bf16[256,2048]{1,0:T(8,128)(2,1)}) %all-reduce.16.cloned.1.call-update) | async-done | bytes 1048592 | tf_op jit(solution)/shard_map/psum | solution.py:404
  439.0 9.4 %collective-permute-done.24.back_ref = bf16[256,256]{1,0:T(8,128)(2,1)S(1)} collective-permute-done((bf16[256,256]{1,0:T(8,128)(2,1)S(1)}, bf16[256,256]{1,0:T(8,128)(2,1)S(1)}, u32[]{:S(2)}, u32[]{:S(2)}) %collective-permute-start.24) | collective-permute-done | bytes 131104 | tf_op jit(solution)/shard_map/ppermute | solution.py:29
  483.6 13.4 %collective-permute-done.26 = bf16[256,640]{1,0:T(8,128)(2,1)S(1)} collective-permute-done((bf16[256,640]{1,0:T(8,128)(2,1)S(1)}, bf16[256,640]{1,0:T(8,128)(2,1)S(1)}, u32[]{:S(2)}, u32[]{:S(2)}) %collective-permute-start.26) | collective-permute-done | bytes 327712 | tf_op jit(solution)/shard_map/ppermute | solution.py:104
  500.5 9.0 %all-reduce.18.cloned.1.call-done = bf16[256,2048]{1,0:T(8,128)(2,1)} async-done(((bf16[256,2048]{1,0:T(8,128)(2,1)}), bf16[256,2048]{1,0:T(8,128)(2,1)}) %all-reduce.18.cloned.1.call-update) | async-done | bytes 1048592 | tf_op jit(solution)/shard_map/psum | solution.py:404
  552.2 23.6 %collective-permute-done.32 = bf16[256,1280]{1,0:T(8,128)(2,1)S(1)} collective-permute-done((bf16[256,1280]{1,0:T(8,128)(2,1)}, bf16[256,1280]{1,0:T(8,128)(2,1)S(1)}, u32[]{:S(2)}, u32[]{:S(2)}) %collective-permute-start.32) | collective-permute-done | bytes 655392 | tf_op jit(solution)/shard_map/ppermute | solution.py:123
  605.4 9.3 %collective-permute-done.33.back_ref = bf16[256,256]{1,0:T(8,128)(2,1)S(1)} collective-permute-done((bf16[256,256]{1,0:T(8,128)(2,1)S(1)}, bf16[256,256]{1,0:T(8,128)(2,1)S(1)}, u32[]{:S(2)}, u32[]{:S(2)}) %collective-permute-start.33) | collective-permute-done | bytes 131104 | tf_op jit(solution)/shard_map/ppermute | solution.py:29
  638.5 15.1 %collective-permute-done.39 = bf16[256,640]{1,0:T(8,128)(2,1)S(1)} collective-permute-done((bf16[256,640]{1,0:T(8,128)(2,1)S(1)}, bf16[256,640]{1,0:T(8,128)(2,1)S(1)}, u32[]{:S(2)}, u32[]{:S(2)}) %collective-permute-start.39) | collective-permute-done | bytes 327712 | tf_op jit(solution)/shard_map/ppermute | solution.py:105
  662.5 22.4 %collective-permute-done.40 = bf16[256,1280]{1,0:T(8,128)(2,1)S(1)} collective-permute-done((bf16[256,1280]{1,0:T(8,128)(2,1)S(1)}, bf16[256,1280]{1,0:T(8,128)(2,1)S(1)}, u32[]{:S(2)}, u32[]{:S(2)}) %collective-permute-start.40) | collective-permute-done | bytes 655392 | tf_op jit(solution)/shard_map/ppermute | solution.py:123
  700.4 10.0 %all-reduce.22.cloned.1.call-done = (bf16[256,2048]{1,0:T(8,128)(2,1)}, bf16[256,2048]{1,0:T(8,128)(2,1)}) async-done(((bf16[256,2048]{1,0:T(8,128)(2,1)}, bf16[256,2048]{1,0:T(8,128)(2,1)}), (bf16[256,2048]{1,0:T(8,128)(2,1)}, bf16[256,2048]{1,0:T(8,128)(2,1)})) %all-reduce.22.cloned.1.call-update) | async-done | bytes 2097168 | tf_op jit(solution)/shard_map/psum | solution.py:404
  (554 shorter events, 402.4 us)
Async XLA Ops:
  8.0 118.2 %all-gather.5.cloned.1.call-start = ((), (), s32[]{:S(2)}) async-start(), calls=%async_computation.4 | async-start | bytes 16515072 | tf_op jit(solution)/shard_map/all_gather | solution.py:866
  23.5 157.5 %all-reduce.10.cloned.1.call-start = ((), (), s32[]{:S(2)}) async-start(), calls=%async_computation.5 | async-start | bytes 2097152 | tf_op jit(solution)/shard_map/psum | solution.py:404
  31.7 33.0 %collective-permute-start.1 = (bf16[272,1280]{1,0:T(8,128)(2,1)S(1)}, bf16[272,1280]{1,0:T(8,128)(2,1)S(1)}, u32[]{:S(2)}, u32[]{:S(2)}) collective-permute-start(bf16[272,1280]{1,0:T(8,128)(2,1)S(1)} %get-tuple-element.198), channel_id=1, source_target_pairs={{0,4},{4,12},{12,8},{8,0},{1,5},{5,13},{13,9},{9,1},{2,6},{6,14},{... | collective-permute-start | bytes 2088968 | tf_op jit(solution)/shard_map/ppermute | solution.py:70
  34.3 33.2 %collective-permute-start.2 = (bf16[272,1280]{1,0:T(8,128)(2,1)S(1)}, bf16[272,1280]{1,0:T(8,128)(2,1)S(1)}, u32[]{:S(2)}, u32[]{:S(2)}) collective-permute-start(bf16[272,1280]{1,0:T(8,128)(2,1)S(1)} %get-tuple-element.198), channel_id=1, source_target_pairs={{4,0},{12,4},{8,12},{0,8},{5,1},{13,5},{9,13},{1,9},{6,2},{14,6},{... | collective-permute-start | bytes 2088968 | tf_op jit(solution)/shard_map/ppermute | solution.py:71
  126.2 70.4 %all-gather.7.cloned.1.call-start = ((), (), s32[]{:S(2)}) async-start(), calls=%async_computation.6 | async-start | bytes 6553600 | tf_op jit(solution)/shard_map/all_gather | solution.py:860
  126.8 133.5 %all-reduce.12.cloned.1.call-start = ((), (), s32[]{:S(2)}) async-start(), calls=%async_computation.7 | async-start | bytes 2097152 | tf_op jit(solution)/shard_map/psum | solution.py:404
  208.7 75.5 %all-gather.9.cloned.1.call-start = ((), (), s32[]{:S(2)}) async-start(), calls=%async_computation.8 | async-start | bytes 7864320 | tf_op jit(solution)/shard_map/all_gather | solution.py:860
  210.1 126.3 %all-reduce.14.cloned.1.call-start = ((), (), s32[]{:S(2)}) async-start(), calls=%async_computation.9 | async-start | bytes 2097152 | tf_op jit(solution)/shard_map/psum | solution.py:404
  284.2 69.7 %all-gather.11.cloned.1.call-start = ((), (), s32[]{:S(2)}) async-start(), calls=%async_computation.10 | async-start | bytes 5242880 | tf_op jit(solution)/shard_map/all_gather | solution.py:860
  284.8 139.8 %all-reduce.16.cloned.1.call-start = ((), (), s32[]{:S(2)}) async-start(), calls=%async_computation.11 | async-start | bytes 2097152 | tf_op jit(solution)/shard_map/psum | solution.py:404
  288.2 38.0 %collective-permute-start.17 = (bf16[256,2048]{1,0:T(8,128)(2,1)S(1)}, bf16[256,2048]{1,0:T(8,128)(2,1)}, u32[]{:S(2)}, u32[]{:S(2)}) collective-permute-start(bf16[256,2048]{1,0:T(8,128)(2,1)S(1)} %add_convert_fusion.1.stream_ref.refs_0_), channel_id=1, source_target_pairs={{0,16},{16,0},{1,17},{17,1},{2,18},{18,2},{3,19},{19,3},{4,20},{20... | collective-permute-start | bytes 3145736 | tf_op jit(solution)/shard_map/ppermute | solution.py:23
  373.2 84.2 %reduce-scatter.5.cloned.1.call-start = ((), (), s32[]{:S(2)}) async-start(), calls=%async_computation.12 | async-start | bytes 7864320 | tf_op jit(solution)/shard_map/reduce_scatter | solution.py:762
  385.3 124.2 %all-reduce.18.cloned.1.call-start = ((), (), s32[]{:S(2)}) async-start(), calls=%async_computation.13 | async-start | bytes 2097152 | tf_op jit(solution)/shard_map/psum | solution.py:404
  457.5 81.2 %reduce-scatter.7.cloned.1.call-start = ((), (), s32[]{:S(2)}) async-start(), calls=%async_computation.14 | async-start | bytes 7864320 | tf_op jit(solution)/shard_map/reduce_scatter | solution.py:883
  458.2 132.7 %all-reduce.20.cloned.1.call-start = ((), (), s32[]{:S(2)}) async-start(), calls=%async_computation.15 | async-start | bytes 2097152 | tf_op jit(solution)/shard_map/psum | solution.py:404
  538.7 84.4 %reduce-scatter.11.cloned.1.call-start = ((), (), s32[]{:S(2)}) async-start(), calls=%async_computation.17 | async-start | bytes 6553600 | tf_op jit(solution)/shard_map/reduce_scatter | solution.py:762
  549.9 160.5 %all-reduce.22.cloned.1.call-start = ((), (), s32[]{:S(2)}) async-start(), calls=%async_computation.18 | async-start | bytes 4194304 | tf_op jit(solution)/shard_map/psum | solution.py:404
  551.3 27.1 %collective-permute-start.31 = (bf16[256,1280]{1,0:T(8,128)(2,1)}, bf16[256,1280]{1,0:T(8,128)(2,1)S(1)}, u32[]{:S(2)}, u32[]{:S(2)}) collective-permute-start(bf16[256,1280]{1,0:T(8,128)(2,1)} %pad_maximum_fusion.14), channel_id=1, source_target_pairs={{0,4},{4,12},{12,8},{8,0},{1,5},{5,13},{13,9},{9,1},{2,6},{6,14},{... | collective-permute-start | bytes 1966088 | tf_op jit(solution)/shard_map/ppermute | solution.py:122
  623.2 104.1 %reduce-scatter.9.cloned.1.call-start = ((), (), s32[]{:S(2)}) async-start(), calls=%async_computation.16 | async-start | bytes 9175040 | tf_op jit(solution)/shard_map/reduce_scatter | solution.py:883
  653.8 31.1 %collective-permute-start.40 = (bf16[256,1280]{1,0:T(8,128)(2,1)S(1)}, bf16[256,1280]{1,0:T(8,128)(2,1)S(1)}, u32[]{:S(2)}, u32[]{:S(2)}) collective-permute-start(bf16[256,1280]{1,0:T(8,128)(2,1)S(1)} %pad_maximum_fusion.17), channel_id=1, source_target_pairs={{4,0},{12,4},{8,12},{0,8},{5,1},{13,5},{9,13},{1,9},{6,2},{14,6},{... | collective-permute-start | bytes 1966088 | tf_op jit(solution)/shard_map/ppermute | solution.py:123
  655.5 31.0 %collective-permute-start.38 = (bf16[256,1280]{1,0:T(8,128)(2,1)S(1)}, bf16[256,1280]{1,0:T(8,128)(2,1)S(1)}, u32[]{:S(2)}, u32[]{:S(2)}) collective-permute-start(bf16[256,1280]{1,0:T(8,128)(2,1)S(1)} %pad_maximum_fusion.16), channel_id=1, source_target_pairs={{0,4},{4,12},{12,8},{8,0},{1,5},{5,13},{13,9},{9,1},{2,6},{6,14},{... | collective-permute-start | bytes 1966088 | tf_op jit(solution)/shard_map/ppermute | solution.py:122
  656.1 39.3 %collective-permute-start.35 = (bf16[512,1536]{1,0:T(8,128)(2,1)}, bf16[512,1536]{1,0:T(8,128)(2,1)}, u32[]{:S(2)}, u32[]{:S(2)}) collective-permute-start(bf16[512,1536]{1,0:T(8,128)(2,1)} %reduce-scatter.5.cloned.1.call-done.high_ref.refs_1_), channel_id=1, source_target_pairs={{0,16},{1,17},{2,18},{3,19},{4,20},{5,21},{6,22},{7,23},{8,24},{9,... | collective-permute-start | bytes 4718600 | tf_op jit(solution)/shard_map/ppermute | solution.py:889
  658.6 41.9 %collective-permute-start.42 = (bf16[512,1536]{1,0:T(8,128)(2,1)}, bf16[512,1536]{1,0:T(8,128)(2,1)}, u32[]{:S(2)}, u32[]{:S(2)}) collective-permute-start(bf16[512,1536]{1,0:T(8,128)(2,1)} %reduce-scatter.7.cloned.1.call-done.refs_5_), channel_id=1, source_target_pairs={{0,16},{1,17},{2,18},{3,19},{4,20},{5,21},{6,22},{7,23},{8,24},{9,... | collective-permute-start | bytes 4718600 | tf_op jit(solution)/shard_map/ppermute | solution.py:889
  661.0 34.5 %collective-permute-start.34 = (bf16[512,1280]{1,0:T(8,128)(2,1)}, bf16[512,1280]{1,0:T(8,128)(2,1)}, u32[]{:S(2)}, u32[]{:S(2)}) collective-permute-start(bf16[512,1280]{1,0:T(8,128)(2,1)} %reduce-scatter.11.cloned.1.call-done.low_ref.refs_0_), channel_id=1, source_target_pairs={{16,0},{17,1},{18,2},{19,3},{20,4},{21,5},{22,6},{23,7},{24,8},{25... | collective-permute-start | bytes 3932168 | tf_op jit(solution)/shard_map/ppermute | solution.py:886
  (176 other events, 1362.3 us)
Sparse Core Ops, SparseCore 0:
  23.6 102.5 all-gather.4
  129.1 51.7 all-reduce.9
  208.8 51.4 all-reduce.11
  284.3 51.9 all-reduce.13
  373.4 51.1 all-reduce.15
  457.6 51.8 all-reduce.17
  538.8 51.8 all-reduce.19
  623.3 87.0 all-reduce.21
Sparse Core Ops, SparseCore 1:
  129.3 66.9 all-gather.6
  211.8 72.4 all-gather.8
  287.3 59.5 all-gather.10
  385.3 72.1 reduce-scatter.4
  461.5 77.1 reduce-scatter.6
  550.0 73.1 reduce-scatter.10
  626.9 99.9 reduce-scatter.8

commit v7 on v6

--- a/solution.py
+++ b/solution.py
@@ -738,7 +738,9 @@
     both = jnp.concatenate([normed, got], axis=0)
     gate_up = [product(both, wide) for wide in wides]
     gate = gate_up[0][:, :hidden_width]
-    up = jnp.concatenate([gate_up[0][:, hidden_width:], *gate_up[1:]], axis=1)
+    if gate_up[0].shape[1] > hidden_width:
+        gate_up.insert(1, gate_up[0][:, hidden_width:])
+    up = jnp.concatenate(gate_up[1:], axis=1)
     hidden = (jax.nn.silu(gate) * up).astype(bf16)
     return (middle, inv_rms, normed, got, gate, up, hidden)
 
@@ -748,14 +750,17 @@
     return own_share(cols_product(hidden, down), middle.shape[0]).astype(bf16)
 
 
-def ffn_backward(own_grad, other_grad, state, wide, down, head, *others):
+def ffn_backward(own_grad, other_grad, state, wides, down, head, *others):
     middle, _, normed, got, gate, up, hidden = state
     hidden_grad = product(jnp.concatenate([own_grad, other_grad], axis=0), down)
     sigmoid_gate = jax.nn.sigmoid(gate)
     gate_grad = (hidden_grad * up * sigmoid_gate * (1.0 + gate * (1.0 - sigmoid_gate))).astype(bf16)
     up_grad = (hidden_grad * gate * sigmoid_gate).astype(bf16)
     units = gate.shape[1]
-    partial = cols_product(jnp.concatenate([gate_grad, up_grad], axis=1), wide)
+    if len(wides) == 1:
+        partial = cols_product(jnp.concatenate([gate_grad, up_grad], axis=1), wides[0])
+    else:
+        partial = cols_product(gate_grad, wides[0]) + cols_product(up_grad, wides[1])
     normed_grad, *others = sum_tensor(own_share(partial, middle.shape[0]), *others)
     own_sides, norm_sides = (own_grad, other_grad), (normed, got)
     early = token_terms([own_sides, norm_sides], [(0, hidden, 0, units), (1, gate_grad, 0, head)])
@@ -908,13 +913,17 @@
         out_low, gains_high[0], attn_high, place, wide_high, wide_parts[1][:, -ring_columns:]
     )
     wide_ring = ring_gather_start(wide_part_high)
-    wide_high = jnp.concatenate(
-        [wide_high, ring_gather(*wide_ring).reshape(width, ring_columns)], axis=1
-    )
+    up_high = jnp.concatenate(
+        [wide_high[:, half:], ring_gather(*wide_ring).reshape(width, ring_columns)], axis=1
+    )
+    wide_high = [wide_high[:, :half], up_high]
     total, got_out_low, wide_high = pin(total, swap_cores(out_low), wide_high)
     middle = attn_saved_high[0] + total.astype(f32)
-    state_high = ffn_forward_in(middle, gains_high[1], [wide_high], half)
-
+    state_high = ffn_forward_in(middle, gains_high[1], wide_high, half)
+
+    gate, up, down_high = pin(state_high[4], state_high[5], down_high)
+    hidden = (jax.nn.silu(gate) * up).astype(bf16)
+    state_high = (*state_high[:4], gate, up, hidden)
     normed_grad, early_high, late_high = ffn_backward(
         own_grad, other_grad, state_high, wide_high, down_high, half // 2
     )
@@ -932,7 +941,7 @@
     )
     got_boundary_high = swap_cores(boundary_high)
     normed_grad, early_low, late_low, late_high = ffn_backward(
-        boundary_high, got_boundary_high, state_low, wide_low, down_low, half // 4, late_high
+        boundary_high, got_boundary_high, state_low, [wide_low], down_low, half // 4, late_high
     )
     normed_grad, late_low, attn_share_high = pin(normed_grad, late_low, ring_scatter(*attn_ring))
     mid_grad, ffn_gain_low = ffn_backward_out(

time: 762 us -> 757 us (level)
  matrix products: 52.2 us -> 44 us
    dot_general x5 -> x6, matrix products: 32.6 us -> 27.3 us  [product(): lax.dot_general(left, right, (((1,), (0,)), ((), ())), preferred_element_...]
    dot_general x4 -> x5, matrix products: 19.7 us -> 16.8 us  [cols_product(): lax.dot_general(left, right, (((1,), (1,)), ((), ())), preferred_element_...]
    unnamed x274 -> x288, local copies, waits for them, and re-layouts: 67.8 us -> 70.6 us
  transfers between devices with their start and end apart: 65 -> 65, of which waited for: 46 -> 46; matrix products, arithmetic and copies ran while one was open for 19% -> 18% of each run, Pallas kernels for 9% -> 9%
where the time goes in v7:
time: 757 us; the launch traced here: 745 us
  waiting for transfers between devices  367 us (48%)
  local copies, waits for them, and re-layouts  118 us (16%)
  other arithmetic  74.7 us (10%)
  Pallas kernels  72.1 us (10%)
  starting transfers between devices  51.1 us (7%)
  matrix products  44 us (6%)
  between operations  17.7 us (2%)
    psum x7, waiting for transfers between devices, sum_tensor(): return (lax.psum(partial, 'tensor'), *others)  116 us
    unnamed x288, local copies, waits for them, and re-layouts  70.6 us
    ppermute x3, waiting for transfers between devices, ring_gather_start(): from_back.append(lax.ppermute(from_back[-1], 'ctx', ahead))  48.1 us
    ppermute x2, waiting for transfers between devices, ring_scatter(): from_front = lax.ppermute(to_back, 'ctx', behind)  46 us
    ppermute x19, waiting for transfers between devices, swap_cores(): return lax.ppermute(block, 'pipe', [(0, 1), (1, 0)])  34.6 us
    ppermute x4, waiting for transfers between devices, from_behind(): return lax.ppermute(block, axis, route)  27.5 us
    dot_general x6, matrix products, product(): lax.dot_general(left, right, (((1,), (0,)), ((), ())), preferred_element_...  27.3 us
    ppermute x3, waiting for transfers between devices, ring_gather(): left = lax.ppermute(from_back[-1][:, :half], 'ctx', ahead)  21.1 us
  transfers between devices with their start and end apart: 65, of which 46 were waited for; matrix products, arithmetic and copies ran while one was open for 18% of the time, Pallas kernels for 9%

profile of v7, /device:TPU:0, one launch (start us, length us, event | category | flops | bytes accessed | tf_op | source)
XLA Modules:
  0.0 745.1 jit_solution(13205034637426196993)
XLA Ops:
  37.8 26.7 %collective-permute-done.1 = bf16[272,1280]{1,0:T(8,128)(2,1)S(1)} collective-permute-done((bf16[272,1280]{1,0:T(8,128)(2,1)S(1)}, bf16[272,1280]{1,0:T(8,128)(2,1)S(1)}, u32[]{:S(2)}, u32[]{:S(2)}) %collective-permute-start.1) | collective-permute-done | bytes 696352 | tf_op jit(solution)/shard_map/ppermute | solution.py:70
  69.0 8.6 %collective-permute-done.3 = bf16[272,640]{1,0:T(8,128)(2,1)S(1)} collective-permute-done((bf16[272,640]{1,0:T(8,128)(2,1)S(1)}, bf16[272,640]{1,0:T(8,128)(2,1)S(1)}, u32[]{:S(2)}, u32[]{:S(2)}) %collective-permute-start.3) | collective-permute-done | bytes 348192 | tf_op jit(solution)/shard_map/ppermute | solution.py:79
  109.1 6.2 mix.2
  118.0 8.6 %all-gather.5.cloned.1.call-done = bf16[4096,1792]{1,0:T(8,128)(2,1)} async-done(((bf16[512,1792]{1,0:T(8,128)(2,1)}), bf16[4096,1792]{1,0:T(8,128)(2,1)}) %all-gather.5.cloned.1.call-update) | async-done | bytes 14680080 | tf_op jit(solution)/shard_map/all_gather | solution.py:871
  129.6 6.5 dynamic-slice_bitcast_fusion
  136.1 14.2 %collective-permute-done.9 = bf16[272,1280]{1,0:T(8,128)(2,1)} collective-permute-done((bf16[272,1280]{1,0:T(8,128)(2,1)}, bf16[272,1280]{1,0:T(8,128)(2,1)}, u32[]{:S(2)}, u32[]{:S(2)}) %collective-permute-start.9) | collective-permute-done | bytes 696352 | tf_op jit(solution)/shard_map/ppermute | solution.py:70
  151.9 29.5 %all-reduce.10.cloned.1.call-done = bf16[256,2048]{1,0:T(8,128)(2,1)} async-done(((bf16[256,2048]{1,0:T(8,128)(2,1)}), bf16[256,2048]{1,0:T(8,128)(2,1)}) %all-reduce.10.cloned.1.call-update) | async-done | bytes 1048592 | tf_op jit(solution)/shard_map/psum | solution.py:404
  186.9 7.4 fusion.52
  238.6 22.3 %all-reduce.12.cloned.1.call-done = bf16[256,2048]{1,0:T(8,128)(2,1)} async-done(((bf16[256,2048]{1,0:T(8,128)(2,1)}), bf16[256,2048]{1,0:T(8,128)(2,1)}) %all-reduce.12.cloned.1.call-update) | async-done | bytes 1048592 | tf_op jit(solution)/shard_map/psum | solution.py:404
  294.0 7.1 collective-permute-done.18
  306.2 8.9 %collective-permute-done.20 = bf16[512,256]{1,0:T(8,128)(2,1)S(1)} collective-permute-done((bf16[512,256]{1,0:T(8,128)(2,1)S(1)}, bf16[512,256]{1,0:T(8,128)(2,1)S(1)}, u32[]{:S(2)}, u32[]{:S(2)}) %collective-permute-start.20) | collective-permute-done | bytes 262176 | tf_op jit(solution)/shard_map/ppermute | solution.py:79
  320.6 16.9 %all-reduce.14.cloned.1.call-done = bf16[256,2048]{1,0:T(8,128)(2,1)} async-done(((bf16[256,2048]{1,0:T(8,128)(2,1)}), bf16[256,2048]{1,0:T(8,128)(2,1)}) %all-reduce.14.cloned.1.call-update) | async-done | bytes 1048592 | tf_op jit(solution)/shard_map/psum | solution.py:404
  390.3 28.4 %all-reduce.16.cloned.1.call-done = bf16[256,2048]{1,0:T(8,128)(2,1)} async-done(((bf16[256,2048]{1,0:T(8,128)(2,1)}), bf16[256,2048]{1,0:T(8,128)(2,1)}) %all-reduce.16.cloned.1.call-update) | async-done | bytes 1048592 | tf_op jit(solution)/shard_map/psum | solution.py:404
  424.4 6.5 mix_back.2
  433.2 9.4 %collective-permute-done.24.back_ref = bf16[256,256]{1,0:T(8,128)(2,1)S(1)} collective-permute-done((bf16[256,256]{1,0:T(8,128)(2,1)S(1)}, bf16[256,256]{1,0:T(8,128)(2,1)S(1)}, u32[]{:S(2)}, u32[]{:S(2)}) %collective-permute-start.24) | collective-permute-done | bytes 131104 | tf_op jit(solution)/shard_map/ppermute | solution.py:29
  477.8 13.4 %collective-permute-done.26 = bf16[256,640]{1,0:T(8,128)(2,1)S(1)} collective-permute-done((bf16[256,640]{1,0:T(8,128)(2,1)S(1)}, bf16[256,640]{1,0:T(8,128)(2,1)S(1)}, u32[]{:S(2)}, u32[]{:S(2)}) %collective-permute-start.26) | collective-permute-done | bytes 327712 | tf_op jit(solution)/shard_map/ppermute | solution.py:104
  494.8 8.9 %all-reduce.18.cloned.1.call-done = bf16[256,2048]{1,0:T(8,128)(2,1)} async-done(((bf16[256,2048]{1,0:T(8,128)(2,1)}), bf16[256,2048]{1,0:T(8,128)(2,1)}) %all-reduce.18.cloned.1.call-update) | async-done | bytes 1048592 | tf_op jit(solution)/shard_map/psum | solution.py:404
  546.4 23.6 %collective-permute-done.32 = bf16[256,1280]{1,0:T(8,128)(2,1)S(1)} collective-permute-done((bf16[256,1280]{1,0:T(8,128)(2,1)}, bf16[256,1280]{1,0:T(8,128)(2,1)S(1)}, u32[]{:S(2)}, u32[]{:S(2)}) %collective-permute-start.32) | collective-permute-done | bytes 655392 | tf_op jit(solution)/shard_map/ppermute | solution.py:123
  591.5 6.5 mix_back.3
  600.3 9.3 %collective-permute-done.33.back_ref = bf16[256,256]{1,0:T(8,128)(2,1)S(1)} collective-permute-done((bf16[256,256]{1,0:T(8,128)(2,1)S(1)}, bf16[256,256]{1,0:T(8,128)(2,1)S(1)}, u32[]{:S(2)}, u32[]{:S(2)}) %collective-permute-start.33) | collective-permute-done | bytes 131104 | tf_op jit(solution)/shard_map/ppermute | solution.py:29
  632.8 15.1 %collective-permute-done.39 = bf16[256,640]{1,0:T(8,128)(2,1)S(1)} collective-permute-done((bf16[256,640]{1,0:T(8,128)(2,1)S(1)}, bf16[256,640]{1,0:T(8,128)(2,1)S(1)}, u32[]{:S(2)}, u32[]{:S(2)}) %collective-permute-start.39) | collective-permute-done | bytes 327712 | tf_op jit(solution)/shard_map/ppermute | solution.py:105
  656.8 22.4 %collective-permute-done.40 = bf16[256,1280]{1,0:T(8,128)(2,1)S(1)} collective-permute-done((bf16[256,1280]{1,0:T(8,128)(2,1)S(1)}, bf16[256,1280]{1,0:T(8,128)(2,1)S(1)}, u32[]{:S(2)}, u32[]{:S(2)}) %collective-permute-start.40) | collective-permute-done | bytes 655392 | tf_op jit(solution)/shard_map/ppermute | solution.py:123
  694.7 9.9 %all-reduce.22.cloned.1.call-done = (bf16[256,2048]{1,0:T(8,128)(2,1)}, bf16[256,2048]{1,0:T(8,128)(2,1)}) async-done(((bf16[256,2048]{1,0:T(8,128)(2,1)}, bf16[256,2048]{1,0:T(8,128)(2,1)}), (bf16[256,2048]{1,0:T(8,128)(2,1)}, bf16[256,2048]{1,0:T(8,128)(2,1)})) %all-reduce.22.cloned.1.call-update) | async-done | bytes 2097168 | tf_op jit(solution)/shard_map/psum | solution.py:404
  731.3 6.1 wide_outputs.1
  (574 shorter events, 404.7 us)
Async XLA Ops:
  8.0 118.6 %all-gather.5.cloned.1.call-start = ((), (), s32[]{:S(2)}) async-start(), calls=%async_computation.4 | async-start | bytes 16515072 | tf_op jit(solution)/shard_map/all_gather | solution.py:871
  23.5 157.8 %all-reduce.10.cloned.1.call-start = ((), (), s32[]{:S(2)}) async-start(), calls=%async_computation.5 | async-start | bytes 2097152 | tf_op jit(solution)/shard_map/psum | solution.py:404
  31.7 32.8 %collective-permute-start.1 = (bf16[272,1280]{1,0:T(8,128)(2,1)S(1)}, bf16[272,1280]{1,0:T(8,128)(2,1)S(1)}, u32[]{:S(2)}, u32[]{:S(2)}) collective-permute-start(bf16[272,1280]{1,0:T(8,128)(2,1)S(1)} %get-tuple-element.206), channel_id=1, source_target_pairs={{0,4},{4,12},{12,8},{8,0},{1,5},{5,13},{13,9},{9,1},{2,6},{6,14},{... | collective-permute-start | bytes 2088968 | tf_op jit(solution)/shard_map/ppermute | solution.py:70
  34.3 32.8 %collective-permute-start.2 = (bf16[272,1280]{1,0:T(8,128)(2,1)S(1)}, bf16[272,1280]{1,0:T(8,128)(2,1)S(1)}, u32[]{:S(2)}, u32[]{:S(2)}) collective-permute-start(bf16[272,1280]{1,0:T(8,128)(2,1)S(1)} %get-tuple-element.206), channel_id=1, source_target_pairs={{4,0},{12,4},{8,12},{0,8},{5,1},{13,5},{9,13},{1,9},{6,2},{14,6},{... | collective-permute-start | bytes 2088968 | tf_op jit(solution)/shard_map/ppermute | solution.py:71
  126.6 70.9 %all-gather.7.cloned.1.call-start = ((), (), s32[]{:S(2)}) async-start(), calls=%async_computation.6 | async-start | bytes 6553600 | tf_op jit(solution)/shard_map/all_gather | solution.py:865
  127.2 133.8 %all-reduce.12.cloned.1.call-start = ((), (), s32[]{:S(2)}) async-start(), calls=%async_computation.7 | async-start | bytes 2097152 | tf_op jit(solution)/shard_map/psum | solution.py:404
  209.6 75.9 %all-gather.9.cloned.1.call-start = ((), (), s32[]{:S(2)}) async-start(), calls=%async_computation.8 | async-start | bytes 7864320 | tf_op jit(solution)/shard_map/all_gather | solution.py:865
  211.0 126.6 %all-reduce.14.cloned.1.call-start = ((), (), s32[]{:S(2)}) async-start(), calls=%async_computation.9 | async-start | bytes 2097152 | tf_op jit(solution)/shard_map/psum | solution.py:404
  285.5 65.1 %all-gather.11.cloned.1.call-start = ((), (), s32[]{:S(2)}) async-start(), calls=%async_computation.10 | async-start | bytes 5242880 | tf_op jit(solution)/shard_map/all_gather | solution.py:865
  286.1 132.6 %all-reduce.16.cloned.1.call-start = ((), (), s32[]{:S(2)}) async-start(), calls=%async_computation.11 | async-start | bytes 2097152 | tf_op jit(solution)/shard_map/psum | solution.py:404
  288.3 31.3 %collective-permute-start.17 = (bf16[256,2048]{1,0:T(8,128)(2,1)S(1)}, bf16[256,2048]{1,0:T(8,128)(2,1)S(1)}, u32[]{:S(2)}, u32[]{:S(2)}) collective-permute-start(bf16[256,2048]{1,0:T(8,128)(2,1)S(1)} %add_convert_fusion.1.stream_ref.refs_0_), channel_id=1, source_target_pairs={{0,16},{16,0},{1,17},{17,1},{2,18},{18,2},{3,19},{19,3},{4,20},{20... | collective-permute-start | bytes 3145736 | tf_op jit(solution)/shard_map/ppermute | solution.py:23
  367.4 84.3 %reduce-scatter.5.cloned.1.call-start = ((), (), s32[]{:S(2)}) async-start(), calls=%async_computation.12 | async-start | bytes 7864320 | tf_op jit(solution)/shard_map/reduce_scatter | solution.py:767
  379.4 124.2 %all-reduce.18.cloned.1.call-start = ((), (), s32[]{:S(2)}) async-start(), calls=%async_computation.13 | async-start | bytes 2097152 | tf_op jit(solution)/shard_map/psum | solution.py:404
  451.7 81.2 %reduce-scatter.7.cloned.1.call-start = ((), (), s32[]{:S(2)}) async-start(), calls=%async_computation.14 | async-start | bytes 7864320 | tf_op jit(solution)/shard_map/reduce_scatter | solution.py:888
  452.4 132.8 %all-reduce.20.cloned.1.call-start = ((), (), s32[]{:S(2)}) async-start(), calls=%async_computation.15 | async-start | bytes 2097152 | tf_op jit(solution)/shard_map/psum | solution.py:404
  532.9 84.5 %reduce-scatter.11.cloned.1.call-start = ((), (), s32[]{:S(2)}) async-start(), calls=%async_computation.17 | async-start | bytes 6553600 | tf_op jit(solution)/shard_map/reduce_scatter | solution.py:767
  544.2 160.4 %all-reduce.22.cloned.1.call-start = ((), (), s32[]{:S(2)}) async-start(), calls=%async_computation.18 | async-start | bytes 4194304 | tf_op jit(solution)/shard_map/psum | solution.py:404
  545.6 27.1 %collective-permute-start.31 = (bf16[256,1280]{1,0:T(8,128)(2,1)}, bf16[256,1280]{1,0:T(8,128)(2,1)S(1)}, u32[]{:S(2)}, u32[]{:S(2)}) collective-permute-start(bf16[256,1280]{1,0:T(8,128)(2,1)} %pad_maximum_fusion.17), channel_id=1, source_target_pairs={{0,4},{4,12},{12,8},{8,0},{1,5},{5,13},{13,9},{9,1},{2,6},{6,14},{... | collective-permute-start | bytes 1966088 | tf_op jit(solution)/shard_map/ppermute | solution.py:122
  617.4 103.9 %reduce-scatter.9.cloned.1.call-start = ((), (), s32[]{:S(2)}) async-start(), calls=%async_computation.16 | async-start | bytes 9175040 | tf_op jit(solution)/shard_map/reduce_scatter | solution.py:888
  648.1 31.1 %collective-permute-start.40 = (bf16[256,1280]{1,0:T(8,128)(2,1)S(1)}, bf16[256,1280]{1,0:T(8,128)(2,1)S(1)}, u32[]{:S(2)}, u32[]{:S(2)}) collective-permute-start(bf16[256,1280]{1,0:T(8,128)(2,1)S(1)} %pad_maximum_fusion.20), channel_id=1, source_target_pairs={{4,0},{12,4},{8,12},{0,8},{5,1},{13,5},{9,13},{1,9},{6,2},{14,6},{... | collective-permute-start | bytes 1966088 | tf_op jit(solution)/shard_map/ppermute | solution.py:123
  649.8 31.0 %collective-permute-start.38 = (bf16[256,1280]{1,0:T(8,128)(2,1)S(1)}, bf16[256,1280]{1,0:T(8,128)(2,1)S(1)}, u32[]{:S(2)}, u32[]{:S(2)}) collective-permute-start(bf16[256,1280]{1,0:T(8,128)(2,1)S(1)} %pad_maximum_fusion.19), channel_id=1, source_target_pairs={{0,4},{4,12},{12,8},{8,0},{1,5},{5,13},{13,9},{9,1},{2,6},{6,14},{... | collective-permute-start | bytes 1966088 | tf_op jit(solution)/shard_map/ppermute | solution.py:122
  650.4 39.3 %collective-permute-start.35 = (bf16[512,1536]{1,0:T(8,128)(2,1)}, bf16[512,1536]{1,0:T(8,128)(2,1)}, u32[]{:S(2)}, u32[]{:S(2)}) collective-permute-start(bf16[512,1536]{1,0:T(8,128)(2,1)} %reduce-scatter.5.cloned.1.call-done.high_ref.refs_1_), channel_id=1, source_target_pairs={{0,16},{1,17},{2,18},{3,19},{4,20},{5,21},{6,22},{7,23},{8,24},{9,... | collective-permute-start | bytes 4718600 | tf_op jit(solution)/shard_map/ppermute | solution.py:894
  652.9 41.8 %collective-permute-start.42 = (bf16[512,1536]{1,0:T(8,128)(2,1)}, bf16[512,1536]{1,0:T(8,128)(2,1)}, u32[]{:S(2)}, u32[]{:S(2)}) collective-permute-start(bf16[512,1536]{1,0:T(8,128)(2,1)} %reduce-scatter.7.cloned.1.call-done.refs_5_), channel_id=1, source_target_pairs={{0,16},{1,17},{2,18},{3,19},{4,20},{5,21},{6,22},{7,23},{8,24},{9,... | collective-permute-start | bytes 4718600 | tf_op jit(solution)/shard_map/ppermute | solution.py:894
  655.3 34.4 %collective-permute-start.34 = (bf16[512,1280]{1,0:T(8,128)(2,1)}, bf16[512,1280]{1,0:T(8,128)(2,1)}, u32[]{:S(2)}, u32[]{:S(2)}) collective-permute-start(bf16[512,1280]{1,0:T(8,128)(2,1)} %reduce-scatter.11.cloned.1.call-done.low_ref.refs_0_), channel_id=1, source_target_pairs={{16,0},{17,1},{18,2},{19,3},{20,4},{21,5},{22,6},{23,7},{24,8},{25... | collective-permute-start | bytes 3932168 | tf_op jit(solution)/shard_map/ppermute | solution.py:891
  (184 other events, 1335.2 us)
Sparse Core Ops, SparseCore 0:
  23.7 102.8 all-gather.4
  129.5 51.7 all-reduce.9
  209.7 51.1 all-reduce.11
  285.7 51.8 all-reduce.13
  367.5 51.1 all-reduce.15
  451.8 51.8 all-reduce.17
  533.0 51.8 all-reduce.19
  617.5 87.0 all-reduce.21
Sparse Core Ops, SparseCore 1:
  129.6 66.9 all-gather.6
  212.7 72.8 all-gather.8
  288.6 58.9 all-gather.10
  379.5 72.1 reduce-scatter.4
  455.7 77.1 reduce-scatter.6
  544.2 73.1 reduce-scatter.10
  621.2 99.9 reduce-scatter.8

commit v8 on v7

--- a/solution.py
+++ b/solution.py
@@ -867,7 +867,7 @@
     attn_parts = for_sections(attn_keep, attn_got)
     wide_parts = for_sections(wide_keep, wide_got)
     down_parts = for_sections(down_keep, down_got)
-    tail_columns = half // 4
+    tail_columns = 3 * half // 8
     wide_low = lax.all_gather(
         wide_parts[0][:, :-tail_columns], ("pipe", "ctx"), axis=0, tiled=True
     )
@@ -877,7 +877,7 @@
     )
     attn_low, gains_low = attn_weights(attn_pieces)
     down_and_tail = gather(down_parts[0])
-    ring_columns = wide_parts[1].shape[1] // 4
+    ring_columns = 3 * wide_parts[1].shape[1] // 8
     wide_high = gather(wide_parts[1][:, :-ring_columns])
     down_high = gather(down_parts[1])
 
@@ -898,12 +898,13 @@
         stream, gains_low[0], attn_low, place, wide_low, attn_parts[1]
     )
     wide_low = pick(wide_low.reshape(2, width, -1), core)
-    total, wide_low, attn_ring = pin(total, wide_low, ring_gather_start(attn_part_high))
+    total, wide_low = pin(total, wide_low)
     middle = attn_saved_low[0] + total.astype(f32)
     down_low, wide_tail = down_and_tail[:, :half], down_and_tail[:, half:]
     state_low = ffn_forward_in(middle, gains_low[1], [wide_low, wide_tail], half)
     own_grad, other_grad = pick(out_grad, core), pick(out_grad, 1 - core)
-    (total,) = sum_tensor(ffn_share(state_low, down_low))
+    total, attn_part_high = sum_tensor(ffn_share(state_low, down_low), attn_part_high)
+    attn_ring = ring_gather_start(attn_part_high)
     wide_low = jnp.concatenate([wide_low, wide_tail], axis=1)
     total, own_grad, other_grad, (attn_high, gains_high), wide_low = pin(
         total, own_grad, other_grad, attn_weights(ring_gather(*attn_ring)), wide_low

time: 757 us -> 750 us (level)
    ppermute x3, waiting for transfers between devices: 48.1 us -> 68.7 us  [ring_gather_start(): from_back.append(lax.ppermute(from_back[-1], 'ctx', ahead))]
    psum x7, waiting for transfers between devices: 116 us -> 104 us  [sum_tensor(): return (lax.psum(partial, 'tensor'), *others)]
    unnamed x288 -> x292, local copies, waits for them, and re-layouts: 70.6 us -> 70.4 us
  transfers between devices with their start and end apart: 65 -> 65, of which waited for: 46 -> 45; matrix products, arithmetic and copies ran while one was open for 18% -> 17% of each run, Pallas kernels for 9% -> 9%
where the time goes in v8:
time: 750 us; the launch traced here: 739 us
  waiting for transfers between devices  372 us (50%)
  local copies, waits for them, and re-layouts  112 us (15%)
  Pallas kernels  72 us (10%)
  other arithmetic  70.1 us (9%)
  starting transfers between devices  49.8 us (7%)
  matrix products  44.7 us (6%)
  between operations  17.8 us (2%)
    psum x7, waiting for transfers between devices, sum_tensor(): return (lax.psum(partial, 'tensor'), *others)  104 us
    unnamed x292, local copies, waits for them, and re-layouts  70.4 us
    ppermute x3, waiting for transfers between devices, ring_gather_start(): from_back.append(lax.ppermute(from_back[-1], 'ctx', ahead))  68.7 us
    ppermute x2, waiting for transfers between devices, ring_scatter(): from_front = lax.ppermute(to_back, 'ctx', behind)  46 us
    ppermute x19, waiting for transfers between devices, swap_cores(): return lax.ppermute(block, 'pipe', [(0, 1), (1, 0)])  31.3 us
    dot_general x6, matrix products, product(): lax.dot_general(left, right, (((1,), (0,)), ((), ())), preferred_element_...  27.8 us
    ppermute x3, waiting for transfers between devices, ring_gather(): left = lax.ppermute(from_back[-1][:, :half], 'ctx', ahead)  27.7 us
    ppermute x4, waiting for transfers between devices, from_behind(): return lax.ppermute(block, axis, route)  27.5 us
  transfers between devices with their start and end apart: 65, of which 45 were waited for; matrix products, arithmetic and copies ran while one was open for 17% of the time, Pallas kernels for 9%

profile of v8, /device:TPU:0, one launch (start us, length us, event | category | flops | bytes accessed | tf_op | source)
XLA Modules:
  0.0 738.7 jit_solution(117929697609451917)
XLA Ops:
  38.4 27.6 %collective-permute-done.1 = bf16[272,1280]{1,0:T(8,128)(2,1)S(1)} collective-permute-done((bf16[272,1280]{1,0:T(8,128)(2,1)S(1)}, bf16[272,1280]{1,0:T(8,128)(2,1)S(1)}, u32[]{:S(2)}, u32[]{:S(2)}) %collective-permute-start.1) | collective-permute-done | bytes 696352 | tf_op jit(solution)/shard_map/ppermute | solution.py:70
  68.4 8.4 %collective-permute-done.3 = bf16[272,640]{1,0:T(8,128)(2,1)S(1)} collective-permute-done((bf16[272,640]{1,0:T(8,128)(2,1)S(1)}, bf16[272,640]{1,0:T(8,128)(2,1)S(1)}, u32[]{:S(2)}, u32[]{:S(2)}) %collective-permute-start.3) | collective-permute-done | bytes 348192 | tf_op jit(solution)/shard_map/ppermute | solution.py:79
  101.7 6.2 mix.2
  110.6 8.0 %all-gather.5.cloned.1.call-done = bf16[4096,1664]{1,0:T(8,128)(2,1)} async-done(((bf16[512,1664]{1,0:T(8,128)(2,1)}), bf16[4096,1664]{1,0:T(8,128)(2,1)}) %all-gather.5.cloned.1.call-update) | async-done | bytes 13631504 | tf_op jit(solution)/shard_map/all_gather | solution.py:871
  119.6 6.3 dynamic-slice_bitcast_fusion
  125.8 47.8 %all-reduce.10.cloned.1.call-done = bf16[256,2048]{1,0:T(8,128)(2,1)} async-done(((bf16[256,2048]{1,0:T(8,128)(2,1)}), bf16[256,2048]{1,0:T(8,128)(2,1)}) %all-reduce.10.cloned.1.call-update) | async-done | bytes 1048592 | tf_op jit(solution)/shard_map/psum | solution.py:404
  179.1 7.3 fusion.52
  204.4 22.0 %collective-permute-done.11 = bf16[272,1280]{1,0:T(8,128)(2,1)S(1)} collective-permute-done((bf16[272,1280]{1,0:T(8,128)(2,1)S(1)}, bf16[272,1280]{1,0:T(8,128)(2,1)S(1)}, u32[]{:S(2)}, u32[]{:S(2)}) %collective-permute-start.11) | collective-permute-done | bytes 696352 | tf_op jit(solution)/shard_map/ppermute | solution.py:70
  230.1 11.2 %collective-permute-done.13 = bf16[272,640]{1,0:T(8,128)(2,1)S(1)} collective-permute-done((bf16[272,640]{1,0:T(8,128)(2,1)S(1)}, bf16[272,640]{1,0:T(8,128)(2,1)S(1)}, u32[]{:S(2)}, u32[]{:S(2)}) %collective-permute-start.13) | collective-permute-done | bytes 348192 | tf_op jit(solution)/shard_map/ppermute | solution.py:79
  287.3 19.1 %collective-permute-done.18 = bf16[512,768]{1,0:T(8,128)(2,1)S(1)} collective-permute-done((bf16[512,768]{1,0:T(8,128)(2,1)}, bf16[512,768]{1,0:T(8,128)(2,1)S(1)}, u32[]{:S(2)}, u32[]{:S(2)}) %collective-permute-start.18) | collective-permute-done | bytes 786464 | tf_op jit(solution)/shard_map/ppermute | solution.py:70
  310.5 8.0 %collective-permute-done.20 = bf16[512,384]{1,0:T(8,128)(2,1)S(1)} collective-permute-done((bf16[512,384]{1,0:T(8,128)(2,1)S(1)}, bf16[512,384]{1,0:T(8,128)(2,1)S(1)}, u32[]{:S(2)}, u32[]{:S(2)}) %collective-permute-start.20) | collective-permute-done | bytes 393248 | tf_op jit(solution)/shard_map/ppermute | solution.py:79
  322.5 8.3 %all-reduce.14.cloned.1.call-done = bf16[256,2048]{1,0:T(8,128)(2,1)} async-done(((bf16[256,2048]{1,0:T(8,128)(2,1)}), bf16[256,2048]{1,0:T(8,128)(2,1)}) %all-reduce.14.cloned.1.call-update) | async-done | bytes 1048592 | tf_op jit(solution)/shard_map/psum | solution.py:404
  383.5 28.8 %all-reduce.16.cloned.1.call-done = bf16[256,2048]{1,0:T(8,128)(2,1)} async-done(((bf16[256,2048]{1,0:T(8,128)(2,1)}), bf16[256,2048]{1,0:T(8,128)(2,1)}) %all-reduce.16.cloned.1.call-update) | async-done | bytes 1048592 | tf_op jit(solution)/shard_map/psum | solution.py:404
  418.0 6.5 mix_back.2
  426.8 9.4 %collective-permute-done.24.back_ref = bf16[256,256]{1,0:T(8,128)(2,1)S(1)} collective-permute-done((bf16[256,256]{1,0:T(8,128)(2,1)S(1)}, bf16[256,256]{1,0:T(8,128)(2,1)S(1)}, u32[]{:S(2)}, u32[]{:S(2)}) %collective-permute-start.24) | collective-permute-done | bytes 131104 | tf_op jit(solution)/shard_map/ppermute | solution.py:29
  471.3 13.4 %collective-permute-done.26 = bf16[256,640]{1,0:T(8,128)(2,1)S(1)} collective-permute-done((bf16[256,640]{1,0:T(8,128)(2,1)S(1)}, bf16[256,640]{1,0:T(8,128)(2,1)S(1)}, u32[]{:S(2)}, u32[]{:S(2)}) %collective-permute-start.26) | collective-permute-done | bytes 327712 | tf_op jit(solution)/shard_map/ppermute | solution.py:104
  488.3 8.9 %all-reduce.18.cloned.1.call-done = bf16[256,2048]{1,0:T(8,128)(2,1)} async-done(((bf16[256,2048]{1,0:T(8,128)(2,1)}), bf16[256,2048]{1,0:T(8,128)(2,1)}) %all-reduce.18.cloned.1.call-update) | async-done | bytes 1048592 | tf_op jit(solution)/shard_map/psum | solution.py:404
  540.0 23.6 %collective-permute-done.32 = bf16[256,1280]{1,0:T(8,128)(2,1)S(1)} collective-permute-done((bf16[256,1280]{1,0:T(8,128)(2,1)}, bf16[256,1280]{1,0:T(8,128)(2,1)S(1)}, u32[]{:S(2)}, u32[]{:S(2)}) %collective-permute-start.32) | collective-permute-done | bytes 655392 | tf_op jit(solution)/shard_map/ppermute | solution.py:123
  585.0 6.5 mix_back.3
  593.8 9.3 %collective-permute-done.33.back_ref = bf16[256,256]{1,0:T(8,128)(2,1)S(1)} collective-permute-done((bf16[256,256]{1,0:T(8,128)(2,1)S(1)}, bf16[256,256]{1,0:T(8,128)(2,1)S(1)}, u32[]{:S(2)}, u32[]{:S(2)}) %collective-permute-start.33) | collective-permute-done | bytes 131104 | tf_op jit(solution)/shard_map/ppermute | solution.py:29
  626.3 15.1 %collective-permute-done.39 = bf16[256,640]{1,0:T(8,128)(2,1)S(1)} collective-permute-done((bf16[256,640]{1,0:T(8,128)(2,1)S(1)}, bf16[256,640]{1,0:T(8,128)(2,1)S(1)}, u32[]{:S(2)}, u32[]{:S(2)}) %collective-permute-start.39) | collective-permute-done | bytes 327712 | tf_op jit(solution)/shard_map/ppermute | solution.py:105
  650.4 22.4 %collective-permute-done.40 = bf16[256,1280]{1,0:T(8,128)(2,1)S(1)} collective-permute-done((bf16[256,1280]{1,0:T(8,128)(2,1)S(1)}, bf16[256,1280]{1,0:T(8,128)(2,1)S(1)}, u32[]{:S(2)}, u32[]{:S(2)}) %collective-permute-start.40) | collective-permute-done | bytes 655392 | tf_op jit(solution)/shard_map/ppermute | solution.py:123
  688.3 9.9 %all-reduce.22.cloned.1.call-done = (bf16[256,2048]{1,0:T(8,128)(2,1)}, bf16[256,2048]{1,0:T(8,128)(2,1)}) async-done(((bf16[256,2048]{1,0:T(8,128)(2,1)}, bf16[256,2048]{1,0:T(8,128)(2,1)}), (bf16[256,2048]{1,0:T(8,128)(2,1)}, bf16[256,2048]{1,0:T(8,128)(2,1)})) %all-reduce.22.cloned.1.call-update) | async-done | bytes 2097168 | tf_op jit(solution)/shard_map/psum | solution.py:404
  725.0 6.1 wide_outputs.1
  (578 shorter events, 380.7 us)
Async XLA Ops:
  8.0 110.6 %all-gather.5.cloned.1.call-start = ((), (), s32[]{:S(2)}) async-start(), calls=%async_computation.4 | async-start | bytes 15335424 | tf_op jit(solution)/shard_map/all_gather | solution.py:871
  22.0 151.6 %all-reduce.10.cloned.1.call-start = ((), (), s32[]{:S(2)}) async-start(), calls=%async_computation.5 | async-start | bytes 2097152 | tf_op jit(solution)/shard_map/psum | solution.py:404
  32.1 33.8 %collective-permute-start.1 = (bf16[272,1280]{1,0:T(8,128)(2,1)S(1)}, bf16[272,1280]{1,0:T(8,128)(2,1)S(1)}, u32[]{:S(2)}, u32[]{:S(2)}) collective-permute-start(bf16[272,1280]{1,0:T(8,128)(2,1)S(1)} %get-tuple-element.204), channel_id=1, source_target_pairs={{0,4},{4,12},{12,8},{8,0},{1,5},{5,13},{13,9},{9,1},{2,6},{6,14},{... | collective-permute-start | bytes 2088968 | tf_op jit(solution)/shard_map/ppermute | solution.py:70
  34.9 33.2 %collective-permute-start.2 = (bf16[272,1280]{1,0:T(8,128)(2,1)S(1)}, bf16[272,1280]{1,0:T(8,128)(2,1)S(1)}, u32[]{:S(2)}, u32[]{:S(2)}) collective-permute-start(bf16[272,1280]{1,0:T(8,128)(2,1)S(1)} %get-tuple-element.204), channel_id=1, source_target_pairs={{4,0},{12,4},{8,12},{0,8},{5,1},{13,5},{9,13},{1,9},{6,2},{14,6},{... | collective-permute-start | bytes 2088968 | tf_op jit(solution)/shard_map/ppermute | solution.py:71
  118.6 70.7 %all-gather.7.cloned.1.call-start = ((), (), s32[]{:S(2)}) async-start(), calls=%async_computation.6 | async-start | bytes 7208960 | tf_op jit(solution)/shard_map/all_gather | solution.py:865
  119.2 134.0 %all-reduce.12.cloned.1.call-start = ((), (), s32[]{:S(2)}) async-start(), calls=%async_computation.7 | async-start | bytes 2097152 | tf_op jit(solution)/shard_map/psum | solution.py:404
  200.8 78.0 %all-gather.9.cloned.1.call-start = ((), (), s32[]{:S(2)}) async-start(), calls=%async_computation.8 | async-start | bytes 6553600 | tf_op jit(solution)/shard_map/all_gather | solution.py:865
  202.0 128.7 %all-reduce.14.cloned.1.call-start = ((), (), s32[]{:S(2)}) async-start(), calls=%async_computation.9 | async-start | bytes 2097152 | tf_op jit(solution)/shard_map/psum | solution.py:404
  278.8 65.1 %all-gather.11.cloned.1.call-start = ((), (), s32[]{:S(2)}) async-start(), calls=%async_computation.10 | async-start | bytes 5242880 | tf_op jit(solution)/shard_map/all_gather | solution.py:865
  279.4 132.9 %all-reduce.16.cloned.1.call-start = ((), (), s32[]{:S(2)}) async-start(), calls=%async_computation.11 | async-start | bytes 2097152 | tf_op jit(solution)/shard_map/psum | solution.py:404
  279.8 27.9 %collective-permute-start.19 = (bf16[512,768]{1,0:T(8,128)(2,1)}, bf16[512,768]{1,0:T(8,128)(2,1)S(1)}, u32[]{:S(2)}, u32[]{:S(2)}) collective-permute-start(bf16[512,768]{1,0:T(8,128)(2,1)} %slice.187), channel_id=1, source_target_pairs={{4,0},{12,4},{8,12},{0,8},{5,1},{13,5},{9,13},{1,9},{6,2},{14,6},{... | collective-permute-start | bytes 2359304 | tf_op jit(solution)/shard_map/ppermute | solution.py:71
  281.5 40.0 %collective-permute-start.17 = (bf16[256,2048]{1,0:T(8,128)(2,1)S(1)}, bf16[256,2048]{1,0:T(8,128)(2,1)S(1)}, u32[]{:S(2)}, u32[]{:S(2)}) collective-permute-start(bf16[256,2048]{1,0:T(8,128)(2,1)S(1)} %add_convert_fusion.1.stream_ref.refs_0_), channel_id=1, source_target_pairs={{0,16},{16,0},{1,17},{17,1},{2,18},{18,2},{3,19},{19,3},{4,20},{20... | collective-permute-start | bytes 3145736 | tf_op jit(solution)/shard_map/ppermute | solution.py:23
  360.6 84.6 %reduce-scatter.5.cloned.1.call-start = ((), (), s32[]{:S(2)}) async-start(), calls=%async_computation.12 | async-start | bytes 7864320 | tf_op jit(solution)/shard_map/reduce_scatter | solution.py:767
  372.6 124.6 %all-reduce.18.cloned.1.call-start = ((), (), s32[]{:S(2)}) async-start(), calls=%async_computation.13 | async-start | bytes 2097152 | tf_op jit(solution)/shard_map/psum | solution.py:404
  445.2 81.2 %reduce-scatter.7.cloned.1.call-start = ((), (), s32[]{:S(2)}) async-start(), calls=%async_computation.14 | async-start | bytes 7864320 | tf_op jit(solution)/shard_map/reduce_scatter | solution.py:888
  446.0 132.9 %all-reduce.20.cloned.1.call-start = ((), (), s32[]{:S(2)}) async-start(), calls=%async_computation.15 | async-start | bytes 2097152 | tf_op jit(solution)/shard_map/psum | solution.py:404
  526.5 84.5 %reduce-scatter.11.cloned.1.call-start = ((), (), s32[]{:S(2)}) async-start(), calls=%async_computation.17 | async-start | bytes 6553600 | tf_op jit(solution)/shard_map/reduce_scatter | solution.py:767
  537.7 160.5 %all-reduce.22.cloned.1.call-start = ((), (), s32[]{:S(2)}) async-start(), calls=%async_computation.18 | async-start | bytes 4194304 | tf_op jit(solution)/shard_map/psum | solution.py:404
  611.0 104.0 %reduce-scatter.9.cloned.1.call-start = ((), (), s32[]{:S(2)}) async-start(), calls=%async_computation.16 | async-start | bytes 9175040 | tf_op jit(solution)/shard_map/reduce_scatter | solution.py:888
  641.6 31.1 %collective-permute-start.40 = (bf16[256,1280]{1,0:T(8,128)(2,1)S(1)}, bf16[256,1280]{1,0:T(8,128)(2,1)S(1)}, u32[]{:S(2)}, u32[]{:S(2)}) collective-permute-start(bf16[256,1280]{1,0:T(8,128)(2,1)S(1)} %pad_maximum_fusion.20), channel_id=1, source_target_pairs={{4,0},{12,4},{8,12},{0,8},{5,1},{13,5},{9,13},{1,9},{6,2},{14,6},{... | collective-permute-start | bytes 1966088 | tf_op jit(solution)/shard_map/ppermute | solution.py:123
  643.3 31.0 %collective-permute-start.38 = (bf16[256,1280]{1,0:T(8,128)(2,1)S(1)}, bf16[256,1280]{1,0:T(8,128)(2,1)S(1)}, u32[]{:S(2)}, u32[]{:S(2)}) collective-permute-start(bf16[256,1280]{1,0:T(8,128)(2,1)S(1)} %pad_maximum_fusion.19), channel_id=1, source_target_pairs={{0,4},{4,12},{12,8},{8,0},{1,5},{5,13},{13,9},{9,1},{2,6},{6,14},{... | collective-permute-start | bytes 1966088 | tf_op jit(solution)/shard_map/ppermute | solution.py:122
  643.9 39.3 %collective-permute-start.35 = (bf16[512,1536]{1,0:T(8,128)(2,1)}, bf16[512,1536]{1,0:T(8,128)(2,1)}, u32[]{:S(2)}, u32[]{:S(2)}) collective-permute-start(bf16[512,1536]{1,0:T(8,128)(2,1)} %reduce-scatter.5.cloned.1.call-done.high_ref.refs_1_), channel_id=1, source_target_pairs={{0,16},{1,17},{2,18},{3,19},{4,20},{5,21},{6,22},{7,23},{8,24},{9,... | collective-permute-start | bytes 4718600 | tf_op jit(solution)/shard_map/ppermute | solution.py:894
  646.4 41.8 %collective-permute-start.42 = (bf16[512,1536]{1,0:T(8,128)(2,1)}, bf16[512,1536]{1,0:T(8,128)(2,1)}, u32[]{:S(2)}, u32[]{:S(2)}) collective-permute-start(bf16[512,1536]{1,0:T(8,128)(2,1)} %reduce-scatter.7.cloned.1.call-done.refs_5_), channel_id=1, source_target_pairs={{0,16},{1,17},{2,18},{3,19},{4,20},{5,21},{6,22},{7,23},{8,24},{9,... | collective-permute-start | bytes 4718600 | tf_op jit(solution)/shard_map/ppermute | solution.py:894
  648.9 34.4 %collective-permute-start.34 = (bf16[512,1280]{1,0:T(8,128)(2,1)}, bf16[512,1280]{1,0:T(8,128)(2,1)}, u32[]{:S(2)}, u32[]{:S(2)}) collective-permute-start(bf16[512,1280]{1,0:T(8,128)(2,1)} %reduce-scatter.11.cloned.1.call-done.low_ref.refs_0_), channel_id=1, source_target_pairs={{16,0},{17,1},{18,2},{19,3},{20,4},{21,5},{22,6},{23,7},{24,8},{25... | collective-permute-start | bytes 3932168 | tf_op jit(solution)/shard_map/ppermute | solution.py:891
  (186 other events, 1366.7 us)
Sparse Core Ops, SparseCore 0:
  22.1 96.4 all-gather.4
  121.5 52.0 all-reduce.9
  200.9 51.1 all-reduce.11
  278.9 51.7 all-reduce.13
  360.7 51.5 all-reduce.15
  445.3 51.8 all-reduce.17
  526.6 51.8 all-reduce.19
  611.1 87.0 all-reduce.21
Sparse Core Ops, SparseCore 1:
  121.7 65.8 all-gather.6
  203.8 74.9 all-gather.8
  281.8 61.7 all-gather.10
  372.7 72.4 reduce-scatter.4
  449.3 77.1 reduce-scatter.6
  537.8 73.1 reduce-scatter.10
  614.7 99.9 reduce-scatter.8

commit v9 on v8

--- a/solution.py
+++ b/solution.py
@@ -166,7 +166,7 @@
         + [pl.BlockSpec(array.shape, lambda i: (0, 0)) for array in arrays],
         out_specs=pl.BlockSpec((tile, columns), lambda i: (i, 0)),
         out_shape=jax.ShapeDtypeStruct((width, columns), bf16),
-        compiler_params=params(),
+        compiler_params=params(58),
         cost_estimate=cost(
             4 * tokens * width * columns,
             2 * (width * columns + 2 * tokens * width * len(lefts) + 2 * tokens * columns),

time: 750 us -> 743 us (level)
  local copies, waits for them, and re-layouts: 112 us -> 83.5 us
  Pallas kernels: 72 us -> 85.9 us
  waiting for transfers between devices: 372 us -> 380 us
    unnamed x292 -> x268, local copies, waits for them, and re-layouts: 70.4 us -> 43.7 us
    pallas_call x4, Pallas kernels: 17.4 us -> 31.3 us  [token_terms(): pl.pallas_call(functools.partial(token_terms_kernel, plan), grid=(width /...]
    psum x7, waiting for transfers between devices: 104 us -> 117 us  [sum_tensor(): return (lax.psum(partial, 'tensor'), *others)]
  transfers between devices with their start and end apart: 65 -> 65, of which waited for: 45 -> 45; matrix products, arithmetic and copies ran while one was open for 17% -> 17% of each run, Pallas kernels for 9% -> 11%
where the time goes in v9:
time: 743 us; the launch traced here: 732 us
  waiting for transfers between devices  380 us (51%)
  Pallas kernels  85.9 us (12%)
  local copies, waits for them, and re-layouts  83.5 us (11%)
  other arithmetic  68.9 us (9%)
  starting transfers between devices  50.3 us (7%)
  matrix products  45.5 us (6%)
  between operations  17.7 us (2%)
    psum x7, waiting for transfers between devices, sum_tensor(): return (lax.psum(partial, 'tensor'), *others)  117 us
    ppermute x3, waiting for transfers between devices, ring_gather_start(): from_back.append(lax.ppermute(from_back[-1], 'ctx', ahead))  69.1 us
    ppermute x2, waiting for transfers between devices, ring_scatter(): from_front = lax.ppermute(to_back, 'ctx', behind)  46.5 us
    unnamed x268, local copies, waits for them, and re-layouts  43.7 us
    pallas_call x4, Pallas kernels, token_terms(): pl.pallas_call(functools.partial(token_terms_kernel, plan), grid=(width /...  31.3 us
    ppermute x19, waiting for transfers between devices, swap_cores(): return lax.ppermute(block, 'pipe', [(0, 1), (1, 0)])  31.3 us
    dot_general x6, matrix products, product(): lax.dot_general(left, right, (((1,), (0,)), ((), ())), preferred_element_...  28.6 us
    ppermute x3, waiting for transfers between devices, ring_gather(): left = lax.ppermute(from_back[-1][:, :half], 'ctx', ahead)  27.9 us
  transfers between devices with their start and end apart: 65, of which 45 were waited for; matrix products, arithmetic and copies ran while one was open for 17% of the time, Pallas kernels for 11%

profile of v9, /device:TPU:0, one launch (start us, length us, event | category | flops | bytes accessed | tf_op | source)
XLA Modules:
  0.0 732.3 jit_solution(10992014745249295844)
XLA Ops:
  38.4 27.5 %collective-permute-done.1 = bf16[272,1280]{1,0:T(8,128)(2,1)S(1)} collective-permute-done((bf16[272,1280]{1,0:T(8,128)(2,1)S(1)}, bf16[272,1280]{1,0:T(8,128)(2,1)S(1)}, u32[]{:S(2)}, u32[]{:S(2)}) %collective-permute-start.1) | collective-permute-done | bytes 696352 | tf_op jit(solution)/shard_map/ppermute | solution.py:70
  68.4 8.4 %collective-permute-done.3 = bf16[272,640]{1,0:T(8,128)(2,1)S(1)} collective-permute-done((bf16[272,640]{1,0:T(8,128)(2,1)S(1)}, bf16[272,640]{1,0:T(8,128)(2,1)S(1)}, u32[]{:S(2)}, u32[]{:S(2)}) %collective-permute-start.3) | collective-permute-done | bytes 348192 | tf_op jit(solution)/shard_map/ppermute | solution.py:79
  110.6 8.0 %all-gather.5.cloned.1.call-done = bf16[4096,1664]{1,0:T(8,128)(2,1)} async-done(((bf16[512,1664]{1,0:T(8,128)(2,1)}), bf16[4096,1664]{1,0:T(8,128)(2,1)}) %all-gather.5.cloned.1.call-update) | async-done | bytes 13631504 | tf_op jit(solution)/shard_map/all_gather | solution.py:871
  126.0 47.6 %all-reduce.10.cloned.1.call-done = bf16[256,2048]{1,0:T(8,128)(2,1)} async-done(((bf16[256,2048]{1,0:T(8,128)(2,1)}), bf16[256,2048]{1,0:T(8,128)(2,1)}) %all-reduce.10.cloned.1.call-update) | async-done | bytes 1048592 | tf_op jit(solution)/shard_map/psum | solution.py:404
  179.2 7.3 fusion.52
  203.8 22.0 %collective-permute-done.11 = bf16[272,1280]{1,0:T(8,128)(2,1)S(1)} collective-permute-done((bf16[272,1280]{1,0:T(8,128)(2,1)S(1)}, bf16[272,1280]{1,0:T(8,128)(2,1)S(1)}, u32[]{:S(2)}, u32[]{:S(2)}) %collective-permute-start.11) | collective-permute-done | bytes 696352 | tf_op jit(solution)/shard_map/ppermute | solution.py:70
  229.4 11.2 %collective-permute-done.13 = bf16[272,640]{1,0:T(8,128)(2,1)S(1)} collective-permute-done((bf16[272,640]{1,0:T(8,128)(2,1)S(1)}, bf16[272,640]{1,0:T(8,128)(2,1)S(1)}, u32[]{:S(2)}, u32[]{:S(2)}) %collective-permute-start.13) | collective-permute-done | bytes 348192 | tf_op jit(solution)/shard_map/ppermute | solution.py:79
  285.8 19.5 %collective-permute-done.18 = bf16[512,768]{1,0:T(8,128)(2,1)S(1)} collective-permute-done((bf16[512,768]{1,0:T(8,128)(2,1)S(1)}, bf16[512,768]{1,0:T(8,128)(2,1)S(1)}, u32[]{:S(2)}, u32[]{:S(2)}) %collective-permute-start.18) | collective-permute-done | bytes 786464 | tf_op jit(solution)/shard_map/ppermute | solution.py:70
  309.5 8.2 %collective-permute-done.20 = bf16[512,384]{1,0:T(8,128)(2,1)S(1)} collective-permute-done((bf16[512,384]{1,0:T(8,128)(2,1)S(1)}, bf16[512,384]{1,0:T(8,128)(2,1)S(1)}, u32[]{:S(2)}, u32[]{:S(2)}) %collective-permute-start.20) | collective-permute-done | bytes 393248 | tf_op jit(solution)/shard_map/ppermute | solution.py:79
  321.1 9.1 %all-reduce.14.cloned.1.call-done = bf16[256,2048]{1,0:T(8,128)(2,1)} async-done(((bf16[256,2048]{1,0:T(8,128)(2,1)}), bf16[256,2048]{1,0:T(8,128)(2,1)}) %all-reduce.14.cloned.1.call-update) | async-done | bytes 1048592 | tf_op jit(solution)/shard_map/psum | solution.py:404
  360.2 8.1 %token_terms.5 = bf16[2048,1536]{1,0:T(8,128)(2,1)} custom-call(bf16[256,2048]{1,0:T(8,128)(2,1)} %get-tuple-element.128.refs_0_, bf16[256,2048]{1,0:T(8,128)(2,1)} %get-tuple-element.129.refs_1_, bf16[256,2048]{1,0:T(8,128)(2,1)} %copy-done.78, bf16[256,2048]{1,0:T(8,128)(2,1)} %copy-done.97, bf16[512,1024]{1,0:T(8,128)(2,1)} %get-tuple-element.211.refs_4_, ...), custom_call_target="tpu_custom_call" | custom-call | flops 3221225472 | bytes 12058624 | tf_op jit(solution)/shard_map/token_terms/pallas_call | solution.py:162
  368.4 7.6 %token_terms.4 = bf16[2048,1536]{1,0:T(8,128)(2,1)} custom-call(bf16[256,2048]{1,0:T(8,128)(2,1)} %copy-done.78, bf16[256,2048]{1,0:T(8,128)(2,1)} %copy-done.97, bf16[512,1024]{1,0:T(8,128)(2,1)} %copy-done.76, bf16[512,1024]{1,0:T(8,128)(2,1)} %copy-done.98), custom_call_target="tpu_custom_call" | custom-call | flops 3221225472 | bytes 9961472 | tf_op jit(solution)/shard_map/token_terms/pallas_call | solution.py:162
  376.0 36.0 %all-reduce.16.cloned.1.call-done = bf16[256,2048]{1,0:T(8,128)(2,1)} async-done(((bf16[256,2048]{1,0:T(8,128)(2,1)}), bf16[256,2048]{1,0:T(8,128)(2,1)}) %all-reduce.16.cloned.1.call-update) | async-done | bytes 1048592 | tf_op jit(solution)/shard_map/psum | solution.py:404
  426.1 9.4 %collective-permute-done.24.back_ref = bf16[256,256]{1,0:T(8,128)(2,1)S(1)} collective-permute-done((bf16[256,256]{1,0:T(8,128)(2,1)S(1)}, bf16[256,256]{1,0:T(8,128)(2,1)S(1)}, u32[]{:S(2)}, u32[]{:S(2)}) %collective-permute-start.24) | collective-permute-done | bytes 131104 | tf_op jit(solution)/shard_map/ppermute | solution.py:29
  466.8 13.4 %collective-permute-done.26 = bf16[256,640]{1,0:T(8,128)(2,1)S(1)} collective-permute-done((bf16[256,640]{1,0:T(8,128)(2,1)S(1)}, bf16[256,640]{1,0:T(8,128)(2,1)S(1)}, u32[]{:S(2)}, u32[]{:S(2)}) %collective-permute-start.26) | collective-permute-done | bytes 327712 | tf_op jit(solution)/shard_map/ppermute | solution.py:104
  483.8 9.3 %all-reduce.18.cloned.1.call-done = bf16[256,2048]{1,0:T(8,128)(2,1)} async-done(((bf16[256,2048]{1,0:T(8,128)(2,1)}), bf16[256,2048]{1,0:T(8,128)(2,1)}) %all-reduce.18.cloned.1.call-update) | async-done | bytes 1048592 | tf_op jit(solution)/shard_map/psum | solution.py:404
  522.4 7.5 %token_terms.7 = bf16[2048,1280]{1,0:T(8,128)(2,1)} custom-call(bf16[256,2048]{1,0:T(8,128)(2,1)} %copy-done.6, bf16[256,2048]{1,0:T(8,128)(2,1)} %copy-done.14, bf16[256,2048]{1,0:T(8,128)(2,1)} %copy-done.86, bf16[256,2048]{1,0:T(8,128)(2,1)} %copy-done.99, bf16[512,1024]{1,0:T(8,128)(2,1)} %copy-done.84, bf16[512,1024]{1,0:T(8,128)(2,1)} %copy-done.100), custom_call_target="tpu_custom_call" | custom-call | flops 2684354560 | bytes 10747904 | tf_op jit(solution)/shard_map/token_terms/pallas_call | solution.py:162
  533.1 24.1 %collective-permute-done.32 = bf16[256,1280]{1,0:T(8,128)(2,1)S(1)} collective-permute-done((bf16[256,1280]{1,0:T(8,128)(2,1)S(1)}, bf16[256,1280]{1,0:T(8,128)(2,1)S(1)}, u32[]{:S(2)}, u32[]{:S(2)}) %collective-permute-start.32) | collective-permute-done | bytes 655392 | tf_op jit(solution)/shard_map/ppermute | solution.py:123
  561.0 8.2 %token_terms.6 = bf16[2048,1792]{1,0:T(8,128)(2,1)} custom-call(bf16[256,2048]{1,0:T(8,128)(2,1)} %copy-done.86, bf16[256,2048]{1,0:T(8,128)(2,1)} %copy-done.99, bf16[512,1024]{1,0:T(8,128)(2,1)} %copy-done.100, bf16[512,1024]{1,0:T(8,128)(2,1)} %copy-done.126), custom_call_target="tpu_custom_call" | custom-call | flops 3758096384 | bytes 11272192 | tf_op jit(solution)/shard_map/token_terms/pallas_call | solution.py:162
  580.0 6.5 mix_back.3
  588.8 9.4 %collective-permute-done.33.back_ref = bf16[256,256]{1,0:T(8,128)(2,1)S(1)} collective-permute-done((bf16[256,256]{1,0:T(8,128)(2,1)S(1)}, bf16[256,256]{1,0:T(8,128)(2,1)S(1)}, u32[]{:S(2)}, u32[]{:S(2)}) %collective-permute-start.33) | collective-permute-done | bytes 131104 | tf_op jit(solution)/shard_map/ppermute | solution.py:29
  619.2 15.1 %collective-permute-done.39 = bf16[256,640]{1,0:T(8,128)(2,1)S(1)} collective-permute-done((bf16[256,640]{1,0:T(8,128)(2,1)S(1)}, bf16[256,640]{1,0:T(8,128)(2,1)S(1)}, u32[]{:S(2)}, u32[]{:S(2)}) %collective-permute-start.39) | collective-permute-done | bytes 327712 | tf_op jit(solution)/shard_map/ppermute | solution.py:105
  643.2 22.4 %collective-permute-done.40 = bf16[256,1280]{1,0:T(8,128)(2,1)S(1)} collective-permute-done((bf16[256,1280]{1,0:T(8,128)(2,1)S(1)}, bf16[256,1280]{1,0:T(8,128)(2,1)S(1)}, u32[]{:S(2)}, u32[]{:S(2)}) %collective-permute-start.40) | collective-permute-done | bytes 655392 | tf_op jit(solution)/shard_map/ppermute | solution.py:123
  681.1 10.0 %all-reduce.22.cloned.1.call-done = (bf16[256,2048]{1,0:T(8,128)(2,1)}, bf16[256,2048]{1,0:T(8,128)(2,1)}) async-done(((bf16[256,2048]{1,0:T(8,128)(2,1)}, bf16[256,2048]{1,0:T(8,128)(2,1)}), (bf16[256,2048]{1,0:T(8,128)(2,1)}, bf16[256,2048]{1,0:T(8,128)(2,1)})) %all-reduce.22.cloned.1.call-update) | async-done | bytes 2097168 | tf_op jit(solution)/shard_map/psum | solution.py:404
  (554 shorter events, 358.6 us)
Async XLA Ops:
  8.0 110.6 %all-gather.5.cloned.1.call-start = ((), (), s32[]{:S(2)}) async-start(), calls=%async_computation.4 | async-start | bytes 15335424 | tf_op jit(solution)/shard_map/all_gather | solution.py:871
  22.0 151.6 %all-reduce.10.cloned.1.call-start = ((), (), s32[]{:S(2)}) async-start(), calls=%async_computation.5 | async-start | bytes 2097152 | tf_op jit(solution)/shard_map/psum | solution.py:404
  32.1 33.8 %collective-permute-start.1 = (bf16[272,1280]{1,0:T(8,128)(2,1)S(1)}, bf16[272,1280]{1,0:T(8,128)(2,1)S(1)}, u32[]{:S(2)}, u32[]{:S(2)}) collective-permute-start(bf16[272,1280]{1,0:T(8,128)(2,1)S(1)} %get-tuple-element.204), channel_id=1, source_target_pairs={{0,4},{4,12},{12,8},{8,0},{1,5},{5,13},{13,9},{9,1},{2,6},{6,14},{... | collective-permute-start | bytes 2088968 | tf_op jit(solution)/shard_map/ppermute | solution.py:70
  34.9 33.2 %collective-permute-start.2 = (bf16[272,1280]{1,0:T(8,128)(2,1)S(1)}, bf16[272,1280]{1,0:T(8,128)(2,1)S(1)}, u32[]{:S(2)}, u32[]{:S(2)}) collective-permute-start(bf16[272,1280]{1,0:T(8,128)(2,1)S(1)} %get-tuple-element.204), channel_id=1, source_target_pairs={{4,0},{12,4},{8,12},{0,8},{5,1},{13,5},{9,13},{1,9},{6,2},{14,6},{... | collective-permute-start | bytes 2088968 | tf_op jit(solution)/shard_map/ppermute | solution.py:71
  118.6 69.7 %all-gather.7.cloned.1.call-start = ((), (), s32[]{:S(2)}) async-start(), calls=%async_computation.6 | async-start | bytes 7208960 | tf_op jit(solution)/shard_map/all_gather | solution.py:865
  119.2 132.9 %all-reduce.12.cloned.1.call-start = ((), (), s32[]{:S(2)}) async-start(), calls=%async_computation.7 | async-start | bytes 2097152 | tf_op jit(solution)/shard_map/psum | solution.py:404
  200.1 78.0 %all-gather.9.cloned.1.call-start = ((), (), s32[]{:S(2)}) async-start(), calls=%async_computation.8 | async-start | bytes 6553600 | tf_op jit(solution)/shard_map/all_gather | solution.py:865
  201.4 128.7 %all-reduce.14.cloned.1.call-start = ((), (), s32[]{:S(2)}) async-start(), calls=%async_computation.9 | async-start | bytes 2097152 | tf_op jit(solution)/shard_map/psum | solution.py:404
  278.2 64.9 %all-gather.11.cloned.1.call-start = ((), (), s32[]{:S(2)}) async-start(), calls=%async_computation.10 | async-start | bytes 5242880 | tf_op jit(solution)/shard_map/all_gather | solution.py:865
  278.7 133.3 %all-reduce.16.cloned.1.call-start = ((), (), s32[]{:S(2)}) async-start(), calls=%async_computation.11 | async-start | bytes 2097152 | tf_op jit(solution)/shard_map/psum | solution.py:404
  279.8 27.8 %collective-permute-start.19 = (bf16[512,768]{1,0:T(8,128)(2,1)S(1)}, bf16[512,768]{1,0:T(8,128)(2,1)S(1)}, u32[]{:S(2)}, u32[]{:S(2)}) collective-permute-start(bf16[512,768]{1,0:T(8,128)(2,1)S(1)} %copy-done.90), channel_id=1, source_target_pairs={{4,0},{12,4},{8,12},{0,8},{5,1},{13,5},{9,13},{1,9},{6,2},{14,6},{... | collective-permute-start | bytes 2359304 | tf_op jit(solution)/shard_map/ppermute | solution.py:71
  280.9 40.2 %collective-permute-start.17 = (bf16[256,2048]{1,0:T(8,128)(2,1)S(1)}, bf16[256,2048]{1,0:T(8,128)(2,1)S(1)}, u32[]{:S(2)}, u32[]{:S(2)}) collective-permute-start(bf16[256,2048]{1,0:T(8,128)(2,1)S(1)} %add_convert_fusion.1.stream_ref.refs_0_), channel_id=1, source_target_pairs={{0,16},{16,0},{1,17},{17,1},{2,18},{18,2},{3,19},{19,3},{4,20},{20... | collective-permute-start | bytes 3145736 | tf_op jit(solution)/shard_map/ppermute | solution.py:23
  360.2 80.9 %reduce-scatter.5.cloned.1.call-start = ((), (), s32[]{:S(2)}) async-start(), calls=%async_computation.12 | async-start | bytes 7864320 | tf_op jit(solution)/shard_map/reduce_scatter | solution.py:767
  368.4 124.7 %all-reduce.18.cloned.1.call-start = ((), (), s32[]{:S(2)}) async-start(), calls=%async_computation.13 | async-start | bytes 2097152 | tf_op jit(solution)/shard_map/psum | solution.py:404
  441.1 81.2 %reduce-scatter.7.cloned.1.call-start = ((), (), s32[]{:S(2)}) async-start(), calls=%async_computation.14 | async-start | bytes 7864320 | tf_op jit(solution)/shard_map/reduce_scatter | solution.py:888
  441.8 132.5 %all-reduce.20.cloned.1.call-start = ((), (), s32[]{:S(2)}) async-start(), calls=%async_computation.15 | async-start | bytes 2097152 | tf_op jit(solution)/shard_map/psum | solution.py:404
  522.3 81.5 %reduce-scatter.11.cloned.1.call-start = ((), (), s32[]{:S(2)}) async-start(), calls=%async_computation.17 | async-start | bytes 6553600 | tf_op jit(solution)/shard_map/reduce_scatter | solution.py:767
  529.9 161.2 %all-reduce.22.cloned.1.call-start = ((), (), s32[]{:S(2)}) async-start(), calls=%async_computation.18 | async-start | bytes 4194304 | tf_op jit(solution)/shard_map/psum | solution.py:404
  603.8 104.7 %reduce-scatter.9.cloned.1.call-start = ((), (), s32[]{:S(2)}) async-start(), calls=%async_computation.16 | async-start | bytes 9175040 | tf_op jit(solution)/shard_map/reduce_scatter | solution.py:888
  634.5 31.1 %collective-permute-start.40 = (bf16[256,1280]{1,0:T(8,128)(2,1)S(1)}, bf16[256,1280]{1,0:T(8,128)(2,1)S(1)}, u32[]{:S(2)}, u32[]{:S(2)}) collective-permute-start(bf16[256,1280]{1,0:T(8,128)(2,1)S(1)} %pad_maximum_fusion.20), channel_id=1, source_target_pairs={{4,0},{12,4},{8,12},{0,8},{5,1},{13,5},{9,13},{1,9},{6,2},{14,6},{... | collective-permute-start | bytes 1966088 | tf_op jit(solution)/shard_map/ppermute | solution.py:123
  636.2 31.0 %collective-permute-start.38 = (bf16[256,1280]{1,0:T(8,128)(2,1)S(1)}, bf16[256,1280]{1,0:T(8,128)(2,1)S(1)}, u32[]{:S(2)}, u32[]{:S(2)}) collective-permute-start(bf16[256,1280]{1,0:T(8,128)(2,1)S(1)} %pad_maximum_fusion.19), channel_id=1, source_target_pairs={{0,4},{4,12},{12,8},{8,0},{1,5},{5,13},{13,9},{9,1},{2,6},{6,14},{... | collective-permute-start | bytes 1966088 | tf_op jit(solution)/shard_map/ppermute | solution.py:122
  636.8 39.4 %collective-permute-start.35 = (bf16[512,1536]{1,0:T(8,128)(2,1)}, bf16[512,1536]{1,0:T(8,128)(2,1)}, u32[]{:S(2)}, u32[]{:S(2)}) collective-permute-start(bf16[512,1536]{1,0:T(8,128)(2,1)} %reduce-scatter.5.cloned.1.call-done.high_ref.refs_1_), channel_id=1, source_target_pairs={{0,16},{1,17},{2,18},{3,19},{4,20},{5,21},{6,22},{7,23},{8,24},{9,... | collective-permute-start | bytes 4718600 | tf_op jit(solution)/shard_map/ppermute | solution.py:894
  639.3 41.8 %collective-permute-start.42 = (bf16[512,1536]{1,0:T(8,128)(2,1)}, bf16[512,1536]{1,0:T(8,128)(2,1)}, u32[]{:S(2)}, u32[]{:S(2)}) collective-permute-start(bf16[512,1536]{1,0:T(8,128)(2,1)} %reduce-scatter.7.cloned.1.call-done.refs_5_), channel_id=1, source_target_pairs={{0,16},{1,17},{2,18},{3,19},{4,20},{5,21},{6,22},{7,23},{8,24},{9,... | collective-permute-start | bytes 4718600 | tf_op jit(solution)/shard_map/ppermute | solution.py:894
  641.7 34.4 %collective-permute-start.34 = (bf16[512,1280]{1,0:T(8,128)(2,1)}, bf16[512,1280]{1,0:T(8,128)(2,1)}, u32[]{:S(2)}, u32[]{:S(2)}) collective-permute-start(bf16[512,1280]{1,0:T(8,128)(2,1)} %reduce-scatter.11.cloned.1.call-done.low_ref.refs_0_), channel_id=1, source_target_pairs={{16,0},{17,1},{18,2},{19,3},{20,4},{21,5},{22,6},{23,7},{24,8},{25... | collective-permute-start | bytes 3932168 | tf_op jit(solution)/shard_map/ppermute | solution.py:891
  (174 other events, 1376.4 us)
Sparse Core Ops, SparseCore 0:
  22.1 96.4 all-gather.4
  121.5 52.0 all-reduce.9
  200.3 51.1 all-reduce.11
  278.3 51.7 all-reduce.13
  360.3 51.6 all-reduce.15
  441.2 51.8 all-reduce.17
  522.4 51.8 all-reduce.19
  603.9 87.0 all-reduce.21
Sparse Core Ops, SparseCore 1:
  121.7 65.8 all-gather.6
  203.2 74.9 all-gather.8
  281.2 61.7 all-gather.10
  368.4 72.6 reduce-scatter.4
  445.1 77.1 reduce-scatter.6
  530.0 73.8 reduce-scatter.10
  607.6 99.9 reduce-scatter.8
